TPU v7x, 128 devices: a whole 4x4x4 slice. The times are simulated.
128 devices in a mesh: expert: 4 (over x_hi, core), context: 8 (over x_lo, y), dp: 4 (over z).
Axes of the slice: x: 4 (x_hi: 2, x_lo: 2; x = x_hi * 2 + x_lo), y: 4, z: 4, core: 2. Of those that a mesh axis runs over, the one named last changes fastest.
Arguments:
- tokens: bfloat16 [16, 1024, 1536], P(('expert', 'dp'), 'context'), may hold values from -6 to 6
- expert_ids: int32 [16, 1024, 8], P(('expert', 'dp'), 'context'), may hold values from 0 to 31, all different within a row; in each aligned block of 128 rows (0 to 127, 128 to 255, ..., all dimensions but the last counted through in order) at most 40 rows name the same one
- w_query: bfloat16 [1536, 1536], replicated, may hold values from -0.15625 to 0.15625
- w_key: bfloat16 [1536, 512], replicated, may hold values from -0.15625 to 0.15625
- w_value: bfloat16 [1536, 512], replicated, may hold values from -0.15625 to 0.15625
- w_out: bfloat16 [1536, 1536], replicated, may hold values from -1.25 to 1.25
- gain_attn: float32 [1536], replicated, may hold values from 0.5 to 1.5
- gain_moe: float32 [1536], replicated, may hold values from 0.5 to 1.5
- w_router: bfloat16 [1536, 32], replicated, may hold values from -0.078125 to 0.078125
- w_gate: bfloat16 [32, 1536, 512], P(('expert', 'dp')), may hold values from -0.15625 to 0.15625
- w_up: bfloat16 [32, 1536, 512], P(('expert', 'dp')), may hold values from -0.15625 to 0.15625
- w_down: bfloat16 [32, 512, 1536], P(('expert', 'dp')), may hold values from -1 to 1
- cotangent: bfloat16 [16, 1024, 1536], P(('expert', 'dp'), 'context'), may hold values from -6 to 6
Outputs:
- mixed: bfloat16 [16, 1024, 1536], P(('expert', 'dp'), 'context')
- grad_tokens: float32 [16, 1024, 1536], P(('expert', 'dp'), 'context')
- grad_w_query: float32 [1536, 1536], P(('context', 'dp'))
- grad_w_key: float32 [1536, 512], P(('context', 'dp'))
- grad_w_value: float32 [1536, 512], P(('context', 'dp'))
- grad_w_out: float32 [1536, 1536], P(('context', 'dp'))
- grad_gain_attn: float32 [1536], P(('context', 'dp'))
- grad_gain_moe: float32 [1536], P(('context', 'dp'))
- grad_w_router: float32 [1536, 32], P(('context', 'dp'))
- grad_w_gate: float32 [32, 1536, 512], P(('expert', 'dp'), 'context')
- grad_w_up: float32 [32, 1536, 512], P(('expert', 'dp'), 'context')
- grad_w_down: float32 [32, 512, 1536], P(('expert', 'dp'), None, 'context')
Inputs may be any that keep to these rules, and one draw needn't show every extreme that they name: `expert_ids`: each token names 8 different experts; among the 128 tokens of one device no expert is named more than 40 times, a bound that some block reaches.
All inputs are finite; a program needn't handle non-finite values.
Results may differ from a plain program's by a relative error of at most 0.03.
Values may be sent and summed in bfloat16 or wider, within the bound.
A program may use at most 192 MiB of HBM per device.

v0:
```python
import math

import jax
import jax.numpy as jnp
from jax import lax
from jax.sharding import PartitionSpec as P

HEADS = 24
KV_HEADS = 8
HEAD_DIM = 64


epsilon = 1e-06
floor_score = -1e30


def normalize(values, gain):
    return values * lax.rsqrt(jnp.mean(values * values, axis=-1, keepdims=True) + epsilon) * gain


def rotary_tables(positions, half):
    index = lax.iota(jnp.float32, half)
    freqs = jnp.exp(index * (-math.log(10000.0) / half))
    angles = positions[:, None] * freqs[None, :]
    return (jnp.cos(angles)[:, None, :], jnp.sin(angles)[:, None, :])


def rotate(values, cosine, sine):
    half = values.shape[-1] // 2
    first = values[..., :half]
    second = values[..., half:]
    return jnp.concatenate(
        [first * cosine - second * sine, second * cosine + first * sine], axis=-1
    )


def block_scores(query, key_block, key_start, positions, scale):
    kv_count = query.shape[1]
    key_heads = key_block.reshape(key_block.shape[0], kv_count, -1)
    scores = (
        jnp.einsum("qkgd,skd->kgqs", query, key_heads, preferred_element_type=jnp.float32) * scale
    )
    key_positions = key_start + lax.iota(jnp.int32, key_block.shape[0])
    return jnp.where(
        key_positions[None, None, None, :] <= positions[None, None, :, None], scores, floor_score
    )


def split_blocks(key_all, value_all, block):
    count = key_all.shape[0] // block
    starts = lax.iota(jnp.int32, count) * block
    return (key_all.reshape(count, block, -1), value_all.reshape(count, block, -1), starts)


def attention_forward(query, key_all, value_all, positions, scale, block):
    key_blocks, value_blocks, starts = split_blocks(key_all, value_all, block)
    stat_shape = (query.shape[1], query.shape[2], query.shape[0])

    def gather_stats(carry, block_item):
        top_score, total = carry
        key_block, key_start = block_item
        scores = block_scores(query, key_block, key_start, positions, scale)
        new_top = jnp.maximum(top_score, jnp.max(scores, axis=-1))
        total = total * jnp.exp(top_score - new_top) + jnp.sum(
            jnp.exp(scores - new_top[..., None]), axis=-1
        )
        return ((new_top, total), None)

    start_stats = (
        jnp.full(stat_shape, floor_score, jnp.float32),
        jnp.zeros(stat_shape, jnp.float32),
    )
    (top_score, total), _ = lax.scan(gather_stats, start_stats, (key_blocks, starts))

    def weigh_values(accum, block_item):
        key_block, value_block, key_start = block_item
        scores = block_scores(query, key_block, key_start, positions, scale)
        probs = (jnp.exp(scores - top_score[..., None]) / total[..., None]).astype(jnp.bfloat16)
        value_heads = value_block.reshape(value_block.shape[0], query.shape[1], -1)
        return (
            accum
            + jnp.einsum("kgqs,skd->qkgd", probs, value_heads, preferred_element_type=jnp.float32),
            None,
        )

    accum, _ = lax.scan(
        weigh_values, jnp.zeros(query.shape, jnp.float32), (key_blocks, value_blocks, starts)
    )
    return (accum, top_score, total)


def attention_backward(
    query, key_all, value_all, positions, scale, block, top_score, total, grad_heads, attn_full
):
    key_blocks, value_blocks, starts = split_blocks(key_all, value_all, block)
    delta = jnp.einsum("qkgd,qkgd->kgq", grad_heads.astype(jnp.float32), attn_full)

    def block_grads(grad_query, block_item):
        key_block, value_block, key_start = block_item
        span = key_block.shape[0]
        scores = block_scores(query, key_block, key_start, positions, scale)
        probs = jnp.exp(scores - top_score[..., None]) / total[..., None]
        probs_low = probs.astype(jnp.bfloat16)
        key_heads = key_block.reshape(span, query.shape[1], -1)
        value_heads = value_block.reshape(span, query.shape[1], -1)
        grad_values = jnp.einsum(
            "kgqs,qkgd->skd", probs_low, grad_heads, preferred_element_type=jnp.float32
        )
        grad_probs = jnp.einsum(
            "qkgd,skd->kgqs", grad_heads, value_heads, preferred_element_type=jnp.float32
        )
        grad_scores = (probs * (grad_probs - delta[..., None])).astype(jnp.bfloat16)
        grad_query = (
            grad_query
            + jnp.einsum(
                "kgqs,skd->qkgd", grad_scores, key_heads, preferred_element_type=jnp.float32
            )
            * scale
        )
        grad_keys = (
            jnp.einsum("kgqs,qkgd->skd", grad_scores, query, preferred_element_type=jnp.float32)
            * scale
        )
        return (grad_query, (grad_keys.reshape(span, -1), grad_values.reshape(span, -1)))

    grad_query, (grad_keys, grad_values) = lax.scan(
        block_grads, jnp.zeros(query.shape, jnp.float32), (key_blocks, value_blocks, starts)
    )
    return (
        grad_query,
        grad_keys.reshape(key_all.shape[0], -1),
        grad_values.reshape(key_all.shape[0], -1),
    )


def shards(
    tokens,
    expert_ids,
    w_query,
    w_key,
    w_value,
    w_out,
    gain_attn,
    gain_moe,
    w_router,
    w_gate,
    w_up,
    w_down,
    cotangent,
):
    row_count = tokens.shape[1]
    model_width = tokens.shape[2]
    group = HEADS // KV_HEADS
    kv_width = KV_HEADS * HEAD_DIM
    route_count = expert_ids.shape[2]
    expert_count = w_router.shape[1]
    local_experts = w_gate.shape[0]
    capacity = row_count * route_count // expert_count + row_count * route_count // (
        4 * expert_count
    )
    scale = HEAD_DIM ** (-0.5)
    sources = lax.axis_size(("expert", "dp"))
    seq_length = row_count * lax.axis_size("context")
    block = min(512, seq_length)
    positions = lax.axis_index("context") * row_count + lax.iota(jnp.int32, row_count)
    cosine, sine = rotary_tables(positions.astype(jnp.float32), HEAD_DIM // 2)
    x_rows = tokens[0].astype(jnp.float32)
    route_ids = expert_ids[0]
    n_first = normalize(x_rows, gain_attn).astype(jnp.bfloat16)
    q_raw = jnp.dot(n_first, w_query, preferred_element_type=jnp.float32).reshape(
        row_count, HEADS, HEAD_DIM
    )
    k_raw = jnp.dot(n_first, w_key, preferred_element_type=jnp.float32).reshape(
        row_count, KV_HEADS, HEAD_DIM
    )
    value_rows = jnp.dot(n_first, w_value, preferred_element_type=jnp.float32).astype(jnp.bfloat16)
    query = (
        rotate(q_raw, cosine, sine)
        .astype(jnp.bfloat16)
        .reshape(row_count, KV_HEADS, group, HEAD_DIM)
    )
    key_rows = rotate(k_raw, cosine, sine).astype(jnp.bfloat16).reshape(row_count, kv_width)
    key_all, value_all = (
        lax.all_gather(key_rows, "context", axis=0, tiled=True),
        lax.all_gather(value_rows, "context", axis=0, tiled=True),
    )
    attn_full, top_score, total = attention_forward(
        query, key_all, value_all, positions, scale, block
    )
    attn_low = attn_full.reshape(row_count, model_width).astype(jnp.bfloat16)
    y_mid = x_rows + jnp.dot(attn_low, w_out, preferred_element_type=jnp.float32)
    n_second = normalize(y_mid, gain_moe).astype(jnp.bfloat16)
    logits = jnp.dot(n_second, w_router, preferred_element_type=jnp.float32)

    def gate_values(logit_rows):
        return jax.nn.softmax(jnp.take_along_axis(logit_rows, route_ids, axis=1), axis=-1)

    gates, gate_pull = jax.vjp(gate_values, logits)
    match = route_ids[:, :, None] == lax.iota(jnp.int32, expert_count)[None, None, :]
    counts = jnp.sum(match.astype(jnp.int32), axis=1)
    before = jnp.cumsum(counts, axis=0) - counts
    slot = jnp.sum(jnp.where(match, before[:, None, :], 0), axis=2)
    target = (route_ids * capacity + slot).reshape(-1)

    def dispatch_rows(route_rows):
        filled = (
            jnp.zeros((expert_count * capacity, model_width), jnp.bfloat16)
            .at[target]
            .set(route_rows)
        )
        return filled.reshape(expert_count, capacity, model_width)

    def collect_rows(returned_rows):
        return returned_rows.reshape(expert_count * capacity, model_width)[target].reshape(
            row_count, route_count, model_width
        )

    spread = jnp.broadcast_to(n_second[:, None, :], (row_count, route_count, model_width)).reshape(
        -1, model_width
    )
    received_rows = lax.all_to_all(
        dispatch_rows(spread), ("expert", "dp"), split_axis=0, concat_axis=0, tiled=True
    )
    grouped = received_rows.reshape(sources, local_experts, -1, model_width)
    hidden_gate = jnp.einsum("sxcd,xdf->sxcf", grouped, w_gate, preferred_element_type=jnp.float32)
    hidden_up = jnp.einsum("sxcd,xdf->sxcf", grouped, w_up, preferred_element_type=jnp.float32)
    active = (jax.nn.silu(hidden_gate) * hidden_up).astype(jnp.bfloat16)
    produced = jnp.einsum("sxcf,xfd->sxcd", active, w_down, preferred_element_type=jnp.float32)
    produced = produced.astype(jnp.bfloat16).reshape(received_rows.shape)
    returned = lax.all_to_all(produced, ("expert", "dp"), split_axis=0, concat_axis=0, tiled=True)
    picked = collect_rows(returned).astype(jnp.float32)
    y_out = y_mid + jnp.sum(gates[:, :, None] * picked, axis=1)
    grad_out = cotangent[0].astype(jnp.float32)
    grad_gate_values = jnp.sum(grad_out[:, None, :] * picked, axis=2)
    weighted = (
        (gates[:, :, None] * grad_out[:, None, :]).astype(jnp.bfloat16).reshape(-1, model_width)
    )
    grad_back = lax.all_to_all(
        dispatch_rows(weighted), ("expert", "dp"), split_axis=0, concat_axis=0, tiled=True
    )
    grouped = received_rows.reshape(sources, local_experts, -1, model_width)
    grad_grouped = grad_back.reshape(sources, local_experts, -1, model_width)
    hidden_gate = jnp.einsum("sxcd,xdf->sxcf", grouped, w_gate, preferred_element_type=jnp.float32)
    hidden_up = jnp.einsum("sxcd,xdf->sxcf", grouped, w_up, preferred_element_type=jnp.float32)

    def activate(gate_part, up_part):
        return jax.nn.silu(gate_part) * up_part

    active_full, act_pull = jax.vjp(activate, hidden_gate, hidden_up)
    active = active_full.astype(jnp.bfloat16)
    grad_w_down = jnp.einsum(
        "sxcf,sxcd->xfd", active, grad_grouped, preferred_element_type=jnp.float32
    )
    grad_active = jnp.einsum(
        "sxcd,xfd->sxcf", grad_grouped, w_down, preferred_element_type=jnp.float32
    )
    grad_hg, grad_hu = act_pull(grad_active)
    grad_hg = grad_hg.astype(jnp.bfloat16)
    grad_hu = grad_hu.astype(jnp.bfloat16)
    grad_w_gate = jnp.einsum("sxcd,sxcf->xdf", grouped, grad_hg, preferred_element_type=jnp.float32)
    grad_w_up = jnp.einsum("sxcd,sxcf->xdf", grouped, grad_hu, preferred_element_type=jnp.float32)
    grad_rows = jnp.einsum("sxcf,xdf->sxcd", grad_hg, w_gate, preferred_element_type=jnp.float32)
    grad_rows = grad_rows + jnp.einsum(
        "sxcf,xdf->sxcd", grad_hu, w_up, preferred_element_type=jnp.float32
    )
    grad_rows = grad_rows.astype(jnp.bfloat16).reshape(expert_count, capacity, model_width)
    grad_home = lax.all_to_all(grad_rows, ("expert", "dp"), split_axis=0, concat_axis=0, tiled=True)
    grad_n_second = jnp.sum(collect_rows(grad_home).astype(jnp.float32), axis=1)
    grad_logits = gate_pull(grad_gate_values)[0].astype(jnp.bfloat16)
    grad_w_router = jnp.einsum(
        "td,te->de", n_second, grad_logits, preferred_element_type=jnp.float32
    )
    grad_n_second = grad_n_second + jnp.einsum(
        "te,de->td", grad_logits, w_router, preferred_element_type=jnp.float32
    )
    _, norm_second_pull = jax.vjp(normalize, y_mid, gain_moe)
    grad_mid_norm, grad_gain_moe = norm_second_pull(grad_n_second)
    grad_mid = grad_out + grad_mid_norm
    grad_branch = grad_mid.astype(jnp.bfloat16)
    grad_w_out = jnp.einsum("td,te->de", attn_low, grad_branch, preferred_element_type=jnp.float32)
    grad_heads = jnp.einsum(
        "te,de->td", grad_branch, w_out, preferred_element_type=jnp.float32
    ).astype(jnp.bfloat16)
    key_again, value_again = (
        lax.all_gather(key_rows, "context", axis=0, tiled=True),
        lax.all_gather(value_rows, "context", axis=0, tiled=True),
    )
    grad_query, grad_key_all, grad_value_all = attention_backward(
        query,
        key_again,
        value_again,
        positions,
        scale,
        block,
        top_score,
        total,
        grad_heads.reshape(row_count, KV_HEADS, group, HEAD_DIM),
        attn_full,
    )
    grad_key_rot, grad_value_rows = (
        lax.psum_scatter(
            grad_key_all.astype(jnp.bfloat16), "context", scatter_dimension=0, tiled=True
        ).astype(jnp.float32),
        lax.psum_scatter(
            grad_value_all.astype(jnp.bfloat16), "context", scatter_dimension=0, tiled=True
        ).astype(jnp.float32),
    )
    grad_q_raw = rotate(grad_query.reshape(row_count, HEADS, HEAD_DIM), cosine, -sine)
    grad_q_raw = grad_q_raw.astype(jnp.bfloat16).reshape(row_count, model_width)
    grad_k_raw = rotate(grad_key_rot.reshape(row_count, KV_HEADS, HEAD_DIM), cosine, -sine)
    grad_k_raw = grad_k_raw.astype(jnp.bfloat16).reshape(row_count, kv_width)
    grad_v_raw = grad_value_rows.astype(jnp.bfloat16)
    grad_w_query = jnp.einsum("td,te->de", n_first, grad_q_raw, preferred_element_type=jnp.float32)
    grad_w_key = jnp.einsum("td,te->de", n_first, grad_k_raw, preferred_element_type=jnp.float32)
    grad_w_value = jnp.einsum("td,te->de", n_first, grad_v_raw, preferred_element_type=jnp.float32)
    grad_n_first = jnp.einsum("te,de->td", grad_q_raw, w_query, preferred_element_type=jnp.float32)
    grad_n_first = grad_n_first + jnp.einsum(
        "te,de->td", grad_k_raw, w_key, preferred_element_type=jnp.float32
    )
    grad_n_first = grad_n_first + jnp.einsum(
        "te,de->td", grad_v_raw, w_value, preferred_element_type=jnp.float32
    )
    _, norm_first_pull = jax.vjp(normalize, x_rows, gain_attn)
    grad_x_norm, grad_gain_attn = norm_first_pull(grad_n_first)
    grad_input = grad_mid + grad_x_norm
    expert_sums = (
        lax.psum_scatter(
            grad_w_gate.astype(jnp.bfloat16), "context", scatter_dimension=1, tiled=True
        ).astype(jnp.float32),
        lax.psum_scatter(
            grad_w_up.astype(jnp.bfloat16), "context", scatter_dimension=1, tiled=True
        ).astype(jnp.float32),
        lax.psum_scatter(
            grad_w_down.astype(jnp.bfloat16), "context", scatter_dimension=2, tiled=True
        ).astype(jnp.float32),
    )
    dense_terms = (
        grad_w_query,
        grad_w_key,
        grad_w_value,
        grad_w_out,
        grad_gain_attn,
        grad_gain_moe,
        grad_w_router,
    )
    partial_sums = (
        lax.psum_scatter(
            dense_terms[0].astype(jnp.bfloat16), ("context", "dp"), scatter_dimension=0, tiled=True
        ).astype(jnp.float32),
        lax.psum_scatter(
            dense_terms[1].astype(jnp.bfloat16), ("context", "dp"), scatter_dimension=0, tiled=True
        ).astype(jnp.float32),
        lax.psum_scatter(
            dense_terms[2].astype(jnp.bfloat16), ("context", "dp"), scatter_dimension=0, tiled=True
        ).astype(jnp.float32),
        lax.psum_scatter(
            dense_terms[3].astype(jnp.bfloat16), ("context", "dp"), scatter_dimension=0, tiled=True
        ).astype(jnp.float32),
        lax.psum_scatter(
            dense_terms[4].astype(jnp.bfloat16), ("context", "dp"), scatter_dimension=0, tiled=True
        ).astype(jnp.float32),
        lax.psum_scatter(
            dense_terms[5].astype(jnp.bfloat16), ("context", "dp"), scatter_dimension=0, tiled=True
        ).astype(jnp.float32),
        lax.psum_scatter(
            dense_terms[6].astype(jnp.bfloat16), ("context", "dp"), scatter_dimension=0, tiled=True
        ).astype(jnp.float32),
    )
    dense_sums = (
        lax.psum(partial_sums[0].astype(jnp.bfloat16), "expert").astype(jnp.float32),
        lax.psum(partial_sums[1].astype(jnp.bfloat16), "expert").astype(jnp.float32),
        lax.psum(partial_sums[2].astype(jnp.bfloat16), "expert").astype(jnp.float32),
        lax.psum(partial_sums[3].astype(jnp.bfloat16), "expert").astype(jnp.float32),
        lax.psum(partial_sums[4].astype(jnp.bfloat16), "expert").astype(jnp.float32),
        lax.psum(partial_sums[5].astype(jnp.bfloat16), "expert").astype(jnp.float32),
        lax.psum(partial_sums[6].astype(jnp.bfloat16), "expert").astype(jnp.float32),
    )
    return (
        y_out.astype(jnp.bfloat16)[None],
        grad_input[None],
        dense_sums[0],
        dense_sums[1],
        dense_sums[2],
        dense_sums[3],
        dense_sums[4],
        dense_sums[5],
        dense_sums[6],
        expert_sums[0],
        expert_sums[1],
        expert_sums[2],
    )


def solution(mesh):
    in_specs = (
        P(("expert", "dp"), "context", None),
        P(("expert", "dp"), "context", None),
        P(),
        P(),
        P(),
        P(),
        P(),
        P(),
        P(),
        P(("expert", "dp"), None, None),
        P(("expert", "dp"), None, None),
        P(("expert", "dp"), None, None),
        P(("expert", "dp"), "context", None),
    )
    out_specs = (
        P(("expert", "dp"), "context", None),
        P(("expert", "dp"), "context", None),
        P(("context", "dp"), None),
        P(("context", "dp"), None),
        P(("context", "dp"), None),
        P(("context", "dp"), None),
        P(("context", "dp")),
        P(("context", "dp")),
        P(("context", "dp"), None),
        P(("expert", "dp"), "context", None),
        P(("expert", "dp"), "context", None),
        P(("expert", "dp"), None, "context"),
    )
    return jax.shard_map(shards, mesh=mesh, in_specs=in_specs, out_specs=out_specs, check_vma=False)
```

profile of v0, /device:TPU:1, one launch (start us, length us, event | category | flops | bytes accessed | tf_op | source)
XLA Modules:
  0.0 1586.9 jit_solution(8403294609992225919)
XLA Ops:
  35.7 6.7 copy.100
  42.9 3.9 fusion.89
  51.6 38.0 %all-gather.5.cloned.1.call-done = bf16[1024,512]{1,0:T(8,128)(2,1)} async-done(((bf16[128,512]{1,0:T(8,128)(2,1)}), bf16[1024,512]{1,0:T(8,128)(2,1)}) %all-gather.5.cloned.1.call-update) | async-done | bytes 1048592 | tf_op jit(solution)/shard_map/all_gather | solution.py:184
  91.9 12.3 while.39
  104.2 18.4 %while.40 = (s32[]{:T(128)}, f32[128,8,3,64]{0,3,2,1:T(8,128)}, bf16[2,512,512]{1,2,0:T(8,128)(2,1)}, s32[2]{0:T(128)}, bf16[2,512,512]{1,2,0:T(8,128)(2,1)}, /*...) while((s32[]{:T(128)}, f32[128,8,3,64]{0,3,2,1:T(8,128)}, ...), condition=%wide.region_6.7_spmd.clone, body=%wide.region_5.6_spmd.clone.sunk | while | flops 410976896 | bytes 5272727 | solution.py:86
  109.1 4.1 fusion.189
  118.1 4.4 fusion.189
  128.5 8.3 scatter_custom_fusion
  136.7 12.2 all-to-all-start
  153.8 7.1 gather_fusion.2
  161.7 8.5 scatter_custom_fusion.1
  170.2 24.2 %all-to-all-done = bf16[32,40,1536]{2,1,0:T(8,128)(2,1)} async-done(((bf16[32,40,1536]{2,1,0:T(8,128)(2,1)}), bf16[32,40,1536]{2,1,0:T(8,128)(2,1)}, u32[]{:S(2)}, u32[]{:S(2)}) %all-to-all-start) | async-done | bytes 3932192 | tf_op jit(solution)/shard_map/all_to_all | solution.py:221
  194.4 11.1 all-to-all-start.2
  205.6 7.1 fusion.42
  212.6 5.9 fusion.44
  218.5 32.6 %all-to-all-done.2 = bf16[32,40,1536]{2,1,0:T(8,128)(2,1)} async-done(((bf16[32,40,1536]{2,1,0:T(8,128)(2,1)}), bf16[32,40,1536]{2,1,0:T(8,128)(2,1)}, u32[]{:S(2)}, u32[]{:S(2)}) %all-to-all-start.2) | async-done | bytes 3932192 | tf_op jit(solution)/shard_map/all_to_all | solution.py:238
  251.1 8.4 fusion.62
  264.2 10.7 all-to-all-start.1
  274.9 3.7 fusion.50
  283.3 37.2 %all-to-all-done.1 = bf16[32,40,1536]{2,1,0:T(8,128)(2,1)} async-done(((bf16[32,40,1536]{2,1,0:T(8,128)(2,1)}), bf16[32,40,1536]{2,1,0:T(8,128)(2,1)}, u32[]{:S(2)}, u32[]{:S(2)}) %all-to-all-start.1) | async-done | bytes 3932192 | tf_op jit(solution)/shard_map/all_to_all | solution.py:230
  320.4 10.7 all-to-all-start.3
  332.5 9.3 gather_fusion
  341.8 4.4 fusion.35
  346.6 30.1 %all-to-all-done.3 = bf16[32,40,1536]{2,1,0:T(8,128)(2,1)} async-done(((bf16[32,40,1536]{2,1,0:T(8,128)(2,1)}), bf16[32,40,1536]{2,1,0:T(8,128)(2,1)}, u32[]{:S(2)}, u32[]{:S(2)}) %all-to-all-start.3) | async-done | bytes 3932192 | tf_op jit(solution)/shard_map/all_to_all | solution.py:267
  376.7 9.9 gather_fusion.1
  386.6 4.1 convert_reduce_fusion
  390.7 6.3 scatter_custom_fusion.2
  399.1 4.3 convolution_convert_fusion.5
  404.4 40.4 %while.41 = (s32[]{:T(128)}, f32[128,8,3,64]{0,3,2,1:T(8,128)}, bf16[2,512,512]{2,1,0:T(8,128)(2,1)}, bf16[2,512,512]{2,1,0:T(8,128)(2,1)}, bf16[2,512,512]{1,2,...) while((s32[]{:T(128)}, f32[128,8,3,64]{0,3,2,1:T(8,128)}, ...), condition=%wide.region_22.23_spmd.clone, body=%wide.region_21.22_spmd.clone.sunk | while | flops 1020396160 | bytes 44311868 | solution.py:126
  447.6 34.0 %reduce-scatter.15.cloned.1.call-done = bf16[128,512]{1,0:T(8,128)(2,1)} async-done(((bf16[1024,512]{1,0:T(8,128)(2,1)}), bf16[128,512]{1,0:T(8,128)(2,1)}) %reduce-scatter.15.cloned.1.call-update) | async-done | bytes 131088 | tf_op jit(solution)/shard_map/reduce_scatter | solution.py:304
  484.5 37.3 %reduce-scatter.13.cloned.1.call-done = bf16[128,512]{1,0:T(8,128)(2,1)} async-done(((bf16[1024,512]{1,0:T(8,128)(2,1)}), bf16[128,512]{1,0:T(8,128)(2,1)}) %reduce-scatter.13.cloned.1.call-update) | async-done | bytes 131088 | tf_op jit(solution)/shard_map/reduce_scatter | solution.py:301
  524.8 3.5 convolution_convert_fusion
  529.7 3.7 convolution_convert_fusion.1
  534.7 6.8 bitcast_convert_fusion
  542.8 6.8 bitcast_convert_fusion.1
  551.0 6.8 bitcast_convert_fusion.2
  559.7 4.0 fusion.116
  563.7 99.3 %reduce-scatter.31.cloned.1.call-done = bf16[48,32]{1,0:T(8,128)(2,1)} async-done(((bf16[1536,32]{1,0:T(8,128)(2,1)}), bf16[48,32]{1,0:T(8,128)(2,1)}) %reduce-scatter.31.cloned.1.call-update) | async-done | bytes 3088
  668.6 65.8 %all-reduce.2 = (bf16[1536]{0:T(1024)(128)(2,1)S(1)}, bf16[1536]{0:T(1024)(128)(2,1)S(1)}) all-reduce(bf16[1536]{0:T(1024)(128)(2,1)S(1)} %get-tuple-element.390, bf16[1536]{0:T(1024)(128)(2,1)S(1)} %copy-done.47), channel_id=8, replica_groups=mesh['expert'=4,'context'=8,'dp'=4] {'context','dp'}, use_global_device_ids=true, to_apply=%region_35.36.clone | all-reduce | flops 3072 | bytes 12288
  735.5 89.7 %reduce-scatter.21.cloned.1.call-done = bf16[48,512]{1,0:T(8,128)(2,1)} async-done(((bf16[1536,512]{1,0:T(8,128)(2,1)}), bf16[48,512]{1,0:T(8,128)(2,1)}) %reduce-scatter.21.cloned.1.call-update) | async-done | bytes 49168 | tf_op jit(solution)/shard_map/reduce_scatter | solution.py:353
  825.2 161.1 %reduce-scatter.19.cloned.1.call-done = bf16[48,512]{1,0:T(8,128)(2,1)} async-done(((bf16[1536,512]{1,0:T(8,128)(2,1)}), bf16[48,512]{1,0:T(8,128)(2,1)}) %reduce-scatter.19.cloned.1.call-update) | async-done | bytes 49168 | tf_op jit(solution)/shard_map/reduce_scatter | solution.py:350
  986.4 169.8 %reduce-scatter.23.cloned.1.call-done = bf16[48,1536]{1,0:T(8,128)(2,1)} async-done(((bf16[1536,1536]{1,0:T(8,128)(2,1)}), bf16[48,1536]{1,0:T(8,128)(2,1)}) %reduce-scatter.23.cloned.1.call-update) | async-done | bytes 147472 | tf_op jit(solution)/shard_map/reduce_scatter | solution.py:356
  1156.2 168.7 %reduce-scatter.17.cloned.1.call-done = bf16[48,1536]{1,0:T(8,128)(2,1)} async-done(((bf16[1536,1536]{1,0:T(8,128)(2,1)}), bf16[48,1536]{1,0:T(8,128)(2,1)}) %reduce-scatter.17.cloned.1.call-update) | async-done | bytes 147472 | tf_op jit(solution)/shard_map/reduce_scatter | solution.py:347
  1327.6 61.0 %reduce-scatter.29.cloned.1.call-done = bf16[2,512,192]{1,2,0:T(8,128)(2,1)} async-done(((bf16[2,512,1536]{1,2,0:T(8,128)(2,1)}), bf16[2,512,192]{1,2,0:T(8,128)(2,1)}) %reduce-scatter.29.cloned.1.call-update) | async-done | bytes 393232 | tf_op jit(solution)/shard_map/reduce_scatter | solution.py:333
  1390.5 46.3 %reduce-scatter.27.cloned.1.call-done = bf16[2,192,512]{2,1,0:T(8,128)(2,1)} async-done(((bf16[2,1536,512]{2,1,0:T(8,128)(2,1)}), bf16[2,192,512]{2,1,0:T(8,128)(2,1)}) %reduce-scatter.27.cloned.1.call-update) | async-done | bytes 393232 | tf_op jit(solution)/shard_map/reduce_scatter | solution.py:330
  1438.8 46.2 %reduce-scatter.25.cloned.1.call-done = bf16[2,192,512]{2,1,0:T(8,128)(2,1)} async-done(((bf16[2,1536,512]{2,1,0:T(8,128)(2,1)}), bf16[2,192,512]{2,1,0:T(8,128)(2,1)}) %reduce-scatter.25.cloned.1.call-update) | async-done | bytes 393232 | tf_op jit(solution)/shard_map/reduce_scatter | solution.py:327
  1486.9 47.1 %all-reduce.8.cloned.1.call-done = (bf16[48,512]{1,0:T(8,128)(2,1)}, bf16[48,512]{1,0:T(8,128)(2,1)}, bf16[48]{0:T(256)(128)(2,1)}, bf16[48]{0:T(256)(128)(2,1)}, bf16[48,32]{0,1:T(8,128)(2,1)}) async-done(((bf16[48,512]{1,0:T(8,128)(2,1)}, bf16[48,512]{1,0:T(8,128)(2,1)}, bf16[48]{0:T(256)(128)(2,1)}, bf16[48]{0:T(256)(128)(2,1)}, bf16[48,32]{0,1:T(8,128)(2,1)}), (bf16[48,512]{1,0:T(8,128)(2,1)}, ...) | async-done | bytes 101584 | tf_op jit(solution)/shard_map/psum | solution.py:371
  1540.6 36.1 %all-reduce.10.cloned.1.call-done = (bf16[48,1536]{1,0:T(8,128)(2,1)}, bf16[48,1536]{1,0:T(8,128)(2,1)}) async-done(((bf16[48,1536]{1,0:T(8,128)(2,1)}, bf16[48,1536]{1,0:T(8,128)(2,1)}), (bf16[48,1536]{1,0:T(8,128)(2,1)}, bf16[48,1536]{1,0:T(8,128)(2,1)})) %all-reduce.10.cloned.1.call-update) | async-done | bytes 294928 | tf_op jit(solution)/shard_map/psum | solution.py:370
  (325 shorter events, 163.8 us)
Async XLA Ops:
  7.2 243.9 %copy-start = (bf16[2,512,1536]{2,1,0:T(8,128)(2,1)S(1)}, bf16[2,512,1536]{2,1,0:T(8,128)(2,1)}, u32[]{:S(2)}) copy-start(bf16[2,512,1536]{2,1,0:T(8,128)(2,1)} %param.30) | copy-start | bytes 9437188
  7.2 8.1 copy-start.6
  7.2 8.1 copy-start.28
  7.2 42.0 %all-gather.3.cloned.1.call-start = ((), (), s32[]{:S(2)}) async-start(), calls=%async_computation.14 | async-start | bytes 1179648 | tf_op jit(solution)/shard_map/all_gather | solution.py:185
  9.2 8.2 copy-start.45
  11.8 77.8 %all-gather.5.cloned.1.call-start = ((), (), s32[]{:S(2)}) async-start(), calls=%async_computation.15 | async-start | bytes 1179648 | tf_op jit(solution)/shard_map/all_gather | solution.py:184
  128.5 8.3 copy-start.14
  136.7 57.7 %all-to-all-start = ((bf16[32,40,1536]{2,1,0:T(8,128)(2,1)}), bf16[32,40,1536]{2,1,0:T(8,128)(2,1)}, u32[]{:S(2)}, u32[]{:S(2)}) async-start(bf16[32,40,1536]{2,1,0:T(8,128)(2,1)} %bitcast.391), calls=%async_computation | async-start | bytes 7864320 | tf_op jit(solution)/shard_map/all_to_all | solution.py:221
  153.8 7.8 copy-start.50
  194.4 56.7 %all-to-all-start.2 = ((bf16[32,40,1536]{2,1,0:T(8,128)(2,1)}), bf16[32,40,1536]{2,1,0:T(8,128)(2,1)}, u32[]{:S(2)}, u32[]{:S(2)}) async-start(bf16[32,40,1536]{2,1,0:T(8,128)(2,1)} %bitcast.392), calls=%async_computation.2 | async-start | bytes 7864320 | tf_op jit(solution)/shard_map/all_to_all | solution.py:238
  205.6 7.1 copy-start.19
  264.2 10.7 copy-start.20
  264.2 56.2 %all-to-all-start.1 = ((bf16[32,40,1536]{2,1,0:T(8,128)(2,1)}), bf16[32,40,1536]{2,1,0:T(8,128)(2,1)}, u32[]{:S(2)}, u32[]{:S(2)}) async-start(bf16[32,40,1536]{2,1,0:T(8,128)(2,1)} %bitcast.393), calls=%async_computation.1 | async-start | bytes 7864320 | tf_op jit(solution)/shard_map/all_to_all | solution.py:230
  320.4 11.0 copy-start.58
  320.4 11.0 copy-start.57
  320.4 56.2 %all-to-all-start.3 = ((bf16[32,40,1536]{2,1,0:T(8,128)(2,1)}), bf16[32,40,1536]{2,1,0:T(8,128)(2,1)}, u32[]{:S(2)}, u32[]{:S(2)}) async-start(bf16[32,40,1536]{2,1,0:T(8,128)(2,1)} %bitcast.390), calls=%async_computation.3 | async-start | bytes 7864320 | tf_op jit(solution)/shard_map/all_to_all | solution.py:267
  331.1 150.4 %reduce-scatter.15.cloned.1.call-start = ((), (), s32[]{:S(2)}) async-start(), calls=%async_computation.17 | async-start | bytes 1179648 | tf_op jit(solution)/shard_map/reduce_scatter | solution.py:304
  386.6 10.4 copy-start.10
  386.6 10.4 copy-start.38
  386.6 10.4 copy-start.44
  386.6 10.4 copy-start.52
  386.6 11.4 copy-start.56
  386.6 11.5 copy-start.18
  386.6 11.4 copy-start.23
  399.1 5.3 copy-start.4
  399.1 5.3 copy-start.36
  444.8 36.8 %copy-start.7 = (bf16[1,128,1536]{2,1,0:T(8,128)(2,1)S(1)}, bf16[1,128,1536]{2,1,0:T(8,128)(2,1)}, u32[]{:S(2)}) copy-start(bf16[1,128,1536]{2,1,0:T(8,128)(2,1)} %param.19) | copy-start | bytes 1179652
  444.8 36.8 %copy-start.29 = (f32[1536]{0:T(1024)S(1)}, f32[1536]{0:T(1024)}, u32[]{:S(2)}) copy-start(f32[1536]{0:T(1024)} %param.25) | copy-start | bytes 18436
  444.8 36.8 %copy-start.46 = (f32[128]{0:T(128)S(1)}, f32[128]{0:T(128)}, u32[]{:S(2)}) copy-start(f32[128]{0:T(128)} %copy-done.45) | copy-start | bytes 1540
  444.8 77.0 %reduce-scatter.13.cloned.1.call-start = ((), (), s32[]{:S(2)}) async-start(), calls=%async_computation.16 | async-start | bytes 1179648 | tf_op jit(solution)/shard_map/reduce_scatter | solution.py:301
  444.9 77.9 %copy-start.33 = (f32[128,32]{0,1:T(8,128)S(1)}, f32[128,32]{0,1:T(8,128)}, u32[]{:S(2)}) copy-start(f32[128,32]{0,1:T(8,128)} %copy-done.31) | copy-start | bytes 49156
  444.9 77.9 %copy-start.40 = (f32[128,32]{0,1:T(8,128)S(1)}, f32[128,32]{0,1:T(8,128)}, u32[]{:S(2)}) copy-start(f32[128,32]{0,1:T(8,128)} %get-tuple-element.482) | copy-start | bytes 49156
  445.4 217.6 %reduce-scatter.31.cloned.1.call-start = ((), (), s32[]{:S(2)}) async-start(), calls=%async_computation.25 | async-start | bytes 405504
  447.6 377.6 %reduce-scatter.21.cloned.1.call-start = ((), (), s32[]{:S(2)}) async-start(), calls=%async_computation.20 | async-start | bytes 1622016 | tf_op jit(solution)/shard_map/reduce_scatter | solution.py:353
  484.4 40.4 %copy-start.12 = (f32[128,1536]{1,0:T(8,128)S(1)}, f32[128,1536]{1,0:T(8,128)}, u32[]{:S(2)}) copy-start(f32[128,1536]{1,0:T(8,128)} %copy-done.11) | copy-start | bytes 2359300
  484.4 40.4 %copy-start.16 = (bf16[128,8,3,64]{0,3,2,1:T(8,128)(2,1)S(1)}, bf16[128,8,3,64]{0,3,2,1:T(8,128)(2,1)}, u32[]{:S(2)}) copy-start(bf16[128,8,3,64]{0,3,2,1:T(8,128)(2,1)} %copy-done.15) | copy-start | bytes 1179652
  484.4 501.9 %reduce-scatter.19.cloned.1.call-start = ((), (), s32[]{:S(2)}) async-start(), calls=%async_computation.19 | async-start | bytes 1622016 | tf_op jit(solution)/shard_map/reduce_scatter | solution.py:350
  522.9 5.5 copy-start.27
  524.8 631.5 %reduce-scatter.23.cloned.1.call-start = ((), (), s32[]{:S(2)}) async-start(), calls=%async_computation.21 | async-start | bytes 4866048 | tf_op jit(solution)/shard_map/reduce_scatter | solution.py:356
  528.4 796.5 %reduce-scatter.17.cloned.1.call-start = ((), (), s32[]{:S(2)}) async-start(), calls=%async_computation.18 | async-start | bytes 4866048 | tf_op jit(solution)/shard_map/reduce_scatter | solution.py:347
  533.4 855.2 %reduce-scatter.29.cloned.1.call-start = ((), (), s32[]{:S(2)}) async-start(), calls=%async_computation.24 | async-start | bytes 3538944 | tf_op jit(solution)/shard_map/reduce_scatter | solution.py:333
  541.5 895.3 %reduce-scatter.27.cloned.1.call-start = ((), (), s32[]{:S(2)}) async-start(), calls=%async_computation.23 | async-start | bytes 3538944 | tf_op jit(solution)/shard_map/reduce_scatter | solution.py:330
  549.7 935.3 %reduce-scatter.25.cloned.1.call-start = ((), (), s32[]{:S(2)}) async-start(), calls=%async_computation.22 | async-start | bytes 3538944 | tf_op jit(solution)/shard_map/reduce_scatter | solution.py:327
  557.8 106.6 %copy-start.13 = (bf16[1536,512]{1,0:T(8,128)(2,1)S(1)}, bf16[1536,512]{1,0:T(8,128)(2,1)}, u32[]{:S(2)}) copy-start(bf16[1536,512]{1,0:T(8,128)(2,1)} %param.22) | copy-start | bytes 4718596
  557.8 976.3 %all-reduce.8.cloned.1.call-start = ((), (), s32[]{:S(2)}) async-start(), calls=%async_computation.26 | async-start | bytes 215040 | tf_op jit(solution)/shard_map/psum | solution.py:371
  666.1 320.3 %copy-start.54 = (f32[128]{0:T(128)S(1)}, f32[128]{0:T(128)}, u32[]{:S(2)}) copy-start(f32[128]{0:T(128)} %copy-done.53) | copy-start | bytes 1540
  986.4 590.3 %all-reduce.10.cloned.1.call-start = ((), (), s32[]{:S(2)}) async-start(), calls=%async_computation.27 | async-start | bytes 589824 | tf_op jit(solution)/shard_map/psum | solution.py:370
  1324.9 255.0 %copy-start.1 = (bf16[2,512,1536]{2,1,0:T(8,128)(2,1)S(1)}, bf16[2,512,1536]{2,1,0:T(8,128)(2,1)}, u32[]{:S(2)}) copy-start(bf16[2,512,1536]{2,1,0:T(8,128)(2,1)} %param.30) | copy-start | bytes 9437188
  (38 other events, 93.9 us)
Sparse Core Ops, SparseCore 0:
  12.0 37.2 all-gather.2
  51.5 38.0 all-gather.4
  444.9 36.6 reduce-scatter.14
  483.8 37.8 reduce-scatter.12
  524.5 138.4 reduce-scatter.30
  665.3 159.8 reduce-scatter.20
  827.6 158.7 reduce-scatter.18
  988.9 167.3 reduce-scatter.22
  1158.8 166.0 reduce-scatter.16
  1327.3 61.2 reduce-scatter.28
  1391.1 45.6 reduce-scatter.26
  1439.2 45.7 reduce-scatter.24
  1489.2 44.8 all-reduce.7
  1536.5 40.1 all-reduce.9
where the time goes:
time: 1600 us; the launch traced here: 1590 us
  waiting for transfers between devices  1160 us (72%)
  matrix products  121 us (8%)
  local copies, waits for them, and re-layouts  109 us (7%)
  other arithmetic  68.3 us (4%)
  blocking collectives  65.8 us (4%)
  starting transfers between devices  45.7 us (3%)
    reduce_scatter x1, waiting for transfers between devices, shards(): lax.psum_scatter(dense_terms[3].astype(jnp.bfloat16), ('context', 'dp'),...  170 us
    reduce_scatter x1, waiting for transfers between devices, shards(): lax.psum_scatter(dense_terms[0].astype(jnp.bfloat16), ('context', 'dp'),...  169 us
    reduce_scatter x1, waiting for transfers between devices, shards(): lax.psum_scatter(dense_terms[1].astype(jnp.bfloat16), ('context', 'dp'),...  161 us
    unnamed x15, waiting for transfers between devices  100 us
    reduce_scatter x1, waiting for transfers between devices, shards(): lax.psum_scatter(dense_terms[2].astype(jnp.bfloat16), ('context', 'dp'),...  89.7 us
    unnamed x1, blocking collectives  65.8 us
    reduce_scatter x1, waiting for transfers between devices, shards(): lax.psum_scatter(grad_w_down.astype(jnp.bfloat16), 'context', scatter_dim...  61 us
    psum x1, waiting for transfers between devices, shards(): lax.psum(partial_sums[1].astype(jnp.bfloat16), 'expert').astype(jnp.float32)  47.1 us
  transfers between devices with their start and end apart: 18, of which 18 were waited for; matrix products, arithmetic and copies ran while one was open for 10% of the time, Pallas kernels for 0%

commit v1 on v0

--- a/solution.py
+++ b/solution.py
@@ -1,9 +1,313 @@
+import functools
 import math
 
 import jax
 import jax.numpy as jnp
 from jax import lax
+from jax.experimental import pallas as pl
+from jax.experimental.pallas import tpu as pltpu
 from jax.sharding import PartitionSpec as P
+
+MESH = pl.DeviceIdType.MESH
+BF = jnp.bfloat16
+F32 = jnp.float32
+
+
+class Place:
+    def __init__(self):
+        e, c = lax.axis_index("expert"), lax.axis_index("context")
+        self.hi, self.core = e // 2, e % 2
+        self.lo, self.y = c // 4, c % 4
+        self.z = lax.axis_index("dp")
+
+    def at(self, hi=0, core=0, lo=0, y=0, z=0):
+        e = (self.hi + hi) % 2 * 2 + (self.core + core) % 2
+        c = (self.lo + lo) % 2 * 4 + (self.y + y) % 4
+        return (e, c, (self.z + z) % 4)
+
+    def line(self, axis):
+        if axis == "y":
+            return [((self.y + d) % 4, self.at(y=d)) for d in (1, 2, 3)]
+        if axis == "z":
+            return [((self.z + d) % 4, self.at(z=d)) for d in (1, 2, 3)]
+        return [
+            ((self.hi + a) % 2 * 2 + (self.lo + b) % 2, self.at(hi=a, lo=b))
+            for a, b in ((0, 1), (1, 0), (1, 1))
+        ]
+
+    def own(self, axis):
+        return {"y": self.y, "z": self.z, "x": self.hi * 2 + self.lo}[axis]
+
+
+def greet(devices):
+    barrier = pltpu.get_barrier_semaphore()
+    for device in devices:
+        pl.semaphore_signal(barrier, inc=1, device_id=device, device_id_type=MESH)
+    pl.semaphore_wait(barrier, len(devices))
+
+
+def send(src, dst, sems, device):
+    copy = pltpu.make_async_remote_copy(
+        src_ref=src, dst_ref=dst, send_sem=sems[0], recv_sem=sems[1],
+        device_id=device, device_id_type=MESH,
+    )
+    copy.start()
+    return copy
+
+
+def scatter_start(place, axis, src, landing, sems, begin):
+    copies = []
+    for d, (index, device) in enumerate(place.line(axis)):
+        pair = (sems.at[0, begin + d], sems.at[1, begin + d])
+        copies.append(send(src.at[index], landing.at[d], pair, device))
+    return copies
+
+
+def add_up(out, own, landing, lead):
+    count = landing.shape[0]
+
+    def body(i, carry):
+        total = own[i].astype(F32)
+        for d in range(count):
+            total = total + landing[d, i].astype(F32)
+        out[i] = total.astype(out.dtype)
+        return carry
+
+    lax.fori_loop(0, lead, body, 0)
+
+
+WIDE = 384
+ORDERS = {"o": "xyz", "q": "zyx", "s": "yzx"}
+
+
+def stream_index(order, block, half):
+    at = {"x": half * 2 + block // 16, "y": block // 4 % 4, "z": block % 4}
+    return tuple(at[axis] for axis in order)
+
+
+def fill_stream(out, order, left, right, width):
+    for half in range(2):
+        columns = right[:, half * width : (half + 1) * width]
+        for tile in range(4):
+            grads = lax.dot_general(
+                left[:, tile * 384 : (tile + 1) * 384], columns,
+                (((0,), (0,)), ((), ())), preferred_element_type=F32,
+            ).astype(BF)
+            for j in range(8):
+                index = stream_index(order, tile * 8 + j, half)
+                out[(*index, slice(None), slice(0, width))] = grads[j * 48 : (j + 1) * 48]
+
+
+def reduce_kernel(
+    n1, attn, dq, dkv, dbr, narrow, eg, eu, ed,
+    gq, gk, gv, go, gs, og, ou, od,
+    n1c, attnc, dqc, dkvc, dbrc, pair_sems,
+    send_o, send_q, send_s, land1_o, land1_q, land1_s, mid_o, mid_q, mid_s,
+    land2_o, land2_q, land2_s, last_o, last_q, last_s, land3_o, land3_q, land3_s, dense_sems,
+    mine, quarters, quarter_sems,
+    own_p, own_q, land_p1, land_q1, sum_p, sum_q, land_p2, land_q2, expert_sems, local_sems,
+):
+    place = Place()
+    y_line, z_line, x_line = (place.line(axis) for axis in "yzx")
+    sibling = place.at(core=1)
+    cross = place.at(hi=1, core=1)
+    greet([device for line in (y_line, z_line, x_line) for _, device in line] + [sibling, cross])
+    pending = []
+
+    pairs = []
+    for i, (rows, both, part) in enumerate(
+        ((attn, attnc, None), (dbr, dbrc, 1), (n1, n1c, None), (dq, dqc, 1), (dkv, dkvc, 1))
+    ):
+        source = rows if part is None else rows.at[1 - place.core]
+        pair = (pair_sems.at[0, i], pair_sems.at[1, i])
+        pairs.append(send(source, both.at[pl.ds(128, 128)], pair, sibling))
+        both[0:128, :] = rows[...] if part is None else rows[place.core]
+
+    mats = (eg, eu, ed)
+    stage_p, stage_q = [], []
+    other_lo = (place.lo + 1) % 2
+    lo_device = place.at(lo=1)
+    at = 0
+    for m, mat in enumerate(mats):
+        for d, (index, device) in enumerate(y_line):
+            pair = (expert_sems.at[0, at], expert_sems.at[1, at])
+            stage_p.append(send(mat.at[0, :, index], land_p1.at[d, m], pair, device))
+            at += 1
+        pair = (expert_sems.at[0, at], expert_sems.at[1, at])
+        stage_q.append(send(mat.at[1, other_lo], land_q1.at[m], pair, lo_device))
+        at += 1
+    local = []
+    for m, mat in enumerate(mats):
+        local.append(pltpu.make_async_copy(mat.at[0, :, place.y], own_p.at[m], local_sems.at[0, m]))
+        local.append(pltpu.make_async_copy(mat.at[1, place.lo], own_q.at[m], local_sems.at[1, m]))
+    for copy in local:
+        copy.start()
+
+    sends = {"o": send_o, "q": send_q, "s": send_s}
+    lands = {
+        "o": (land1_o, land2_o, land3_o), "q": (land1_q, land2_q, land3_q),
+        "s": (land1_s, land2_s, land3_s),
+    }
+    mids = {"o": (mid_o, last_o), "q": (mid_q, last_q), "s": (mid_s, last_s)}
+    begin = {"o": 0, "q": 9, "s": 18}
+    flight = {}
+
+    def launch(name, phase):
+        source = sends[name] if phase == 0 else mids[name][phase - 1]
+        flight[name] = scatter_start(
+            place, ORDERS[name][phase], source, lands[name][phase], dense_sems,
+            begin[name] + 3 * phase,
+        )
+
+    def land(name, phase):
+        for copy in flight[name]:
+            copy.wait_recv()
+        pending.extend(flight[name])
+        source = sends[name] if phase == 0 else mids[name][phase - 1]
+        own = source.at[place.own(ORDERS[name][phase])]
+        landing = lands[name][phase]
+        if phase == 0:
+            out = mids[name][0]
+
+            def body(i, carry):
+                a, b = i // 4, i % 4
+                total = own[a, b].astype(F32)
+                for d in range(3):
+                    total = total + landing[d, a, b].astype(F32)
+                out[a, b] = total.astype(BF)
+                return carry
+
+            lax.fori_loop(0, 16, body, 0)
+        elif phase == 1:
+            add_up(mids[name][1], own, landing, 4)
+        else:
+            total = own[...].astype(F32)
+            for d in range(3):
+                total = total + landing[d].astype(F32)
+            mine["oqs".index(name)] = total.astype(BF)
+
+    for copy in pairs[:2]:
+        copy.wait_recv()
+    fill_stream(send_o, ORDERS["o"], attnc, dbrc, 384)
+    launch("o", 0)
+    for copy in pairs[2:4]:
+        copy.wait_recv()
+    fill_stream(send_q, ORDERS["q"], n1c, dqc, 384)
+    launch("q", 0)
+    pairs[4].wait_recv()
+    fill_stream(send_s, ORDERS["s"], n1c, dkvc, 256)
+    for block in range(32):
+        for half in range(2):
+            index = stream_index(ORDERS["s"], block, half)
+            send_s[(*index, slice(None), slice(256, 384))] = narrow[block * 48 : (block + 1) * 48, :]
+    launch("s", 0)
+    pending.extend(pairs)
+    for phase in range(3):
+        for name in "oqs":
+            land(name, phase)
+            if phase < 2:
+                launch(name, phase + 1)
+
+    own_quarter = place.core * 2 + place.hi
+    gathered = []
+    for i, (a, b) in enumerate(((0, 1), (1, 0), (1, 1))):
+        pair = (quarter_sems.at[0, i], quarter_sems.at[1, i])
+        gathered.append(send(mine, quarters.at[own_quarter], pair, place.at(hi=a, core=b)))
+    quarters[own_quarter] = mine[...]
+
+    for copy in stage_p + stage_q:
+        copy.wait_recv()
+    for copy in local:
+        copy.wait()
+    pending.extend(stage_p + stage_q)
+
+    def fold_p(i, carry):
+        m, lo, part = i // 8, i // 4 % 2, pl.ds(i % 4 * 48, 48)
+        total = own_p[m, lo, part].astype(F32)
+        for d in range(3):
+            total = total + land_p1[d, m, lo, part].astype(F32)
+        sum_p[lo, m, part] = total.astype(BF)
+        return carry
+
+    lax.fori_loop(0, 24, fold_p, 0)
+    pair = (expert_sems.at[0, 12], expert_sems.at[1, 12])
+    second = [send(sum_p.at[other_lo], land_p2, pair, lo_device)]
+
+    def fold_q(i, carry):
+        m, y, part = i // 16, i // 4 % 4, pl.ds(i % 4 * 48, 48)
+        total = own_q[m, y, part].astype(F32) + land_q1[m, y, part].astype(F32)
+        sum_q[y, m, part] = total.astype(BF)
+        return carry
+
+    lax.fori_loop(0, 48, fold_q, 0)
+    for d, (index, device) in enumerate(y_line):
+        pair = (expert_sems.at[0, 13 + d], expert_sems.at[1, 13 + d])
+        second.append(send(sum_q.at[index], land_q2.at[d], pair, device))
+
+    for copy in gathered:
+        copy.wait_recv()
+    pending.extend(gathered)
+    for q in range(4):
+        go[:, q * 384 : (q + 1) * 384] = quarters[q, 0].astype(F32)
+        gq[:, q * 384 : (q + 1) * 384] = quarters[q, 1].astype(F32)
+        gk[:, q * 128 : (q + 1) * 128] = quarters[q, 2, :, 0:128].astype(F32)
+        gv[:, q * 128 : (q + 1) * 128] = quarters[q, 2, :, 128:256].astype(F32)
+    gs[...] = quarters[0, 2, :, 256:384].astype(F32) + quarters[2, 2, :, 256:384].astype(F32)
+
+    for copy in second:
+        copy.wait_recv()
+    pending.extend(second)
+    for m, out in enumerate((og, ou, od)):
+        def finish(i, carry):
+            part = pl.ds(i * 48, 48)
+            out[0, part] = sum_p[place.lo, m, part].astype(F32) + land_p2[m, part].astype(F32)
+            total = sum_q[place.y, m, part].astype(F32)
+            for d in range(3):
+                total = total + land_q2[d, m, part].astype(F32)
+            out[1, part] = total
+            return carry
+
+        lax.fori_loop(0, 4, finish, 0)
+    for copy in pending:
+        copy.wait_send()
+
+
+def reduce_gradients(n1, attn, dq, dkv, dbr, narrow, eg, eu, ed):
+    vmem = pl.BlockSpec(memory_space=pltpu.VMEM)
+    sems = pltpu.SemaphoreType.DMA
+    f32 = lambda *shape: jax.ShapeDtypeStruct(shape, F32)
+    low = lambda *shape: pltpu.VMEM(shape, BF)
+    streams = 3
+    return pl.pallas_call(
+        reduce_kernel,
+        out_shape=(
+            f32(48, 1536), f32(48, 512), f32(48, 512), f32(48, 1536), f32(48, 128),
+            f32(2, 192, 512), f32(2, 192, 512), f32(2, 192, 512),
+        ),
+        in_specs=[vmem] * 6 + [pl.BlockSpec(memory_space=pl.ANY)] * 3,
+        out_specs=[vmem] * 8,
+        scratch_shapes=[
+            low(256, 1536), low(256, 1536), low(256, 768), low(256, 512), low(256, 768),
+            sems((2, 5)),
+            *[low(4, 4, 4, 48, WIDE)] * streams,
+            *[low(3, 4, 4, 48, WIDE)] * streams,
+            *[low(4, 4, 48, WIDE)] * streams,
+            *[low(3, 4, 48, WIDE)] * streams,
+            *[low(4, 48, WIDE)] * streams,
+            *[low(3, 48, WIDE)] * streams,
+            sems((2, 27)),
+            low(3, 48, WIDE), low(4, 3, 48, WIDE), sems((2, 3)),
+            low(3, 2, 192, 512), low(3, 4, 192, 512),
+            low(3, 3, 2, 192, 512), low(3, 4, 192, 512),
+            low(2, 3, 192, 512), low(4, 3, 192, 512),
+            low(3, 192, 512), low(3, 3, 192, 512),
+            sems((2, 16)), sems((2, 3)),
+        ],
+        compiler_params=pltpu.CompilerParams(
+            collective_id=0, has_side_effects=True, vmem_limit_bytes=60 << 20
+        ),
+    )(n1, attn, dq, dkv, dbr, narrow, eg, eu, ed)
+
 
 HEADS = 24
 KV_HEADS = 8
@@ -249,7 +553,7 @@
     active_full, act_pull = jax.vjp(activate, hidden_gate, hidden_up)
     active = active_full.astype(jnp.bfloat16)
     grad_w_down = jnp.einsum(
-        "sxcf,sxcd->xfd", active, grad_grouped, preferred_element_type=jnp.float32
+        "sxcd,sxcf->xdf", grad_grouped, active, preferred_element_type=jnp.float32
     )
     grad_active = jnp.einsum(
         "sxcd,xfd->sxcf", grad_grouped, w_down, preferred_element_type=jnp.float32
@@ -323,71 +627,33 @@
     _, norm_first_pull = jax.vjp(normalize, x_rows, gain_attn)
     grad_x_norm, grad_gain_attn = norm_first_pull(grad_n_first)
     grad_input = grad_mid + grad_x_norm
-    expert_sums = (
-        lax.psum_scatter(
-            grad_w_gate.astype(jnp.bfloat16), "context", scatter_dimension=1, tiled=True
-        ).astype(jnp.float32),
-        lax.psum_scatter(
-            grad_w_up.astype(jnp.bfloat16), "context", scatter_dimension=1, tiled=True
-        ).astype(jnp.float32),
-        lax.psum_scatter(
-            grad_w_down.astype(jnp.bfloat16), "context", scatter_dimension=2, tiled=True
-        ).astype(jnp.float32),
-    )
-    dense_terms = (
-        grad_w_query,
-        grad_w_key,
-        grad_w_value,
-        grad_w_out,
-        grad_gain_attn,
-        grad_gain_moe,
-        grad_w_router,
-    )
-    partial_sums = (
-        lax.psum_scatter(
-            dense_terms[0].astype(jnp.bfloat16), ("context", "dp"), scatter_dimension=0, tiled=True
-        ).astype(jnp.float32),
-        lax.psum_scatter(
-            dense_terms[1].astype(jnp.bfloat16), ("context", "dp"), scatter_dimension=0, tiled=True
-        ).astype(jnp.float32),
-        lax.psum_scatter(
-            dense_terms[2].astype(jnp.bfloat16), ("context", "dp"), scatter_dimension=0, tiled=True
-        ).astype(jnp.float32),
-        lax.psum_scatter(
-            dense_terms[3].astype(jnp.bfloat16), ("context", "dp"), scatter_dimension=0, tiled=True
-        ).astype(jnp.float32),
-        lax.psum_scatter(
-            dense_terms[4].astype(jnp.bfloat16), ("context", "dp"), scatter_dimension=0, tiled=True
-        ).astype(jnp.float32),
-        lax.psum_scatter(
-            dense_terms[5].astype(jnp.bfloat16), ("context", "dp"), scatter_dimension=0, tiled=True
-        ).astype(jnp.float32),
-        lax.psum_scatter(
-            dense_terms[6].astype(jnp.bfloat16), ("context", "dp"), scatter_dimension=0, tiled=True
-        ).astype(jnp.float32),
-    )
-    dense_sums = (
-        lax.psum(partial_sums[0].astype(jnp.bfloat16), "expert").astype(jnp.float32),
-        lax.psum(partial_sums[1].astype(jnp.bfloat16), "expert").astype(jnp.float32),
-        lax.psum(partial_sums[2].astype(jnp.bfloat16), "expert").astype(jnp.float32),
-        lax.psum(partial_sums[3].astype(jnp.bfloat16), "expert").astype(jnp.float32),
-        lax.psum(partial_sums[4].astype(jnp.bfloat16), "expert").astype(jnp.float32),
-        lax.psum(partial_sums[5].astype(jnp.bfloat16), "expert").astype(jnp.float32),
-        lax.psum(partial_sums[6].astype(jnp.bfloat16), "expert").astype(jnp.float32),
+    halves = lambda rows: rows.reshape(row_count, 2, -1).transpose(1, 0, 2)
+    grad_kv = jnp.stack(
+        [grad_k_raw.reshape(row_count, 2, 2, 128), grad_v_raw.reshape(row_count, 2, 2, 128)],
+        axis=3,
+    )
+    grad_kv = grad_kv.transpose(1, 0, 2, 3, 4).reshape(2, row_count, kv_width)
+    narrow = jnp.concatenate(
+        [grad_w_router, grad_gain_attn[:, None], grad_gain_moe[:, None],
+         jnp.zeros((model_width, 94), jnp.float32)], axis=1).astype(jnp.bfloat16)
+    blocks = lambda grads: grads.astype(jnp.bfloat16).reshape(local_experts, 2, 4, 192, -1)
+    sums = reduce_gradients(
+        n_first, attn_low, halves(grad_q_raw), grad_kv, halves(grad_branch), narrow,
+        blocks(grad_w_gate), blocks(grad_w_up), blocks(grad_w_down),
     )
     return (
         y_out.astype(jnp.bfloat16)[None],
         grad_input[None],
-        dense_sums[0],
-        dense_sums[1],
-        dense_sums[2],
-        dense_sums[3],
-        dense_sums[4],
-        dense_sums[5],
-        dense_sums[6],
-        expert_sums[0],
-        expert_sums[1],
-        expert_sums[2],
+        sums[0],
+        sums[1],
+        sums[2],
+        sums[3],
+        sums[4][:, 32],
+        sums[4][:, 33],
+        sums[4][:, :32],
+        sums[5],
+        sums[6],
+        sums[7].transpose(0, 2, 1),
     )
 
 

time: 1600 us -> 698 us (0.44)
  waiting for transfers between devices: 1160 us -> 209 us
  Pallas kernels: 0 us -> 137 us
  blocking collectives: 65.8 us -> 0 us
    reduce_scatter x7 -> x0, waiting for transfers between devices: 743 us -> none  [the longest x1 170 us: shards(): lax.psum_scatter(dense_terms[3].astype(jnp.bfloat16), ('context', 'dp'),...]
    pallas_call x0 -> x1, Pallas kernels: none -> 137 us  [reduce_gradients(): pl.pallas_call(reduce_kernel, out_shape=(f32(48, 1536), f32(48, 512), f32...]
    unnamed x15 -> x4, waiting for transfers between devices: 100 us -> 0.07 us
    psum x2 -> x0, waiting for transfers between devices: 83.2 us -> none  [the longest x1 47.1 us: shards(): lax.psum(partial_sums[1].astype(jnp.bfloat16), 'expert').astype(jnp.float32)]
    unnamed x1 -> x0, blocking collectives: 65.8 us -> none
    reduce_scatter x1, waiting for transfers between devices: 37.3 us -> 6.77 us  [shards(): lax.psum_scatter(grad_key_all.astype(jnp.bfloat16), 'context', scatter_di...]
  transfers between devices with their start and end apart: 18 -> 8, of which waited for: 18 -> 8; matrix products, arithmetic and copies ran while one was open for 10% -> 19% of each run, Pallas kernels for 0% -> 0%
where the time goes in v1:
time: 698 us; the launch traced here: 685 us
  waiting for transfers between devices  209 us (30%)
  Pallas kernels  137 us (20%)
  local copies, waits for them, and re-layouts  114 us (16%)
  matrix products  110 us (16%)
  other arithmetic  54.6 us (8%)
  starting transfers between devices  45 us (6%)
  between operations  15.3 us (2%)
    pallas_call x1, Pallas kernels, reduce_gradients(): pl.pallas_call(reduce_kernel, out_shape=(f32(48, 1536), f32(48, 512), f32...  137 us
    reduce_scatter x1, waiting for transfers between devices, shards(): lax.psum_scatter(grad_value_all.astype(jnp.bfloat16), 'context', scatter_...  39.1 us
    all_gather x1, waiting for transfers between devices, shards(): lax.all_gather(key_rows, 'context', axis=0, tiled=True)  38 us
    all_to_all x1, waiting for transfers between devices, shards(): lax.all_to_all(produced, ('expert', 'dp'), split_axis=0, concat_axis=0, t...  37.2 us
    all_to_all x1, waiting for transfers between devices, shards(): lax.all_to_all(dispatch_rows(weighted), ('expert', 'dp'), split_axis=0, c...  32.7 us
    all_to_all x1, waiting for transfers between devices, shards(): lax.all_to_all(grad_rows, ('expert', 'dp'), split_axis=0, concat_axis=0,...  29.1 us
    unnamed x161, local copies, waits for them, and re-layouts  24.9 us
    all_to_all x1, waiting for transfers between devices, shards(): lax.all_to_all(dispatch_rows(spread), ('expert', 'dp'), split_axis=0, con...  24.2 us
  transfers between devices with their start and end apart: 8, of which 8 were waited for; matrix products, arithmetic and copies ran while one was open for 19% of the time, Pallas kernels for 0%

profile of v1, /device:TPU:1, one launch (start us, length us, event | category | flops | bytes accessed | tf_op | source)
XLA Modules:
  0.0 685.1 jit_solution(8245599209274980356)
XLA Ops:
  11.1 2.4 convolution_convert_fusion.3
  13.6 2.6 copy.166
  37.4 6.6 copy.168
  44.6 3.9 fusion.90
  50.8 2.3 copy.170
  53.1 38.0 %all-gather.5.cloned.1.call-done = bf16[1024,512]{1,0:T(8,128)(2,1)} async-done(((bf16[128,512]{1,0:T(8,128)(2,1)}), bf16[1024,512]{1,0:T(8,128)(2,1)}) %all-gather.5.cloned.1.call-update) | async-done | bytes 1048592 | tf_op jit(solution)/shard_map/all_gather | solution.py:488
  91.1 2.3 copy.171
  93.4 12.3 %while.39 = (s32[]{:T(128)}, f32[8,3,128]{2,1,0:T(4,128)S(1)}, f32[8,3,128]{2,1,0:T(4,128)}, s32[2]{0:T(128)}, bf16[2,512,512]{1,2,0:T(8,128)(2,1)}, /*index=5*/...) while((s32[]{:T(128)}, f32[8,3,128]{2,1,0:T(4,128)S(1)}, ...), condition=%wide.region_4.5_spmd.clone, body=%wide.region_1.4_spmd.clone.sunk | while | flops 212418176 | bytes 15008960 | solution.py:377
  105.8 18.4 %while.40 = (s32[]{:T(128)}, f32[128,8,3,64]{0,3,2,1:T(8,128)}, bf16[2,512,512]{1,2,0:T(8,128)(2,1)}, s32[2]{0:T(128)}, bf16[2,512,512]{1,2,0:T(8,128)(2,1)}, /*...) while((s32[]{:T(128)}, f32[128,8,3,64]{0,3,2,1:T(8,128)}, ...), condition=%wide.region_6.7_spmd.clone, body=%wide.region_5.6_spmd.clone.sunk | while | flops 410976896 | bytes 5272727 | solution.py:390
  110.7 4.1 fusion.179
  119.7 4.4 fusion.179
  125.5 3.5 multiply_reduce_fusion.2
  130.0 8.3 %scatter_custom_fusion = bf16[1280,1536]{1,0:T(8,128)(2,1)} fusion(s32[1024]{0:T(1024)} %bitcast.427, bf16[]{:T(256)} %constant.106.clone.1, bf16[128,1536]{1,0:T(8,128)(2,1)S(1)} %multiply_convert_fusion), kind=kCustom, calls=%fused_computation.85 | custom fusion | bytes 4325888 | tf_op jit(solution)/shard_map/scatter | solution.py:513
  138.3 12.2 %all-to-all-start = ((bf16[32,40,1536]{2,1,0:T(8,128)(2,1)}), bf16[32,40,1536]{2,1,0:T(8,128)(2,1)}, u32[]{:S(2)}, u32[]{:S(2)}) async-start(bf16[32,40,1536]{2,1,0:T(8,128)(2,1)} %bitcast.396), calls=%async_computation | async-start | bytes 7864320 | tf_op jit(solution)/shard_map/all_to_all | solution.py:525
  155.4 7.1 %gather_fusion.2 = f32[1024]{0:T(1024)S(1)} fusion(f32[128,32]{0,1:T(8,128)S(1)} %fusion.107, s32[1024]{0:T(1024)S(1)} %reshape.629), kind=kCustom, calls=%fused_computation.2 | custom fusion | bytes 16384 | tf_op jit(solution)/shard_map/jvp(jit(take_along_axis))/gather | solution.py:500
  163.3 8.5 %scatter_custom_fusion.1 = bf16[1280,1536]{1,0:T(8,128)(2,1)} fusion(s32[1024]{0:T(1024)S(1)} %bitcast.428, f32[128,1536]{1,0:T(8,128)} %bitcast_convert_fusion.3, f32[1024]{0:T(1024)S(1)} %exponential_divide_fusion, bf16[]{:T(256)} %constant.106.clone.1), kind=kCustom, calls=%fused_computation.77 | custom fusion | flops 3145728 | bytes 4722690 | tf_op jit(solution)/shard_map/scatter | solution.py:513
  171.8 24.2 %all-to-all-done = bf16[32,40,1536]{2,1,0:T(8,128)(2,1)} async-done(((bf16[32,40,1536]{2,1,0:T(8,128)(2,1)}), bf16[32,40,1536]{2,1,0:T(8,128)(2,1)}, u32[]{:S(2)}, u32[]{:S(2)}) %all-to-all-start) | async-done | bytes 3932192 | tf_op jit(solution)/shard_map/all_to_all | solution.py:525
  196.0 11.1 %all-to-all-start.2 = ((bf16[32,40,1536]{2,1,0:T(8,128)(2,1)}), bf16[32,40,1536]{2,1,0:T(8,128)(2,1)}, u32[]{:S(2)}, u32[]{:S(2)}) async-start(bf16[32,40,1536]{2,1,0:T(8,128)(2,1)} %bitcast.397), calls=%async_computation.2 | async-start | bytes 7864320 | tf_op jit(solution)/shard_map/all_to_all | solution.py:542
  207.2 6.9 %fusion.41 = f32[2,16,40,512]{3,2,1,0:T(8,128)} fusion(bf16[16,2,40,1536]{3,2,1,0:T(8,128)(2,1)} %bitcast.21, bf16[2,1536,512]{2,1,0:T(8,128)(2,1)} %param.29), kind=kOutput, calls=%fused_computation.73 | convolution fusion | flops 2013265920 | bytes 9699328 | tf_op jit(solution)/shard_map/sxcd,xdf->sxcf/dot_general | solution.py:530
  214.1 5.9 fusion.43
  220.0 32.7 %all-to-all-done.2 = bf16[32,40,1536]{2,1,0:T(8,128)(2,1)} async-done(((bf16[32,40,1536]{2,1,0:T(8,128)(2,1)}), bf16[32,40,1536]{2,1,0:T(8,128)(2,1)}, u32[]{:S(2)}, u32[]{:S(2)}) %all-to-all-start.2) | async-done | bytes 3932192 | tf_op jit(solution)/shard_map/all_to_all | solution.py:542
  252.7 8.4 %fusion.61 = (bf16[16,2,40,512]{3,2,0,1:T(8,128)(2,1)}, bf16[16,2,40,512]{3,2,0,1:T(8,128)(2,1)}, bf16[16,2,40,512]{3,2,0,1:T(8,128)(2,1)S(1)}) fusion(f32[2,16,40,512]{3,2,1,0:T(8,128)} %fusion.43, f32[2,16,40,512]{3,2,1,0:T(8,128)} %fusion.41, bf16[2,512,1536]{2,1,0:T(8,128)(2,1)S(1)} %copy-done, bf16[16,2,40,1536]{3,2,1,0:T(8,128)(2,1)} %bitcast.39), kind=kOutput, calls=%fused_computation.94 | convolution fusion | flops 2023751680 | bytes 16252928 | tf_op jit(solution)/shard_map/sxcd,xfd->sxcf/dot_general | solution.py:558
  263.4 2.4 copy.182
  265.7 10.7 %all-to-all-start.1 = ((bf16[32,40,1536]{2,1,0:T(8,128)(2,1)}), bf16[32,40,1536]{2,1,0:T(8,128)(2,1)}, u32[]{:S(2)}, u32[]{:S(2)}) async-start(bf16[32,40,1536]{2,1,0:T(8,128)(2,1)} %bitcast.398), calls=%async_computation.1 | async-start | bytes 7864320 | tf_op jit(solution)/shard_map/all_to_all | solution.py:534
  276.5 3.7 fusion.49
  284.8 37.2 %all-to-all-done.1 = bf16[32,40,1536]{2,1,0:T(8,128)(2,1)} async-done(((bf16[32,40,1536]{2,1,0:T(8,128)(2,1)}), bf16[32,40,1536]{2,1,0:T(8,128)(2,1)}, u32[]{:S(2)}, u32[]{:S(2)}) %all-to-all-start.1) | async-done | bytes 3932192 | tf_op jit(solution)/shard_map/all_to_all | solution.py:534
  322.0 10.7 %all-to-all-start.3 = ((bf16[32,40,1536]{2,1,0:T(8,128)(2,1)}), bf16[32,40,1536]{2,1,0:T(8,128)(2,1)}, u32[]{:S(2)}, u32[]{:S(2)}) async-start(bf16[32,40,1536]{2,1,0:T(8,128)(2,1)} %bitcast.395), calls=%async_computation.3 | async-start | bytes 7864320 | tf_op jit(solution)/shard_map/all_to_all | solution.py:571
  335.0 9.3 %gather_fusion = bf16[1024,1536]{1,0:T(8,128)(2,1)S(1)} fusion(bf16[1280,1536]{1,0:T(8,128)(2,1)} %bitcast.32, s32[1024]{0:T(1024)S(1)} %broadcast_clamp_fusion), kind=kCustom, calls=%fused_computation | custom fusion | bytes 6295552 | tf_op jit(solution)/shard_map/gather | solution.py:518
  344.3 4.4 fusion.35
  349.1 29.1 %all-to-all-done.3 = bf16[32,40,1536]{2,1,0:T(8,128)(2,1)} async-done(((bf16[32,40,1536]{2,1,0:T(8,128)(2,1)}), bf16[32,40,1536]{2,1,0:T(8,128)(2,1)}, u32[]{:S(2)}, u32[]{:S(2)}) %all-to-all-start.3) | async-done | bytes 3932192 | tf_op jit(solution)/shard_map/all_to_all | solution.py:571
  378.2 9.9 %gather_fusion.1 = bf16[1024,1536]{1,0:T(8,128)(2,1)} fusion(bf16[1280,1536]{1,0:T(8,128)(2,1)} %bitcast.46, s32[1024]{0:T(1024)S(1)} %broadcast_clamp_fusion), kind=kCustom, calls=%fused_computation.1 | custom fusion | bytes 6295552 | tf_op jit(solution)/shard_map/gather | solution.py:518
  388.2 4.1 convert_reduce_fusion
  392.2 6.1 scatter_custom_fusion.2
  400.6 4.1 convolution_convert_fusion.1
  405.7 38.6 %while.41 = (s32[]{:T(128)}, f32[128,8,3,64]{0,3,2,1:T(8,128)}, bf16[2,512,512]{2,1,0:T(8,128)(2,1)}, bf16[2,512,512]{2,1,0:T(8,128)(2,1)}, bf16[2,512,512]{1,2,...) while((s32[]{:T(128)}, f32[128,8,3,64]{0,3,2,1:T(8,128)}, ...), condition=%wide.region_22.23_spmd.clone, body=%wide.region_21.22_spmd.clone.sunk | while | flops 1020396160 | bytes 44311936 | solution.py:430
  416.0 2.6 fusion.192
  418.6 2.9 fusion.194
  435.2 2.8 fusion.192
  438.0 2.9 fusion.194
  444.4 7.0 %bitcast_convert_fusion = bf16[2,1536,512]{2,1,0:T(8,128)(2,1)} fusion(bf16[16,2,40,1536]{3,2,1,0:T(8,128)(2,1)} %bitcast.39, bf16[16,2,40,512]{3,2,0,1:T(8,128)(2,1)} %copy-done.79), kind=kOutput, calls=%fused_computation.62 | convolution fusion | flops 2014838784 | bytes 8388608 | tf_op jit(solution)/shard_map/sxcd,sxcf->xdf/dot_general | solution.py:555
  451.4 7.2 %bitcast_convert_fusion.1 = bf16[2,1536,512]{2,1,0:T(8,128)(2,1)} fusion(bf16[16,2,40,1536]{3,2,1,0:T(8,128)(2,1)} %bitcast.21, bf16[16,2,40,512]{3,2,0,1:T(8,128)(2,1)S(1)} %copy-done.32), kind=kOutput, calls=%fused_computation.63 | convolution fusion | flops 2014838784 | bytes 8388608 | tf_op jit(solution)/shard_map/sxcd,sxcf->xdf/dot_general | solution.py:565
  458.6 6.9 %bitcast_convert_fusion.2 = bf16[2,1536,512]{2,1,0:T(8,128)(2,1)} fusion(bf16[16,2,40,1536]{3,2,1,0:T(8,128)(2,1)} %bitcast.21, bf16[16,2,40,512]{3,2,0,1:T(8,128)(2,1)S(1)} %copy-done.30), kind=kOutput, calls=%fused_computation.64 | convolution fusion | flops 2014838784 | bytes 8388608 | tf_op jit(solution)/shard_map/sxcd,sxcf->xdf/dot_general | solution.py:564
  469.2 5.0 fusion.108
  474.2 6.8 reduce-scatter.3.cloned.1.call-done
  482.1 39.1 %reduce-scatter.5.cloned.1.call-done = bf16[128,512]{1,0:T(8,128)(2,1)} async-done(((bf16[1024,512]{1,0:T(8,128)(2,1)}), bf16[128,512]{1,0:T(8,128)(2,1)}) %reduce-scatter.5.cloned.1.call-update) | async-done | bytes 131088 | tf_op jit(solution)/shard_map/reduce_scatter | solution.py:608
  525.2 3.0 fusion.79
  530.2 136.9 %shard_map.220 = (f32[48,1536]{1,0:T(8,128)}, f32[48,512]{1,0:T(8,128)}, f32[48,512]{1,0:T(8,128)}, f32[48,1536]{1,0:T(8,128)}, f32[48,128]{1,0:T(8,128)}, /*ind...) custom-call(bf16[128,1536]{1,0:T(8,128)(2,1)} %copy-done.17, bf16[128,1536]{1,0:T(8,128)(2,1)} %copy.204.attn, ...), custom_call_target="tpu_custom_call" | custom-call | tf_op jit(solution)/shard_map/pallas_call | solution.py:281
  670.2 2.6 fusion.86
  (338 shorter events, 116.7 us)
Async XLA Ops:
  7.2 245.5 %copy-start = (bf16[2,512,1536]{2,1,0:T(8,128)(2,1)S(1)}, bf16[2,512,1536]{2,1,0:T(8,128)(2,1)}, u32[]{:S(2)}) copy-start(bf16[2,512,1536]{2,1,0:T(8,128)(2,1)} %param.30) | copy-start | bytes 9437188
  7.2 43.6 %all-gather.3.cloned.1.call-start = ((), (), s32[]{:S(2)}) async-start(), calls=%async_computation.6 | async-start | bytes 1179648 | tf_op jit(solution)/shard_map/all_gather | solution.py:489
  9.1 7.9 %copy-start.10 = (bf16[1,128,1536]{2,1,0:T(8,128)(2,1)S(1)}, bf16[1,128,1536]{2,1,0:T(8,128)(2,1)}, u32[]{:S(2)}) copy-start(bf16[1,128,1536]{2,1,0:T(8,128)(2,1)} %param.19) | copy-start | bytes 1179652
  9.1 7.9 %copy-start.49 = (f32[1536]{0:T(1024)S(1)}, f32[1536]{0:T(1024)}, u32[]{:S(2)}) copy-start(f32[1536]{0:T(1024)} %param.25) | copy-start | bytes 18436
  9.1 9.9 %copy-start.66 = (f32[128]{0:T(128)}, f32[128]{0:T(128)S(1)}, u32[]{:S(2)}) copy-start(f32[128]{0:T(128)S(1)} %fusion.103) | copy-start | bytes 1540
  13.5 77.6 %all-gather.5.cloned.1.call-start = ((), (), s32[]{:S(2)}) async-start(), calls=%async_computation.7 | async-start | bytes 1179648 | tf_op jit(solution)/shard_map/all_gather | solution.py:488
  130.0 8.3 %copy-start.15 = (bf16[128,1536]{1,0:T(8,128)(2,1)}, bf16[128,1536]{1,0:T(8,128)(2,1)S(1)}, u32[]{:S(2)}) copy-start(bf16[128,1536]{1,0:T(8,128)(2,1)S(1)} %multiply_convert_fusion) | copy-start | bytes 1179652
  138.3 57.7 %all-to-all-start = ((bf16[32,40,1536]{2,1,0:T(8,128)(2,1)}), bf16[32,40,1536]{2,1,0:T(8,128)(2,1)}, u32[]{:S(2)}, u32[]{:S(2)}) async-start(bf16[32,40,1536]{2,1,0:T(8,128)(2,1)} %bitcast.396), calls=%async_computation | async-start | bytes 7864320 | tf_op jit(solution)/shard_map/all_to_all | solution.py:525
  155.4 7.8 %copy-start.65 = (s32[1024,1]{0,1:T(1,128)S(1)}, s32[1024,1]{0,1:T(1,128)}, u32[]{:S(2)}) copy-start(s32[1024,1]{0,1:T(1,128)} %compare_select_fusion.1) | copy-start | bytes 12292
  196.0 56.7 %all-to-all-start.2 = ((bf16[32,40,1536]{2,1,0:T(8,128)(2,1)}), bf16[32,40,1536]{2,1,0:T(8,128)(2,1)}, u32[]{:S(2)}, u32[]{:S(2)}) async-start(bf16[32,40,1536]{2,1,0:T(8,128)(2,1)} %bitcast.397), calls=%async_computation.2 | async-start | bytes 7864320 | tf_op jit(solution)/shard_map/all_to_all | solution.py:542
  207.1 7.0 %copy-start.26 = (bf16[2,1536,512]{2,1,0:T(8,128)(2,1)S(1)}, bf16[2,1536,512]{2,1,0:T(8,128)(2,1)}, u32[]{:S(2)}) copy-start(bf16[2,1536,512]{2,1,0:T(8,128)(2,1)} %param.28) | copy-start | bytes 9437188
  265.7 10.7 %copy-start.27 = (bf16[2,1536,512]{2,1,0:T(8,128)(2,1)S(1)}, bf16[2,1536,512]{2,1,0:T(8,128)(2,1)}, u32[]{:S(2)}) copy-start(bf16[2,1536,512]{2,1,0:T(8,128)(2,1)} %param.28) | copy-start | bytes 9437188
  265.7 56.2 %all-to-all-start.1 = ((bf16[32,40,1536]{2,1,0:T(8,128)(2,1)}), bf16[32,40,1536]{2,1,0:T(8,128)(2,1)}, u32[]{:S(2)}, u32[]{:S(2)}) async-start(bf16[32,40,1536]{2,1,0:T(8,128)(2,1)} %bitcast.398), calls=%async_computation.1 | async-start | bytes 7864320 | tf_op jit(solution)/shard_map/all_to_all | solution.py:534
  322.0 11.0 %copy-start.76 = (s32[2]{0:T(128)S(1)}, s32[2]{0:T(128)}, u32[]{:S(2)}) copy-start(s32[2]{0:T(128)} %constant.117) | copy-start | bytes 28
  322.0 11.0 %copy-start.75 = (s32[2]{0:T(128)S(1)}, s32[2]{0:T(128)}, u32[]{:S(2)}) copy-start(s32[2]{0:T(128)} %constant.120) | copy-start | bytes 28
  322.0 12.0 %copy-start.19 = (bf16[128,8,3,64]{0,3,2,1:T(8,128)(2,1)S(1)}, bf16[128,8,3,64]{0,3,2,1:T(8,128)(2,1)}, u32[]{:S(2)}) copy-start(bf16[128,8,3,64]{0,3,2,1:T(8,128)(2,1)} %copy-done.18) | copy-start | bytes 1179652
  322.0 56.2 %all-to-all-start.3 = ((bf16[32,40,1536]{2,1,0:T(8,128)(2,1)}), bf16[32,40,1536]{2,1,0:T(8,128)(2,1)}, u32[]{:S(2)}, u32[]{:S(2)}) async-start(bf16[32,40,1536]{2,1,0:T(8,128)(2,1)} %bitcast.395), calls=%async_computation.3 | async-start | bytes 7864320 | tf_op jit(solution)/shard_map/all_to_all | solution.py:571
  332.7 148.3 %reduce-scatter.3.cloned.1.call-start = ((), (), s32[]{:S(2)}) async-start(), calls=%async_computation.8 | async-start | bytes 1179648 | tf_op jit(solution)/shard_map/reduce_scatter | solution.py:605
  388.1 10.2 %copy-start.8 = (f32[128,1536]{1,0:T(8,128)S(1)}, f32[128,1536]{1,0:T(8,128)}, u32[]{:S(2)}) copy-start(f32[128,1536]{1,0:T(8,128)} %copy-done.7) | copy-start | bytes 2359300
  388.1 10.2 %copy-start.46 = (bf16[1536,32]{0,1:T(8,128)(2,1)S(1)}, bf16[1536,32]{0,1:T(8,128)(2,1)}, u32[]{:S(2)}) copy-start(bf16[1536,32]{0,1:T(8,128)(2,1)} %param.27) | copy-start | bytes 294916
  388.1 10.2 %copy-start.58 = (f32[1536]{0:T(1024)S(1)}, f32[1536]{0:T(1024)}, u32[]{:S(2)}) copy-start(f32[1536]{0:T(1024)} %param.26) | copy-start | bytes 18436
  388.1 10.3 %copy-start.68 = (f32[128]{0:T(128)S(1)}, f32[128]{0:T(128)}, u32[]{:S(2)}) copy-start(f32[128]{0:T(128)} %copy-done.67) | copy-start | bytes 1540
  388.1 11.3 %copy-start.74 = (f32[128]{0:T(128)S(1)}, f32[128]{0:T(128)}, u32[]{:S(2)}) copy-start(f32[128]{0:T(128)} %copy-done.73) | copy-start | bytes 1540
  388.2 12.1 %copy-start.20 = (bf16[1,128,1536]{2,1,0:T(8,128)(2,1)S(1)}, bf16[1,128,1536]{2,1,0:T(8,128)(2,1)}, u32[]{:S(2)}) copy-start(bf16[1,128,1536]{2,1,0:T(8,128)(2,1)} %param.31) | copy-start | bytes 1179652
  444.3 7.0 %copy-start.32 = (bf16[16,2,40,512]{3,2,0,1:T(8,128)(2,1)S(1)}, bf16[16,2,40,512]{3,2,0,1:T(8,128)(2,1)}, u32[]{:S(2)}) copy-start(bf16[16,2,40,512]{3,2,0,1:T(8,128)(2,1)} %get-tuple-element.565) | copy-start | bytes 3932164
  444.4 76.9 %reduce-scatter.5.cloned.1.call-start = ((), (), s32[]{:S(2)}) async-start(), calls=%async_computation.9 | async-start | bytes 1179648 | tf_op jit(solution)/shard_map/reduce_scatter | solution.py:608
  451.4 7.2 %copy-start.30 = (bf16[16,2,40,512]{3,2,0,1:T(8,128)(2,1)S(1)}, bf16[16,2,40,512]{3,2,0,1:T(8,128)(2,1)}, u32[]{:S(2)}) copy-start(bf16[16,2,40,512]{3,2,0,1:T(8,128)(2,1)} %get-tuple-element.566) | copy-start | bytes 3932164
  458.6 7.0 %copy-start.23 = (bf16[128,1536]{1,0:T(8,128)(2,1)S(1)}, bf16[128,1536]{1,0:T(8,128)(2,1)}, u32[]{:S(2)}) copy-start(bf16[128,1536]{1,0:T(8,128)(2,1)} %copy-done.22) | copy-start | bytes 1179652
  458.6 7.2 %copy-start.16 = (bf16[128,1536]{1,0:T(8,128)(2,1)S(1)}, bf16[128,1536]{1,0:T(8,128)(2,1)}, u32[]{:S(2)}) copy-start(bf16[128,1536]{1,0:T(8,128)(2,1)} %copy-done.15) | copy-start | bytes 1179652
  458.6 7.2 %copy-start.52 = (f32[4096]{0:T(1024)S(1)}, f32[4096]{0:T(1024)}, u32[]{:S(2)}) copy-start(f32[4096]{0:T(1024)} %copy-done.51) | copy-start | bytes 49156
  458.6 8.3 %copy-start.62 = (bf16[1536]{0:T(1024)(128)(2,1)S(1)}, bf16[1536]{0:T(1024)(128)(2,1)}, u32[]{:S(2)}) copy-start(bf16[1536]{0:T(1024)(128)(2,1)} %get-tuple-element.493) | copy-start | bytes 9220
  458.6 9.5 %copy-start.41 = (f32[128,32]{0,1:T(8,128)S(1)}, f32[128,32]{0,1:T(8,128)}, u32[]{:S(2)}) copy-start(f32[128,32]{0,1:T(8,128)} %copy-done.39) | copy-start | bytes 49156
  458.6 9.5 %copy-start.53 = (f32[128,32]{0,1:T(8,128)S(1)}, f32[128,32]{0,1:T(8,128)}, u32[]{:S(2)}) copy-start(f32[128,32]{0,1:T(8,128)} %get-tuple-element.580) | copy-start | bytes 49156
  469.2 12.8 %copy-start.54 = (f32[128,32]{0,1:T(8,128)S(1)}, f32[128,32]{0,1:T(8,128)}, u32[]{:S(2)}) copy-start(f32[128,32]{0,1:T(8,128)} %get-tuple-element.580) | copy-start | bytes 49156
  469.2 54.1 %copy-start.14 = (bf16[1536,512]{1,0:T(8,128)(2,1)S(1)}, bf16[1536,512]{1,0:T(8,128)(2,1)}, u32[]{:S(2)}) copy-start(bf16[1536,512]{1,0:T(8,128)(2,1)} %param.22) | copy-start | bytes 4718596
  474.2 51.0 %copy-start.11 = (bf16[1,128,1536]{2,1,0:T(8,128)(2,1)S(1)}, bf16[1,128,1536]{2,1,0:T(8,128)(2,1)}, u32[]{:S(2)}) copy-start(bf16[1,128,1536]{2,1,0:T(8,128)(2,1)} %param.19) | copy-start | bytes 1179652
  482.1 41.2 %copy-start.33 = (bf16[128,8,64]{0,2,1:T(8,128)(2,1)}, bf16[128,8,64]{0,2,1:T(8,128)(2,1)S(1)}, u32[]{:S(2)}) copy-start(bf16[128,8,64]{0,2,1:T(8,128)(2,1)S(1)} %maximum_convert_fusion.1) | copy-start | bytes 393220
  523.3 5.8 copy-start.29
  523.3 5.8 copy-start.72
  530.2 139.9 %copy-start.9 = (f32[128,1536]{1,0:T(8,128)S(1)}, f32[128,1536]{1,0:T(8,128)}, u32[]{:S(2)}) copy-start(f32[128,1536]{1,0:T(8,128)} %copy-done.7) | copy-start | bytes 2359300
  530.2 139.9 %copy-start.13 = (f32[128,1536]{1,0:T(8,128)S(1)}, f32[128,1536]{1,0:T(8,128)}, u32[]{:S(2)}) copy-start(f32[128,1536]{1,0:T(8,128)} %copy-done.12) | copy-start | bytes 2359300
  530.2 139.9 %copy-start.21 = (bf16[1,128,1536]{2,1,0:T(8,128)(2,1)S(1)}, bf16[1,128,1536]{2,1,0:T(8,128)(2,1)}, u32[]{:S(2)}) copy-start(bf16[1,128,1536]{2,1,0:T(8,128)(2,1)} %param.31) | copy-start | bytes 1179652
  530.2 139.9 %copy-start.24 = (f32[128,1536]{1,0:T(8,128)S(1)}, f32[128,1536]{1,0:T(8,128)}, u32[]{:S(2)}) copy-start(f32[128,1536]{1,0:T(8,128)} %get-tuple-element.492) | copy-start | bytes 2359300
  530.2 139.9 %copy-start.50 = (f32[1536]{0:T(1024)S(1)}, f32[1536]{0:T(1024)}, u32[]{:S(2)}) copy-start(f32[1536]{0:T(1024)} %param.25) | copy-start | bytes 18436
  530.2 139.9 %copy-start.59 = (f32[1536]{0:T(1024)S(1)}, f32[1536]{0:T(1024)}, u32[]{:S(2)}) copy-start(f32[1536]{0:T(1024)} %param.26) | copy-start | bytes 18436
  667.1 7.0 %copy-start.60 = (f32[48,512]{1,0:T(8,128)S(1)}, f32[48,512]{1,0:T(8,128)}, u32[]{:S(2)}) copy-start(f32[48,512]{1,0:T(8,128)} %get-tuple-element.897) | copy-start | bytes 294916
  667.1 7.7 %copy-start.47 = (f32[48,1536]{1,0:T(8,128)S(1)}, f32[48,1536]{1,0:T(8,128)}, u32[]{:S(2)}) copy-start(f32[48,1536]{1,0:T(8,128)} %get-tuple-element.898) | copy-start | bytes 884740
  670.2 6.3 copy-start.35
  (47 other events, 136.9 us)
Sparse Core Ops, SparseCore 0:
  13.6 37.0 all-gather.2
  53.0 38.0 all-gather.4
  444.5 36.4 reduce-scatter.2
  483.2 37.9 reduce-scatter.4

commit v2 on v1

--- a/solution.py
+++ b/solution.py
@@ -74,6 +74,384 @@
         return carry
 
     lax.fori_loop(0, lead, body, 0)
+
+
+def group_peers(place):
+    return {
+        (c, h, d): place.at(core=c, hi=h, z=d)
+        for c in (0, 1) for h in (0, 1) for d in range(4) if (c, h, d) != (0, 0, 0)
+    }
+
+
+def group_index(place, core=0, hi=0, z=0):
+    return ((place.hi + hi) % 2 * 2 + (place.core + core) % 2) * 4 + (place.z + z) % 4
+
+
+class Spread:
+    def __init__(self, place, held, sems):
+        self.place, self.held, self.sems = place, held, sems
+        self.sent, self.waits = [], {}
+
+    def pair(self, c, h, d):
+        slot = c * 8 + h * 4 + d
+        return (self.sems.at[0, slot], self.sems.at[1, slot])
+
+    def push(self, origin, target, slot):
+        c, h, d = target
+        index = group_index(self.place, hi=origin[0], z=origin[1])
+        block = self.held.at[index]
+        copy = send(block, block, self.pair(*slot), self.place.at(core=c, hi=h, z=d))
+        self.sent.append(copy)
+        self.waits[slot] = copy
+
+    def land(self, slot):
+        self.waits[slot].wait_recv()
+
+    def first(self):
+        for d in (1, 3, 2):
+            self.push((0, 0), (0, 0, d), (0, 0, (4 - d) % 4))
+        self.push((0, 0), (0, 1, 0), (0, 1, 0))
+        self.push((0, 0), (1, 0, 0), (1, 0, 0))
+
+    def relay(self):
+        self.land((0, 1, 0))
+        for d in (1, 3):
+            self.push((1, 0), (0, 0, d), (0, 1, (4 - d) % 4))
+        self.push((1, 0), (1, 0, 0), (1, 1, 0))
+        self.land((0, 0, 2))
+        self.push((0, 2), (0, 1, 0), (0, 1, 2))
+        self.push((0, 2), (1, 0, 0), (1, 0, 2))
+        for d in (1, 3):
+            self.land((0, 0, d))
+            self.push((0, d), (1, 0, 0), (1, 0, d))
+
+    def finish_near(self):
+        for d in range(4):
+            self.land((1, 0, d))
+
+    def relay_far(self):
+        for d in (1, 3, 2):
+            self.land((0, 1, d))
+            self.push((1, d), (1, 0, 0), (1, 1, d))
+
+    def finish_far(self):
+        for d in range(4):
+            self.land((1, 1, d))
+
+    def drain(self):
+        for copy in self.sent:
+            copy.wait_send()
+
+
+def add_rows(out, terms):
+    def body(i, carry):
+        part = pl.ds(pl.multiple_of(i * 16, 16), 16)
+        total = terms[0][part].astype(F32)
+        for term in terms[1:]:
+            total = total + term[part].astype(F32)
+        out[part] = total.astype(out.dtype)
+        return carry
+
+    lax.fori_loop(0, 8, body, 0)
+
+
+class Gather:
+    def __init__(self, place, parts, pool, landing, sems, own=None):
+        self.place, self.parts, self.pool, self.landing, self.sems = place, parts, pool, landing, sems
+        self.own = own
+        self.sent = []
+
+    def pair(self, slot):
+        return (self.sems.at[0, slot], self.sems.at[1, slot])
+
+    def push(self, src, dst, slot, device):
+        copy = send(src, dst, self.pair(slot), device)
+        self.sent.append(copy)
+        return copy
+
+    def swap(self, hi):
+        half = (self.place.hi + hi) % 2
+        start = group_index(self.place, core=1, hi=hi) - self.place.z
+        return self.push(
+            self.parts.at[pl.ds(start, 4)], self.pool.at[pl.ds(half * 4, 4)], hi, self.place.at(core=1)
+        )
+
+    def chunk(self, hi, z):
+        return self.pool.at[(self.place.hi + hi) % 2 * 4 + (self.place.z + z) % 4]
+
+    def mine(self, hi, z):
+        if self.own is not None:
+            return self.own.at[(self.place.hi + hi) % 2 * 4 + (self.place.z + z) % 4]
+        return self.parts.at[group_index(self.place, hi=hi, z=z)]
+
+    def join(self, hi, z, more=()):
+        block = self.chunk(hi, z)
+        add_rows(block, [block, self.mine(hi, z), *more])
+        return block
+
+    def first(self):
+        place, land = self.place, self.landing
+        self.cross, self.direct = [], []
+        for i, d in enumerate((1, 3)):
+            self.cross.append(self.push(self.join(1, d), land.at[i], 2 + i, place.at(z=d)))
+        self.far = self.push(self.join(1, 2), land.at[2], 4, place.at(hi=1))
+        for i, d in enumerate((1, 3)):
+            self.direct.append(self.push(self.join(0, d), land.at[3 + i], 5 + i, place.at(z=d)))
+
+    def second(self):
+        place, land = self.place, self.landing
+        for copy in self.cross:
+            copy.wait_recv()
+        block = self.join(1, 0, [land.at[0], land.at[1]])
+        self.last = [self.push(block, land.at[5], 7, place.at(hi=1))]
+        self.far.wait_recv()
+        block = self.join(0, 2, [land.at[2]])
+        self.last.append(self.push(block, land.at[6], 8, place.at(z=2)))
+
+    def finish(self, out):
+        for copy in self.direct + self.last:
+            copy.wait_recv()
+        land = self.landing
+        add_rows(out, [self.chunk(0, 0), self.mine(0, 0), land.at[3], land.at[4], land.at[5], land.at[6]])
+
+    def drain(self):
+        for copy in self.sent:
+            copy.wait_send()
+
+
+def contract(left, right, dims):
+    return lax.dot_general(left, right, (dims, ((), ())), preferred_element_type=F32)
+
+
+def expert_kernel(
+    n2, cot, table, wg, wu, wd,
+    dn2, dgate, eo, eg, eu, ed,
+    rows, cots, tables, table_sems, rows_sems, cots_sems,
+    x_rows, c_rows, pick, gate, dhg, dhu, gact, dg, drow,
+    pool, landing, gather_sems, dgate_out, dgate_sems, stage, stage_sems,
+):
+    place = Place()
+    peers = group_peers(place)
+    greet(list(peers.values()))
+    me = group_index(place)
+
+    small = []
+    tables[me] = table[me]
+    for (c, h, d), device in peers.items():
+        slot = c * 8 + h * 4 + d
+        pair = (table_sems.at[0, slot], table_sems.at[1, c * 8 + h * 4 + (4 - d) % 4])
+        small.append(send(table.at[group_index(place, c, h, d)], tables.at[me], pair, device))
+    rows[me] = n2[...]
+    cots[me] = cot[...]
+    spread_rows = Spread(place, rows, rows_sems)
+    spread_cots = Spread(place, cots, cots_sems)
+    spread_rows.first()
+    spread_cots.first()
+    spread_rows.relay()
+    spread_cots.relay()
+    for copy in small:
+        copy.wait_recv()
+
+    slots = lax.broadcasted_iota(jnp.int32, (80, 256), 0).astype(F32)
+    second = lax.broadcasted_iota(jnp.int32, (1, 256), 1) >= 128
+
+    def select(pair_index):
+        parts = []
+        for e in range(2):
+            here = jnp.concatenate(
+                [tables[pair_index * 2, e : e + 1, :], tables[pair_index * 2 + 1, e : e + 1, :]], axis=1
+            )
+            here = jnp.where(here < 0.0, -1000.0, here + jnp.where(second, 40.0, 0.0))
+            weight = jnp.concatenate(
+                [tables[pair_index * 2, 2 + e : 3 + e, :], tables[pair_index * 2 + 1, 2 + e : 3 + e, :]],
+                axis=1,
+            )
+            hit = slots == here
+            parts.append(jnp.where(hit, 1.0, 0.0).astype(BF))
+            place_rows = pl.ds(pl.multiple_of(pair_index * 80, 80), 80)
+            gate[e, place_rows, :] = jnp.sum(jnp.where(hit, weight, 0.0), axis=1, keepdims=True)
+        pick[pair_index] = jnp.concatenate(parts, axis=0)
+
+    def pull(pair_index, held, out):
+        both = jnp.concatenate([held[pair_index * 2], held[pair_index * 2 + 1]], axis=0)
+        picked = contract(pick[pair_index], both, ((1,), (0,))).astype(BF)
+        place_rows = pl.ds(pl.multiple_of(pair_index * 80, 80), 80)
+        out[0, place_rows, :] = picked[0:80]
+        out[1, place_rows, :] = picked[80:160]
+
+    def all_pairs(body):
+        def step(i, carry):
+            body(i)
+            return carry
+        lax.fori_loop(0, 8, step, 0)
+
+    all_pairs(select)
+
+    def pull_side(c, h, held, out):
+        start = group_index(place, core=c, hi=h) - place.z
+        base = start // 2
+
+        def step(i, carry):
+            pull(base + i, held, out)
+            return carry
+
+        lax.fori_loop(0, 2, step, 0)
+
+    spread_rows.finish_near()
+    pull_side(0, 0, rows, x_rows)
+    pull_side(1, 0, rows, x_rows)
+    spread_rows.relay_far()
+    pull_side(0, 1, rows, x_rows)
+    spread_rows.finish_far()
+    pull_side(1, 1, rows, x_rows)
+    spread_cots.finish_near()
+    pull_side(0, 0, cots, c_rows)
+    pull_side(1, 0, cots, c_rows)
+    spread_cots.relay_far()
+    pull_side(0, 1, cots, c_rows)
+    spread_cots.finish_far()
+    pull_side(1, 1, cots, c_rows)
+
+    def work(i, carry):
+        e, m = i // 2, i % 2
+        part = pl.ds(pl.multiple_of(m * 320, 320), 320)
+        x = x_rows[e, part, :]
+        hg = contract(x, wg[e], ((1,), (0,)))
+        hu = contract(x, wu[e], ((1,), (0,)))
+        back = contract(c_rows[e, part, :], wd[e], ((1,), (1,)))
+        weight = gate[e, part, :]
+        sig = 1.0 / (1.0 + jnp.exp(-hg))
+        silu = hg * sig
+        act = silu * hu
+        dg[e, part, :] = jnp.sum(act * back, axis=1, keepdims=True)
+        gact[e, part, :] = (weight * act).astype(BF)
+        dact = weight * back
+        low_hg = (dact * hu * (sig + silu * (1.0 - sig))).astype(BF)
+        low_hu = (dact * silu).astype(BF)
+        dhg[e, part, :] = low_hg
+        dhu[e, part, :] = low_hu
+        back_rows = (
+            contract(low_hg, wg[e], ((1,), (1,))) + contract(low_hu, wu[e], ((1,), (1,)))
+        ).astype(BF)
+        for j in range(4):
+            drow[m * 4 + j, pl.ds(pl.multiple_of(e * 80, 80), 80), :] = back_rows[j * 80 : (j + 1) * 80]
+        return carry
+
+    lax.fori_loop(0, 4, work, 0)
+    spread_rows.drain()
+    spread_cots.drain()
+
+    def put_back(pair_index, out):
+        both = contract(pick[pair_index], drow[pair_index], ((0,), (0,))).astype(BF)
+        out[pair_index * 2] = both[0:128]
+        out[pair_index * 2 + 1] = both[128:256]
+
+    def put_side(c, h, out):
+        base = (group_index(place, core=c, hi=h) - place.z) // 2
+
+        def step(i, carry):
+            put_back(base + i, out)
+            return carry
+
+        lax.fori_loop(0, 2, step, 0)
+
+    home = Gather(place, rows, pool, landing, gather_sems)
+    put_side(1, 1, rows)
+    swaps = [home.swap(1)]
+    put_side(1, 0, rows)
+    swaps.append(home.swap(0))
+
+    def gate_grads(pair_index):
+        chosen = pick[pair_index].astype(F32)
+        for e in range(2):
+            column = dg[e, pl.ds(pl.multiple_of(pair_index * 80, 80), 80), :]
+            line = jnp.sum(chosen[e * 80 : (e + 1) * 80] * column, axis=0, keepdims=True)
+            dgate_out[pair_index * 2, e : e + 1, :] = line[:, 0:128]
+            dgate_out[pair_index * 2 + 1, e : e + 1, :] = line[:, 128:256]
+
+    dgate_out[...] = jnp.zeros_like(dgate_out)
+    all_pairs(gate_grads)
+    small_back = []
+    dgate[me] = dgate_out[me]
+    for (c, h, d), device in peers.items():
+        slot = c * 8 + h * 4 + d
+        pair = (dgate_sems.at[0, slot], dgate_sems.at[1, c * 8 + h * 4 + (4 - d) % 4])
+        small_back.append(send(dgate_out.at[group_index(place, c, h, d)], dgate.at[me], pair, device))
+    put_side(0, 1, rows)
+    swaps[0].wait_recv()
+    put_side(0, 0, rows)
+    swaps[1].wait_recv()
+    home.first()
+
+    def outputs(i, carry):
+        e, m = i // 2, i % 2
+        part = pl.ds(pl.multiple_of(m * 320, 320), 320)
+        made = contract(gact[e, part, :], wd[e], ((1,), (0,))).astype(BF)
+        for j in range(4):
+            drow[m * 4 + j, pl.ds(pl.multiple_of(e * 80, 80), 80), :] = made[j * 80 : (j + 1) * 80]
+        return carry
+
+    lax.fori_loop(0, 4, outputs, 0)
+    all_pairs(lambda p: put_back(p, cots))
+    eo_copy = pltpu.make_async_copy(cots, eo, stage_sems.at[2])
+    eo_copy.start()
+    home.second()
+    copies = {}
+    step = 0
+    for e in range(2):
+        for left, right, out in ((x_rows, dhg, eg), (x_rows, dhu, eu), (c_rows, gact, ed)):
+            slot = step % 2
+            if step >= 2:
+                copies[step - 2].wait()
+
+            def weight_grad(i, carry):
+                tile = pl.ds(pl.multiple_of(i * 256, 256), 256)
+                stage[slot, tile, :] = contract(left[e, :, tile], right[e], ((0,), (0,))).astype(BF)
+                return carry
+
+            lax.fori_loop(0, 6, weight_grad, 0)
+            copies[step] = pltpu.make_async_copy(stage.at[slot], out.at[e], stage_sems.at[slot])
+            copies[step].start()
+            step += 1
+    home.finish(dn2)
+    for copy in small_back:
+        copy.wait_recv()
+    for copy in small + small_back:
+        copy.wait_send()
+    home.drain()
+    copies[4].wait()
+    copies[5].wait()
+    eo_copy.wait()
+
+
+def run_experts(n2, cot, table, wg, wu, wd):
+    vmem = pl.BlockSpec(memory_space=pltpu.VMEM)
+    hbm = pl.BlockSpec(memory_space=pl.ANY)
+    sems = pltpu.SemaphoreType.DMA
+    low = lambda *shape: pltpu.VMEM(shape, BF)
+    struct = jax.ShapeDtypeStruct
+    return pl.pallas_call(
+        expert_kernel,
+        out_shape=(
+            struct((128, 1536), F32), struct((16, 8, 128), F32), struct((16, 128, 1536), BF),
+            struct((2, 1536, 512), BF), struct((2, 1536, 512), BF), struct((2, 1536, 512), BF),
+        ),
+        in_specs=[vmem] * 6,
+        out_specs=[vmem, vmem, hbm, hbm, hbm, hbm],
+        scratch_shapes=[
+            low(16, 128, 1536), low(16, 128, 1536), pltpu.VMEM((16, 8, 128), F32),
+            sems((2, 16)), sems((2, 16)), sems((2, 16)),
+            low(2, 640, 1536), low(2, 640, 1536), low(8, 160, 256), pltpu.VMEM((2, 640, 1), F32),
+            low(2, 640, 512), low(2, 640, 512), low(2, 640, 512), pltpu.VMEM((2, 640, 1), F32),
+            low(8, 160, 1536),
+            low(8, 128, 1536), low(7, 128, 1536), sems((2, 9)),
+            pltpu.VMEM((16, 8, 128), F32), sems((2, 16)),
+            low(2, 1536, 512), sems((3,)),
+        ],
+        compiler_params=pltpu.CompilerParams(
+            collective_id=1, has_side_effects=True, vmem_limit_bytes=62 << 20
+        ),
+    )(n2, cot, table, wg, wu, wd)
 
 
 WIDE = 384
@@ -99,13 +477,14 @@
 
 
 def reduce_kernel(
-    n1, attn, dq, dkv, dbr, narrow, eg, eu, ed,
-    gq, gk, gv, go, gs, og, ou, od,
+    n1, attn, dq, dkv, dbr, narrow, eo, eg, eu, ed,
+    moe, gq, gk, gv, go, gs, og, ou, od,
     n1c, attnc, dqc, dkvc, dbrc, pair_sems,
     send_o, send_q, send_s, land1_o, land1_q, land1_s, mid_o, mid_q, mid_s,
     land2_o, land2_q, land2_s, last_o, last_q, last_s, land3_o, land3_q, land3_s, dense_sems,
     mine, quarters, quarter_sems,
     own_p, own_q, land_p1, land_q1, sum_p, sum_q, land_p2, land_q2, expert_sems, local_sems,
+    eo_own, eo_pool, eo_landing, eo_sems, eo_local,
 ):
     place = Place()
     y_line, z_line, x_line = (place.line(axis) for axis in "yzx")
@@ -143,6 +522,19 @@
     for copy in local:
         copy.start()
 
+    home = Gather(place, eo, eo_pool, eo_landing, eo_sems, eo_own)
+    swaps = [home.swap(1), home.swap(0)]
+    own_rows = []
+    for h in range(2):
+        start = group_index(place, hi=h) - place.z
+        half = (place.hi + h) % 2
+        own_rows.append(
+            pltpu.make_async_copy(
+                eo.at[pl.ds(start, 4)], eo_own.at[pl.ds(half * 4, 4)], eo_local.at[h]
+            )
+        )
+        own_rows[-1].start()
+
     sends = {"o": send_o, "q": send_q, "s": send_s}
     lands = {
         "o": (land1_o, land2_o, land3_o), "q": (land1_q, land2_q, land3_q),
@@ -202,7 +594,14 @@
             send_s[(*index, slice(None), slice(256, 384))] = narrow[block * 48 : (block + 1) * 48, :]
     launch("s", 0)
     pending.extend(pairs)
+    for copy in swaps:
+        copy.wait_recv()
+    for copy in own_rows:
+        copy.wait()
+    home.first()
     for phase in range(3):
+        if phase == 1:
+            home.second()
         for name in "oqs":
             land(name, phase)
             if phase < 2:
@@ -244,6 +643,8 @@
         pair = (expert_sems.at[0, 13 + d], expert_sems.at[1, 13 + d])
         second.append(send(sum_q.at[index], land_q2.at[d], pair, device))
 
+    home.finish(moe)
+    home.drain()
     for copy in gathered:
         copy.wait_recv()
     pending.extend(gathered)
@@ -272,7 +673,7 @@
         copy.wait_send()
 
 
-def reduce_gradients(n1, attn, dq, dkv, dbr, narrow, eg, eu, ed):
+def reduce_gradients(n1, attn, dq, dkv, dbr, narrow, eo, eg, eu, ed):
     vmem = pl.BlockSpec(memory_space=pltpu.VMEM)
     sems = pltpu.SemaphoreType.DMA
     f32 = lambda *shape: jax.ShapeDtypeStruct(shape, F32)
@@ -281,11 +682,11 @@
     return pl.pallas_call(
         reduce_kernel,
         out_shape=(
-            f32(48, 1536), f32(48, 512), f32(48, 512), f32(48, 1536), f32(48, 128),
+            f32(128, 1536), f32(48, 1536), f32(48, 512), f32(48, 512), f32(48, 1536), f32(48, 128),
             f32(2, 192, 512), f32(2, 192, 512), f32(2, 192, 512),
         ),
-        in_specs=[vmem] * 6 + [pl.BlockSpec(memory_space=pl.ANY)] * 3,
-        out_specs=[vmem] * 8,
+        in_specs=[vmem] * 6 + [pl.BlockSpec(memory_space=pl.ANY)] * 4,
+        out_specs=[vmem] * 9,
         scratch_shapes=[
             low(256, 1536), low(256, 1536), low(256, 768), low(256, 512), low(256, 768),
             sems((2, 5)),
@@ -302,11 +703,12 @@
             low(2, 3, 192, 512), low(4, 3, 192, 512),
             low(3, 192, 512), low(3, 3, 192, 512),
             sems((2, 16)), sems((2, 3)),
+            low(8, 128, 1536), low(8, 128, 1536), low(7, 128, 1536), sems((2, 9)), sems((2,)),
         ],
         compiler_params=pltpu.CompilerParams(
             collective_id=0, has_side_effects=True, vmem_limit_bytes=60 << 20
         ),
-    )(n1, attn, dq, dkv, dbr, narrow, eg, eu, ed)
+    )(n1, attn, dq, dkv, dbr, narrow, eo, eg, eu, ed)
 
 
 HEADS = 24
@@ -496,81 +898,30 @@
     n_second = normalize(y_mid, gain_moe).astype(jnp.bfloat16)
     logits = jnp.dot(n_second, w_router, preferred_element_type=jnp.float32)
 
-    def gate_values(logit_rows):
-        return jax.nn.softmax(jnp.take_along_axis(logit_rows, route_ids, axis=1), axis=-1)
-
-    gates, gate_pull = jax.vjp(gate_values, logits)
-    match = route_ids[:, :, None] == lax.iota(jnp.int32, expert_count)[None, None, :]
-    counts = jnp.sum(match.astype(jnp.int32), axis=1)
-    before = jnp.cumsum(counts, axis=0) - counts
-    slot = jnp.sum(jnp.where(match, before[:, None, :], 0), axis=2)
-    target = (route_ids * capacity + slot).reshape(-1)
-
-    def dispatch_rows(route_rows):
-        filled = (
-            jnp.zeros((expert_count * capacity, model_width), jnp.bfloat16)
-            .at[target]
-            .set(route_rows)
-        )
-        return filled.reshape(expert_count, capacity, model_width)
-
-    def collect_rows(returned_rows):
-        return returned_rows.reshape(expert_count * capacity, model_width)[target].reshape(
-            row_count, route_count, model_width
-        )
-
-    spread = jnp.broadcast_to(n_second[:, None, :], (row_count, route_count, model_width)).reshape(
-        -1, model_width
-    )
-    received_rows = lax.all_to_all(
-        dispatch_rows(spread), ("expert", "dp"), split_axis=0, concat_axis=0, tiled=True
-    )
-    grouped = received_rows.reshape(sources, local_experts, -1, model_width)
-    hidden_gate = jnp.einsum("sxcd,xdf->sxcf", grouped, w_gate, preferred_element_type=jnp.float32)
-    hidden_up = jnp.einsum("sxcd,xdf->sxcf", grouped, w_up, preferred_element_type=jnp.float32)
-    active = (jax.nn.silu(hidden_gate) * hidden_up).astype(jnp.bfloat16)
-    produced = jnp.einsum("sxcf,xfd->sxcd", active, w_down, preferred_element_type=jnp.float32)
-    produced = produced.astype(jnp.bfloat16).reshape(received_rows.shape)
-    returned = lax.all_to_all(produced, ("expert", "dp"), split_axis=0, concat_axis=0, tiled=True)
-    picked = collect_rows(returned).astype(jnp.float32)
-    y_out = y_mid + jnp.sum(gates[:, :, None] * picked, axis=1)
+    chosen = jnp.sum(
+        (route_ids[:, :, None] == lax.iota(jnp.int32, expert_count)[None, None, :]).astype(
+            jnp.float32
+        ),
+        axis=1,
+    )
+    gates = jax.nn.softmax(jnp.where(chosen > 0.0, logits, -jnp.inf), axis=-1)
+    before = jnp.cumsum(chosen, axis=0) - chosen
+    table = jnp.concatenate(
+        [
+            jnp.where(chosen > 0.0, before, -1.0).T.reshape(16, 2, row_count),
+            gates.T.reshape(16, 2, row_count),
+            jnp.zeros((16, 4, row_count), jnp.float32),
+        ],
+        axis=1,
+    )
     grad_out = cotangent[0].astype(jnp.float32)
-    grad_gate_values = jnp.sum(grad_out[:, None, :] * picked, axis=2)
-    weighted = (
-        (gates[:, :, None] * grad_out[:, None, :]).astype(jnp.bfloat16).reshape(-1, model_width)
-    )
-    grad_back = lax.all_to_all(
-        dispatch_rows(weighted), ("expert", "dp"), split_axis=0, concat_axis=0, tiled=True
-    )
-    grouped = received_rows.reshape(sources, local_experts, -1, model_width)
-    grad_grouped = grad_back.reshape(sources, local_experts, -1, model_width)
-    hidden_gate = jnp.einsum("sxcd,xdf->sxcf", grouped, w_gate, preferred_element_type=jnp.float32)
-    hidden_up = jnp.einsum("sxcd,xdf->sxcf", grouped, w_up, preferred_element_type=jnp.float32)
-
-    def activate(gate_part, up_part):
-        return jax.nn.silu(gate_part) * up_part
-
-    active_full, act_pull = jax.vjp(activate, hidden_gate, hidden_up)
-    active = active_full.astype(jnp.bfloat16)
-    grad_w_down = jnp.einsum(
-        "sxcd,sxcf->xdf", grad_grouped, active, preferred_element_type=jnp.float32
-    )
-    grad_active = jnp.einsum(
-        "sxcd,xfd->sxcf", grad_grouped, w_down, preferred_element_type=jnp.float32
-    )
-    grad_hg, grad_hu = act_pull(grad_active)
-    grad_hg = grad_hg.astype(jnp.bfloat16)
-    grad_hu = grad_hu.astype(jnp.bfloat16)
-    grad_w_gate = jnp.einsum("sxcd,sxcf->xdf", grouped, grad_hg, preferred_element_type=jnp.float32)
-    grad_w_up = jnp.einsum("sxcd,sxcf->xdf", grouped, grad_hu, preferred_element_type=jnp.float32)
-    grad_rows = jnp.einsum("sxcf,xdf->sxcd", grad_hg, w_gate, preferred_element_type=jnp.float32)
-    grad_rows = grad_rows + jnp.einsum(
-        "sxcf,xdf->sxcd", grad_hu, w_up, preferred_element_type=jnp.float32
-    )
-    grad_rows = grad_rows.astype(jnp.bfloat16).reshape(expert_count, capacity, model_width)
-    grad_home = lax.all_to_all(grad_rows, ("expert", "dp"), split_axis=0, concat_axis=0, tiled=True)
-    grad_n_second = jnp.sum(collect_rows(grad_home).astype(jnp.float32), axis=1)
-    grad_logits = gate_pull(grad_gate_values)[0].astype(jnp.bfloat16)
+    grad_n_second, grad_gates, produced, grad_w_gate, grad_w_up, grad_w_down = run_experts(
+        n_second, cotangent[0], table, w_gate, w_up, w_down
+    )
+    grad_gates = grad_gates[:, :2].reshape(expert_count, row_count).T
+    grad_logits = (
+        gates * (grad_gates - jnp.sum(gates * grad_gates, axis=-1, keepdims=True))
+    ).astype(jnp.bfloat16)
     grad_w_router = jnp.einsum(
         "td,te->de", n_second, grad_logits, preferred_element_type=jnp.float32
     )
@@ -636,24 +987,25 @@
     narrow = jnp.concatenate(
         [grad_w_router, grad_gain_attn[:, None], grad_gain_moe[:, None],
          jnp.zeros((model_width, 94), jnp.float32)], axis=1).astype(jnp.bfloat16)
-    blocks = lambda grads: grads.astype(jnp.bfloat16).reshape(local_experts, 2, 4, 192, -1)
+    blocks = lambda grads: grads.reshape(local_experts, 2, 4, 192, -1)
     sums = reduce_gradients(
-        n_first, attn_low, halves(grad_q_raw), grad_kv, halves(grad_branch), narrow,
+        n_first, attn_low, halves(grad_q_raw), grad_kv, halves(grad_branch), narrow, produced,
         blocks(grad_w_gate), blocks(grad_w_up), blocks(grad_w_down),
     )
+    y_out = y_mid + sums[0]
     return (
         y_out.astype(jnp.bfloat16)[None],
         grad_input[None],
-        sums[0],
         sums[1],
         sums[2],
         sums[3],
-        sums[4][:, 32],
-        sums[4][:, 33],
-        sums[4][:, :32],
-        sums[5],
+        sums[4],
+        sums[5][:, 32],
+        sums[5][:, 33],
+        sums[5][:, :32],
         sums[6],
-        sums[7].transpose(0, 2, 1),
+        sums[7],
+        sums[8].transpose(0, 2, 1),
     )
 
 

time: 698 us -> 534 us (0.77); the launches traced: 685 us -> 531 us
  Pallas kernels: 137 us -> 260 us
  waiting for transfers between devices: 209 us -> 87.7 us
  local copies, waits for them, and re-layouts: 114 us -> 59 us
  starting transfers between devices: 45 us -> 0.38 us
  matrix products: 110 us -> 76.1 us
  other arithmetic: 54.6 us -> 34 us
    all_to_all x4 -> x0, waiting for transfers between devices: 123 us -> none  [the longest x1 37.2 us: shards(): lax.all_to_all(produced, ('expert', 'dp'), split_axis=0, concat_axis=0, t...]
    pallas_call x1 -> x2, Pallas kernels: 137 us -> 260 us  [the longest x1 141 us: reduce_gradients(): pl.pallas_call(reduce_kernel, out_shape=(f32(128, 1536), f32(48, 1536), f...]
    dot_general x9 -> x0, matrix products: 50.5 us -> none  [the longest x1 8.43 us: shards(): jnp.einsum('sxcd,xfd->sxcf', grad_grouped, w_down, preferred_element_type...]
    all_to_all x4 -> x0, starting transfers between devices: 44.7 us -> none  [the longest x1 12.2 us: shards(): lax.all_to_all(dispatch_rows(spread), ('expert', 'dp'), split_axis=0, con...]
    gather x7 -> x0, local copies, waits for them, and re-layouts: 26.5 us -> none  [the longest x2 19.2 us: collect_rows(): returned_rows.reshape(expert_count * capacity, model_width)[target]]
    all_gather x1, waiting for transfers between devices: 38 us -> 22.2 us  [shards(): lax.all_gather(key_rows, 'context', axis=0, tiled=True)]
    reduce_sum x6 -> x3, other arithmetic: 11.5 us -> 0.08 us  [the longest x1 0.03 us: shards(): jnp.sum(gates * grad_gates, axis=-1, keepdims=True)]
    reduce_scatter x1, waiting for transfers between devices: 6.77 us -> 17.5 us  [shards(): lax.psum_scatter(grad_key_all.astype(jnp.bfloat16), 'context', scatter_di...]
  transfers between devices with their start and end apart: 8 -> 4, of which waited for: 8 -> 4; matrix products, arithmetic and copies ran while one was open for 19% -> 11% of each run, Pallas kernels for 0% -> 0%
where the time goes in v2:
time: 534 us; the launch traced here: 531 us
  Pallas kernels  260 us (49%)
  waiting for transfers between devices  87.7 us (16%)
  matrix products  76.1 us (14%)
  local copies, waits for them, and re-layouts  59 us (11%)
  other arithmetic  34 us (6%)
  between operations  14.4 us (3%)
    pallas_call x1, Pallas kernels, reduce_gradients(): pl.pallas_call(reduce_kernel, out_shape=(f32(128, 1536), f32(48, 1536), f...  141 us
    pallas_call x1, Pallas kernels, run_experts(): pl.pallas_call(expert_kernel, out_shape=(struct((128, 1536), F32), struct...  119 us
    reduce_scatter x1, waiting for transfers between devices, shards(): lax.psum_scatter(grad_value_all.astype(jnp.bfloat16), 'context', scatter_...  35.5 us
    unnamed x104, local copies, waits for them, and re-layouts  24 us
    all_gather x1, waiting for transfers between devices, shards(): lax.all_gather(key_rows, 'context', axis=0, tiled=True)  22.2 us
    reduce_scatter x1, waiting for transfers between devices, shards(): lax.psum_scatter(grad_key_all.astype(jnp.bfloat16), 'context', scatter_di...  17.5 us
    dynamic_slice x14, local copies, waits for them, and re-layouts, attention_forward(): lax.scan(gather_stats, start_stats, (key_blocks, starts))  17.1 us
    dot_general x4, matrix products, block_scores(): jnp.einsum('qkgd,skd->kgqs', query, key_heads, preferred_element_type=jnp...  14.7 us
  transfers between devices with their start and end apart: 4, of which 4 were waited for; matrix products, arithmetic and copies ran while one was open for 11% of the time, Pallas kernels for 0%

profile of v2, /device:TPU:1, one launch (start us, length us, event | category | flops | bytes accessed | tf_op | source)
XLA Modules:
  0.0 531.3 jit_solution(17641427885585913235)
XLA Ops:
  7.3 1.3 fusion.42
  9.1 1.7 copy.103
  11.6 1.6 fusion.54
  16.9 6.6 %copy.105 = bf16[1536,1536]{0,1:T(8,128)(2,1)} copy(bf16[1536,1536]{1,0:T(8,128)(2,1)} %param.21) | data formatting | bytes 9437184 | tf_op args[2]
  23.5 3.8 fusion.52
  29.3 22.2 %all-gather.5.cloned.1.call-done = bf16[1024,512]{1,0:T(8,128)(2,1)} async-done(((bf16[128,512]{1,0:T(8,128)(2,1)}), bf16[1024,512]{1,0:T(8,128)(2,1)}) %all-gather.5.cloned.1.call-update) | async-done | bytes 1048592 | tf_op jit(solution)/shard_map/all_gather | solution.py:890
  51.5 2.3 copy.108
  53.8 25.8 %while.39 = (s32[]{:T(128)}, f32[8,3,128]{2,1,0:T(4,128)S(1)}, f32[8,3,128]{2,1,0:T(4,128)}, s32[2]{0:T(128)}, bf16[2,512,512]{1,2,0:T(8,128)(2,1)}, /*index=5*/...) while((s32[]{:T(128)}, f32[8,3,128]{2,1,0:T(4,128)S(1)}, f32[8,3,128]{2,1,0:T(4,128)}, ...), condition=%wide.region_4.5_spmd.clone, body=%wide.region_1.4_spmd.clone.sunk | while | flops 212418176 | bytes 14910600 | solution.py:779
  56.9 4.7 fusion.124
  61.6 4.1 exponential_reduce_fusion.2
  69.5 4.7 fusion.124
  74.2 4.1 exponential_reduce_fusion.2
  78.3 1.3 fusion.125
  79.6 12.1 %all-gather.3.cloned.1.call-done = bf16[1024,512]{1,0:T(8,128)(2,1)} async-done(((bf16[128,512]{1,0:T(8,128)(2,1)}), bf16[1024,512]{1,0:T(8,128)(2,1)}) %all-gather.3.cloned.1.call-update) | async-done | bytes 1048592 | tf_op jit(solution)/shard_map/all_gather | solution.py:891
  91.7 2.3 copy.107
  94.0 14.8 %while.40 = (s32[]{:T(128)}, f32[128,8,3,64]{0,3,2,1:T(8,128)}, bf16[2,512,512]{1,2,0:T(8,128)(2,1)}, s32[2]{0:T(128)}, bf16[2,512,512]{1,2,0:T(8,128)(2,1)}, /*...) while((s32[]{:T(128)}, f32[128,8,3,64]{0,3,2,1:T(8,128)}, ...), condition=%wide.region_6.7_spmd.clone, body=%wide.region_5.6_spmd.clone.sunk | while | flops 410976896 | bytes 5272727 | solution.py:792
  94.0 1.3 constant_dynamic-slice_fusion.10
  97.3 4.0 fusion.130
  104.6 4.2 fusion.130
  110.0 3.4 multiply_reduce_fusion.2
  115.5 118.5 %shard_map.220 = (f32[128,1536]{1,0:T(8,128)}, f32[16,8,128]{2,1,0:T(8,128)}, bf16[16,128,1536]{2,1,0:T(8,128)(2,1)}, bf16[2,1536,512]{2,1,0:T(8,128)(2,1)}, bf1...) custom-call(bf16[128,1536]{1,0:T(8,128)(2,1)} %copy-done.8, bf16[128,1536]{1,0:T(8,128)(2,1)} %bitcast.288, ...), custom_call_target="tpu_custom_call" | custom-call | tf_op jit(solution)/shard_map/pallas_call | solution.py:433
  235.7 2.5 multiply_reduce_fusion
  239.4 1.5 fusion.61
  241.7 4.0 convolution_convert_fusion
  246.6 45.3 %while.41 = (s32[]{:T(128)}, f32[128,8,3,64]{0,3,2,1:T(8,128)}, bf16[2,512,512]{2,1,0:T(8,128)(2,1)}, bf16[2,512,512]{2,1,0:T(8,128)(2,1)}, bf16[2,512,512]{1,2,...) while((s32[]{:T(128)}, f32[128,8,3,64]{0,3,2,1:T(8,128)}, ...), condition=%wide.region_15.16_spmd.clone, body=%wide.region_14.15_spmd.clone.sunk | while | flops 1020396160 | bytes 65709272 | solution.py:832
  249.7 2.6 fusion.141
  252.4 1.5 constant_dynamic-slice_fusion.12
  253.9 3.5 fusion.142
  257.3 3.4 fusion.143
  260.7 3.9 fusion.144
  264.9 3.1 fusion.145
  272.3 2.6 fusion.141
  274.9 1.5 constant_dynamic-slice_fusion.12
  276.4 3.5 fusion.142
  279.9 3.6 fusion.143
  283.5 3.9 fusion.144
  287.6 3.0 fusion.145
  293.1 1.9 copy.125.attn
  301.6 4.1 fusion.63
  305.7 17.5 %reduce-scatter.3.cloned.1.call-done = bf16[128,512]{1,0:T(8,128)(2,1)} async-done(((bf16[1024,512]{1,0:T(8,128)(2,1)}), bf16[128,512]{1,0:T(8,128)(2,1)}) %reduce-scatter.3.cloned.1.call-update) | async-done | bytes 131088 | tf_op jit(solution)/shard_map/reduce_scatter | solution.py:956
  325.7 2.1 convolution_add_fusion.1
  327.7 35.5 %reduce-scatter.5.cloned.1.call-done = bf16[128,512]{1,0:T(8,128)(2,1)} async-done(((bf16[1024,512]{1,0:T(8,128)(2,1)}), bf16[128,512]{1,0:T(8,128)(2,1)}) %reduce-scatter.5.cloned.1.call-update) | async-done | bytes 131088 | tf_op jit(solution)/shard_map/reduce_scatter | solution.py:959
  363.3 2.5 fusion.43
  370.1 2.3 maximum_maximum_fusion.narrow
  372.4 141.0 %shard_map.221 = (f32[128,1536]{1,0:T(8,128)}, f32[48,1536]{1,0:T(8,128)}, f32[48,512]{1,0:T(8,128)}, f32[48,512]{1,0:T(8,128)}, f32[48,1536]{1,0:T(8,128)}, /*i...) custom-call(bf16[128,1536]{1,0:T(8,128)(2,1)} %copy-done.11, ...), custom_call_target="tpu_custom_call" | custom-call | tf_op jit(solution)/shard_map/pallas_call | solution.py:682
  513.4 1.5 slice_reduce_fusion
  514.9 1.4 copy.126
  516.4 3.0 fusion.48
  (208 shorter events, 55.5 us)
Async XLA Ops:
  7.2 8.0 %copy-start = (bf16[1536,512]{1,0:T(8,128)(2,1)S(1)}, bf16[1536,512]{1,0:T(8,128)(2,1)}, u32[]{:S(2)}) copy-start(bf16[1536,512]{1,0:T(8,128)(2,1)} %param.23) | copy-start | bytes 4718596
  7.2 7.0 %copy-start.4 = (bf16[1,128,1536]{2,1,0:T(8,128)(2,1)S(1)}, bf16[1,128,1536]{2,1,0:T(8,128)(2,1)}, u32[]{:S(2)}) copy-start(bf16[1,128,1536]{2,1,0:T(8,128)(2,1)} %param.19) | copy-start | bytes 1179652
  7.2 7.0 %copy-start.24 = (f32[1536]{0:T(1024)S(1)}, f32[1536]{0:T(1024)}, u32[]{:S(2)}) copy-start(f32[1536]{0:T(1024)} %param.25) | copy-start | bytes 18436
  7.2 44.3 %all-gather.5.cloned.1.call-start = ((), (), s32[]{:S(2)}) async-start(), calls=%async_computation.3 | async-start | bytes 1179648 | tf_op jit(solution)/shard_map/all_gather | solution.py:890
  9.1 7.1 %copy-start.37 = (f32[128]{0:T(128)}, f32[128]{0:T(128)S(1)}, u32[]{:S(2)}) copy-start(f32[128]{0:T(128)S(1)} %fusion.59) | copy-start | bytes 1540
  11.6 1.7 copy-start.18
  11.6 1.7 copy-start.27
  14.1 77.6 %all-gather.3.cloned.1.call-start = ((), (), s32[]{:S(2)}) async-start(), calls=%async_computation.2 | async-start | bytes 1179648 | tf_op jit(solution)/shard_map/all_gather | solution.py:891
  14.4 0.8 copy-start.11
  16.2 307.0 %reduce-scatter.3.cloned.1.call-start = ((), (), s32[]{:S(2)}) async-start(), calls=%async_computation.4 | async-start | bytes 1179648 | tf_op jit(solution)/shard_map/reduce_scatter | solution.py:956
  16.9 6.7 %copy-start.25 = (f32[1536]{0:T(1024)S(1)}, f32[1536]{0:T(1024)}, u32[]{:S(2)}) copy-start(f32[1536]{0:T(1024)} %param.25) | copy-start | bytes 18436
  16.9 6.7 %copy-start.38 = (f32[128]{0:T(128)S(1)}, f32[128]{0:T(128)}, u32[]{:S(2)}) copy-start(f32[128]{0:T(128)} %copy-done.37) | copy-start | bytes 1540
  23.5 3.9 copy-start.19
  23.5 3.9 copy-start.28
  23.5 4.0 copy-start.41
  108.8 5.5 %copy-start.29 = (f32[1536]{0:T(1024)S(1)}, f32[1536]{0:T(1024)}, u32[]{:S(2)}) copy-start(f32[1536]{0:T(1024)} %param.26) | copy-start | bytes 18436
  108.8 5.7 %copy-start.21 = (bf16[1536,32]{0,1:T(8,128)(2,1)S(1)}, bf16[1536,32]{0,1:T(8,128)(2,1)}, u32[]{:S(2)}) copy-start(bf16[1536,32]{0,1:T(8,128)(2,1)} %param.27) | copy-start | bytes 294916
  108.8 6.0 %copy-start.44 = (f32[8]{0:T(128)S(1)}, f32[8]{0:T(128)}, u32[]{:S(2)}) copy-start(f32[8]{0:T(128)} %pad.12.clone) | copy-start | bytes 100
  110.0 4.4 copy-start.10
  113.4 0.9 copy-start.2
  113.4 1.3 copy-start.46
  113.5 0.9 copy-start.39
  114.5 1.1 copy-start.8
  114.7 120.2 %copy-start.36 = (f32[128]{0:T(128)}, f32[128]{0:T(128)S(1)}, u32[]{:S(2)}) copy-start(f32[128]{0:T(128)S(1)} %get-tuple-element.549) | copy-start | bytes 1540
  114.8 120.1 %copy-start.40 = (f32[128]{0:T(128)}, f32[128]{0:T(128)S(1)}, u32[]{:S(2)}) copy-start(f32[128]{0:T(128)S(1)} %fusion.56) | copy-start | bytes 1540
  235.6 10.0 %copy-start.33 = (bf16[128,32]{0,1:T(8,128)(2,1)}, bf16[128,32]{0,1:T(8,128)(2,1)S(1)}, u32[]{:S(2)}) copy-start(bf16[128,32]{0,1:T(8,128)(2,1)S(1)} %multiply_convert_fusion.1) | copy-start | bytes 24580
  238.1 0.9 copy-start.6
  238.1 7.8 %copy-start.13 = (f32[128,8,3,64]{0,3,2,1:T(8,128)S(1)}, f32[128,8,3,64]{0,3,2,1:T(8,128)}, u32[]{:S(2)}) copy-start(f32[128,8,3,64]{0,3,2,1:T(8,128)} %get-tuple-element.183) | copy-start | bytes 2359300
  252.4 5.0 copy-start.1
  274.9 5.0 copy-start.1
  291.9 7.5 %copy-start.35 = (bf16[1536]{0:T(1024)(128)(2,1)S(1)}, bf16[1536]{0:T(1024)(128)(2,1)}, u32[]{:S(2)}) copy-start(bf16[1536]{0:T(1024)(128)(2,1)} %get-tuple-element.464) | copy-start | bytes 9220
  291.9 8.6 %copy-start.9 = (bf16[128,1536]{1,0:T(8,128)(2,1)S(1)}, bf16[128,1536]{1,0:T(8,128)(2,1)}, u32[]{:S(2)}) copy-start(bf16[128,1536]{1,0:T(8,128)(2,1)} %copy-done.8) | copy-start | bytes 1179652
  291.9 8.6 %copy-start.34 = (bf16[128,32]{0,1:T(8,128)(2,1)S(1)}, bf16[128,32]{0,1:T(8,128)(2,1)}, u32[]{:S(2)}) copy-start(bf16[128,32]{0,1:T(8,128)(2,1)} %copy-done.33) | copy-start | bytes 24580
  291.9 71.3 %reduce-scatter.5.cloned.1.call-start = ((), (), s32[]{:S(2)}) async-start(), calls=%async_computation.5 | async-start | bytes 1179648 | tf_op jit(solution)/shard_map/reduce_scatter | solution.py:959
  297.5 26.7 %copy-start.20 = (f32[128,32]{0,1:T(8,128)S(1)}, f32[128,32]{0,1:T(8,128)}, u32[]{:S(2)}) copy-start(f32[128,32]{0,1:T(8,128)} %copy-done.18) | copy-start | bytes 49156
  301.6 61.6 %copy-start.5 = (bf16[1,128,1536]{2,1,0:T(8,128)(2,1)S(1)}, bf16[1,128,1536]{2,1,0:T(8,128)(2,1)}, u32[]{:S(2)}) copy-start(bf16[1,128,1536]{2,1,0:T(8,128)(2,1)} %param.19) | copy-start | bytes 1179652
  325.0 45.1 %copy-start.45 = (bf16[128]{0:T(256)(128)(2,1)S(1)}, bf16[128]{0:T(256)(128)(2,1)}, u32[]{:S(2)}) copy-start(bf16[128]{0:T(256)(128)(2,1)} %pad.3.clone) | copy-start | bytes 772
  372.4 144.0 %copy-start.3 = (f32[128,1536]{1,0:T(8,128)S(1)}, f32[128,1536]{1,0:T(8,128)}, u32[]{:S(2)}) copy-start(f32[128,1536]{1,0:T(8,128)} %copy-done.2) | copy-start | bytes 2359300
  372.4 144.0 %copy-start.7 = (f32[128,1536]{1,0:T(8,128)S(1)}, f32[128,1536]{1,0:T(8,128)}, u32[]{:S(2)}) copy-start(f32[128,1536]{1,0:T(8,128)} %copy-done.6) | copy-start | bytes 2359300
  372.4 144.0 %copy-start.26 = (f32[1536]{0:T(1024)S(1)}, f32[1536]{0:T(1024)}, u32[]{:S(2)}) copy-start(f32[1536]{0:T(1024)} %param.25) | copy-start | bytes 18436
  372.4 144.0 %copy-start.30 = (f32[1536]{0:T(1024)S(1)}, f32[1536]{0:T(1024)}, u32[]{:S(2)}) copy-start(f32[1536]{0:T(1024)} %param.26) | copy-start | bytes 18436
  516.3 3.1 copy-start.23
  516.3 3.8 copy-start.32
  516.3 4.4 copy-start.31
  516.3 5.1 copy-start.22
  516.4 5.8 %copy-start.17 = (f32[2,192,512]{2,1,0:T(8,128)S(1)}, f32[2,192,512]{2,1,0:T(8,128)}, u32[]{:S(2)}) copy-start(f32[2,192,512]{2,1,0:T(8,128)} %get-tuple-element.868) | copy-start | bytes 2359300
  516.4 6.7 %copy-start.16 = (f32[2,192,512]{2,1,0:T(8,128)S(1)}, f32[2,192,512]{2,1,0:T(8,128)}, u32[]{:S(2)}) copy-start(f32[2,192,512]{2,1,0:T(8,128)} %get-tuple-element.869) | copy-start | bytes 2359300
  516.4 7.5 %copy-start.15 = (f32[2,192,512]{2,1,0:T(8,128)S(1)}, f32[2,192,512]{2,1,0:T(8,128)}, u32[]{:S(2)}) copy-start(f32[2,192,512]{2,1,0:T(8,128)} %get-tuple-element.201) | copy-start | bytes 2359300
  (4 other events, 2.5 us)
Sparse Core Ops, SparseCore 0:
  14.3 37.1 all-gather.4
  53.7 37.9 all-gather.2
  292.1 31.0 reduce-scatter.2
  325.4 37.7 reduce-scatter.4

commit v3 on v2

v3 whole, which is shorter than its diff:
```python
import math

import jax
import jax.numpy as jnp
from jax import lax
from jax.experimental import pallas as pl
from jax.experimental.pallas import tpu as pltpu
from jax.sharding import PartitionSpec as P

epsilon = 1e-06
floor_score = -1e30
MESH = pl.DeviceIdType.MESH
BF = jnp.bfloat16
F32 = jnp.float32


class Place:
    def __init__(self):
        e, c = lax.axis_index("expert"), lax.axis_index("context")
        self.hi, self.core = e // 2, e % 2
        self.lo, self.y = c // 4, c % 4
        self.z = lax.axis_index("dp")

    def at(self, hi=0, core=0, lo=0, y=0, z=0):
        e = (self.hi + hi) % 2 * 2 + (self.core + core) % 2
        c = (self.lo + lo) % 2 * 4 + (self.y + y) % 4
        return (e, c, (self.z + z) % 4)

    def line(self, axis):
        if axis == "y":
            return [((self.y + d) % 4, self.at(y=d)) for d in (1, 2, 3)]
        if axis == "z":
            return [((self.z + d) % 4, self.at(z=d)) for d in (1, 2, 3)]
        return [
            ((self.hi + a) % 2 * 2 + (self.lo + b) % 2, self.at(hi=a, lo=b))
            for a, b in ((0, 1), (1, 0), (1, 1))
        ]

    def own(self, axis):
        return {"y": self.y, "z": self.z, "x": self.hi * 2 + self.lo}[axis]


def greet(devices):
    barrier = pltpu.get_barrier_semaphore()
    for device in devices:
        pl.semaphore_signal(barrier, inc=1, device_id=device, device_id_type=MESH)
    pl.semaphore_wait(barrier, len(devices))


def send(src, dst, sems, device):
    copy = pltpu.make_async_remote_copy(
        src_ref=src, dst_ref=dst, send_sem=sems[0], recv_sem=sems[1],
        device_id=device, device_id_type=MESH,
    )
    copy.start()
    return copy


def scatter_start(place, axis, src, landing, sems, begin):
    copies = []
    for d, (index, device) in enumerate(place.line(axis)):
        pair = (sems.at[0, begin + d], sems.at[1, begin + d])
        copies.append(send(src.at[index], landing.at[d], pair, device))
    return copies


def add_up(out, own, landing, lead):
    count = landing.shape[0]

    def body(i, carry):
        total = own[i].astype(F32)
        for d in range(count):
            total = total + landing[d, i].astype(F32)
        out[i] = total.astype(out.dtype)
        return carry

    lax.fori_loop(0, lead, body, 0)


def roll_lanes(u, shift):
    return pltpu.roll(u, shift, 1)


def swap_halves(u):
    lane = lax.broadcasted_iota(jnp.int32, u.shape, 1)
    return jnp.where(lane % 64 < 32, roll_lanes(u, 96), roll_lanes(u, 32))


def to_pairs(blocks):
    a, b, c = blocks
    low = lax.broadcasted_iota(jnp.int32, a.shape, 1) < 64
    return [
        jnp.where(low, a, b), jnp.where(low, roll_lanes(a, 64), roll_lanes(c, 64)), jnp.where(low, b, c)
    ]


def from_pairs(blocks):
    a, b, c = blocks
    low = lax.broadcasted_iota(jnp.int32, a.shape, 1) < 64
    turned = roll_lanes(b, 64)
    return [jnp.where(low, a, turned), jnp.where(low, c, a), jnp.where(low, turned, c)]


def inverse_root(values):
    return lax.rsqrt(jnp.mean(values * values, axis=-1, keepdims=True) + epsilon)


def visible(place, start, rows):
    key = lax.broadcasted_iota(jnp.int32, (rows, 384), 0) + start
    query = lax.broadcasted_iota(jnp.int32, (rows, 384), 1) % 128
    return key <= query + (place.lo * 4 + place.y) * 128


def half_mask(s):
    lane = lax.broadcasted_iota(jnp.int32, (1, 128), 1)
    return jnp.where((lane >= 64) == (s == 1), 1.0, 0.0).astype(BF)


def group_peers(place):
    return {
        (c, h, d): place.at(core=c, hi=h, z=d)
        for c in (0, 1) for h in (0, 1) for d in range(4) if (c, h, d) != (0, 0, 0)
    }


def group_index(place, core=0, hi=0, z=0):
    return ((place.hi + hi) % 2 * 2 + (place.core + core) % 2) * 4 + (place.z + z) % 4


class Spread:
    def __init__(self, place, held, sems):
        self.place, self.held, self.sems = place, held, sems
        self.sent, self.waits = [], {}

    def pair(self, c, h, d):
        slot = c * 8 + h * 4 + d
        return (self.sems.at[0, slot], self.sems.at[1, slot])

    def push(self, origin, target, slot):
        c, h, d = target
        index = group_index(self.place, hi=origin[0], z=origin[1])
        block = self.held.at[index]
        copy = send(block, block, self.pair(*slot), self.place.at(core=c, hi=h, z=d))
        self.sent.append(copy)
        self.waits[slot] = copy

    def land(self, slot):
        self.waits[slot].wait_recv()

    def first(self):
        for d in (1, 3, 2):
            self.push((0, 0), (0, 0, d), (0, 0, (4 - d) % 4))
        self.push((0, 0), (0, 1, 0), (0, 1, 0))
        self.push((0, 0), (1, 0, 0), (1, 0, 0))

    def relay_a(self):
        self.land((0, 1, 0))
        for d in (1, 3):
            self.push((1, 0), (0, 0, d), (0, 1, (4 - d) % 4))
        self.push((1, 0), (1, 0, 0), (1, 1, 0))

    def relay_b(self):
        self.land((0, 0, 2))
        self.push((0, 2), (0, 1, 0), (0, 1, 2))
        self.push((0, 2), (1, 0, 0), (1, 0, 2))
        for d in (1, 3):
            self.land((0, 0, d))
            self.push((0, d), (1, 0, 0), (1, 0, d))

    def finish_near(self):
        for d in range(4):
            self.land((1, 0, d))

    def relay_far(self):
        for d in (1, 3, 2):
            self.land((0, 1, d))
            self.push((1, d), (1, 0, 0), (1, 1, d))

    def finish_far(self):
        for d in range(4):
            self.land((1, 1, d))

    def drain(self):
        for copy in self.sent:
            copy.wait_send()


def add_rows(out, terms):
    def body(i, carry):
        part = pl.ds(pl.multiple_of(i * 16, 16), 16)
        total = terms[0][part].astype(F32)
        for term in terms[1:]:
            total = total + term[part].astype(F32)
        out[part] = total.astype(out.dtype)
        return carry

    lax.fori_loop(0, 8, body, 0)


class Gather:
    def __init__(self, place, parts, pool, landing, sems, own=None):
        self.place, self.parts, self.pool, self.landing, self.sems = place, parts, pool, landing, sems
        self.own = own
        self.sent = []

    def pair(self, slot):
        return (self.sems.at[0, slot], self.sems.at[1, slot])

    def push(self, src, dst, slot, device):
        copy = send(src, dst, self.pair(slot), device)
        self.sent.append(copy)
        return copy

    def swap(self, hi):
        half = (self.place.hi + hi) % 2
        start = group_index(self.place, core=1, hi=hi) - self.place.z
        return self.push(
            self.parts.at[pl.ds(start, 4)], self.pool.at[pl.ds(half * 4, 4)], hi, self.place.at(core=1)
        )

    def chunk(self, hi, z):
        return self.pool.at[(self.place.hi + hi) % 2 * 4 + (self.place.z + z) % 4]

    def mine(self, hi, z):
        if self.own is not None:
            return self.own.at[(self.place.hi + hi) % 2 * 4 + (self.place.z + z) % 4]
        return self.parts.at[group_index(self.place, hi=hi, z=z)]

    def join(self, hi, z, more=()):
        block = self.chunk(hi, z)
        add_rows(block, [block, self.mine(hi, z), *more])
        return block

    def first(self):
        place, land = self.place, self.landing
        self.cross, self.direct = [], []
        for i, d in enumerate((1, 3)):
            self.cross.append(self.push(self.join(1, d), land.at[i], 2 + i, place.at(z=d)))
        self.far = self.push(self.join(1, 2), land.at[2], 4, place.at(hi=1))
        for i, d in enumerate((1, 3)):
            self.direct.append(self.push(self.join(0, d), land.at[3 + i], 5 + i, place.at(z=d)))

    def second(self):
        place, land = self.place, self.landing
        for copy in self.cross:
            copy.wait_recv()
        block = self.join(1, 0, [land.at[0], land.at[1]])
        self.last = [self.push(block, land.at[5], 7, place.at(hi=1))]
        self.far.wait_recv()
        block = self.join(0, 2, [land.at[2]])
        self.last.append(self.push(block, land.at[6], 8, place.at(z=2)))

    def finish(self, out):
        for copy in self.direct + self.last:
            copy.wait_recv()
        land = self.landing
        add_rows(out, [self.chunk(0, 0), self.mine(0, 0), land.at[3], land.at[4], land.at[5], land.at[6]])

    def drain(self):
        for copy in self.sent:
            copy.wait_send()


def contract(left, right, dims):
    return lax.dot_general(left, right, (dims, ((), ())), preferred_element_type=F32)


def expert_kernel(
    n2, cots_far, table, wg, wu, wd,
    dn2, dgate, eo, eg, eu, ed,
    rows, cots, tables, table_sems, rows_sems, cots_sem,
    x_rows, c_rows, pick, gate, dhg, dhu, gact, dg, drow,
    pool, landing, gather_sems, dgate_out, dgate_sems, stage, stage_sems, eo_pool, eo_sems,
):
    place = Place()
    peers = group_peers(place)
    greet(list(peers.values()))
    me = group_index(place)

    small = []
    tables[me] = table[me]
    for (c, h, d), device in peers.items():
        slot = c * 8 + h * 4 + d
        pair = (table_sems.at[0, slot], table_sems.at[1, c * 8 + h * 4 + (4 - d) % 4])
        small.append(send(table.at[group_index(place, c, h, d)], tables.at[me], pair, device))
    rows[me] = n2[...]
    spread_rows = Spread(place, rows, rows_sems)
    spread_rows.first()
    cots_load = pltpu.make_async_copy(cots_far, cots, cots_sem)
    cots_load.start()
    for copy in small:
        copy.wait_recv()

    slots = lax.broadcasted_iota(jnp.int32, (80, 256), 0).astype(F32)
    second = lax.broadcasted_iota(jnp.int32, (1, 256), 1) >= 128

    def select(pair_index):
        parts = []
        for e in range(2):
            here = jnp.concatenate(
                [tables[pair_index * 2, e : e + 1, :], tables[pair_index * 2 + 1, e : e + 1, :]], axis=1
            )
            here = jnp.where(here < 0.0, -1000.0, here + jnp.where(second, 40.0, 0.0))
            weight = jnp.concatenate(
                [tables[pair_index * 2, 2 + e : 3 + e, :], tables[pair_index * 2 + 1, 2 + e : 3 + e, :]],
                axis=1,
            )
            hit = slots == here
            parts.append(jnp.where(hit, 1.0, 0.0).astype(BF))
            place_rows = pl.ds(pl.multiple_of(pair_index * 80, 80), 80)
            gate[e, place_rows, :] = jnp.sum(jnp.where(hit, weight, 0.0), axis=1, keepdims=True)
        pick[pair_index] = jnp.concatenate(parts, axis=0)

    def pull(pair_index, held, out):
        both = jnp.concatenate([held[pair_index * 2], held[pair_index * 2 + 1]], axis=0)
        picked = contract(pick[pair_index], both, ((1,), (0,))).astype(BF)
        place_rows = pl.ds(pl.multiple_of(pair_index * 80, 80), 80)
        out[0, place_rows, :] = picked[0:80]
        out[1, place_rows, :] = picked[80:160]

    def all_pairs(body):
        def step(i, carry):
            body(i)
            return carry
        lax.fori_loop(0, 8, step, 0)

    all_pairs(select)
    spread_rows.relay_a()
    spread_rows.relay_b()
    cots_load.wait()
    all_pairs(lambda p: pull(p, cots, c_rows))

    def pull_side(c, h, held, out):
        start = group_index(place, core=c, hi=h) - place.z
        base = start // 2

        def step(i, carry):
            pull(base + i, held, out)
            return carry

        lax.fori_loop(0, 2, step, 0)

    spread_rows.finish_near()
    pull_side(0, 0, rows, x_rows)
    pull_side(1, 0, rows, x_rows)
    spread_rows.relay_far()
    pull_side(0, 1, rows, x_rows)
    spread_rows.finish_far()
    pull_side(1, 1, rows, x_rows)

    def work(i, carry):
        e, m = i // 2, i % 2
        part = pl.ds(pl.multiple_of(m * 320, 320), 320)
        x = x_rows[e, part, :]
        hg = contract(x, wg[e], ((1,), (0,)))
        hu = contract(x, wu[e], ((1,), (0,)))
        back = contract(c_rows[e, part, :], wd[e], ((1,), (1,)))
        weight = gate[e, part, :]
        sig = 1.0 / (1.0 + jnp.exp(-hg))
        silu = hg * sig
        act = silu * hu
        dg[e, part, :] = jnp.sum(act * back, axis=1, keepdims=True)
        gact[e, part, :] = (weight * act).astype(BF)
        dact = weight * back
        low_hg = (dact * hu * (sig + silu * (1.0 - sig))).astype(BF)
        low_hu = (dact * silu).astype(BF)
        dhg[e, part, :] = low_hg
        dhu[e, part, :] = low_hu
        back_rows = (
            contract(low_hg, wg[e], ((1,), (1,))) + contract(low_hu, wu[e], ((1,), (1,)))
        ).astype(BF)
        for j in range(4):
            drow[m * 4 + j, pl.ds(pl.multiple_of(e * 80, 80), 80), :] = back_rows[j * 80 : (j + 1) * 80]
        return carry

    lax.fori_loop(0, 4, work, 0)
    spread_rows.drain()

    def put_back(pair_index, out):
        both = contract(pick[pair_index], drow[pair_index], ((0,), (0,))).astype(BF)
        out[pair_index * 2] = both[0:128]
        out[pair_index * 2 + 1] = both[128:256]

    def put_side(c, h, out):
        base = (group_index(place, core=c, hi=h) - place.z) // 2

        def step(i, carry):
            put_back(base + i, out)
            return carry

        lax.fori_loop(0, 2, step, 0)

    home = Gather(place, rows, pool, landing, gather_sems)
    put_side(1, 1, rows)
    swaps = [home.swap(1)]
    put_side(1, 0, rows)
    swaps.append(home.swap(0))

    def gate_grads(pair_index):
        chosen = pick[pair_index].astype(F32)
        for e in range(2):
            column = dg[e, pl.ds(pl.multiple_of(pair_index * 80, 80), 80), :]
            line = jnp.sum(chosen[e * 80 : (e + 1) * 80] * column, axis=0, keepdims=True)
            dgate_out[pair_index * 2, e : e + 1, :] = line[:, 0:128]
            dgate_out[pair_index * 2 + 1, e : e + 1, :] = line[:, 128:256]

    dgate_out[...] = jnp.zeros_like(dgate_out)
    all_pairs(gate_grads)
    small_back = []
    dgate[me] = dgate_out[me]
    for (c, h, d), device in peers.items():
        slot = c * 8 + h * 4 + d
        pair = (dgate_sems.at[0, slot], dgate_sems.at[1, c * 8 + h * 4 + (4 - d) % 4])
        small_back.append(send(dgate_out.at[group_index(place, c, h, d)], dgate.at[me], pair, device))
    put_side(0, 1, rows)
    swaps[0].wait_recv()
    put_side(0, 0, rows)
    swaps[1].wait_recv()
    home.first()

    def outputs(i, carry):
        e, m = i // 2, i % 2
        part = pl.ds(pl.multiple_of(m * 320, 320), 320)
        made = contract(gact[e, part, :], wd[e], ((1,), (0,))).astype(BF)
        for j in range(4):
            drow[m * 4 + j, pl.ds(pl.multiple_of(e * 80, 80), 80), :] = made[j * 80 : (j + 1) * 80]
        return carry

    lax.fori_loop(0, 4, outputs, 0)
    all_pairs(lambda p: put_back(p, cots))
    outward = Gather(place, cots, eo_pool, landing, eo_sems)
    out_swaps = [outward.swap(0), outward.swap(1)]
    home.second()
    copies = {}
    step = 0
    for e in range(2):
        for left, right, out in ((x_rows, dhg, eg), (x_rows, dhu, eu), (c_rows, gact, ed)):
            slot = step % 2
            if step >= 2:
                copies[step - 2].wait()

            def weight_grad(i, carry):
                tile = pl.ds(pl.multiple_of(i * 256, 256), 256)
                stage[slot, tile, :] = contract(left[e, :, tile], right[e], ((0,), (0,))).astype(BF)
                return carry

            lax.fori_loop(0, 6, weight_grad, 0)
            copies[step] = pltpu.make_async_copy(stage.at[slot], out.at[e], stage_sems.at[slot])
            copies[step].start()
            step += 1
    for copy in out_swaps:
        copy.wait_recv()
    for h in range(2):
        for d in range(4):
            outward.join(h, d)
    eo_copy = pltpu.make_async_copy(eo_pool, eo, stage_sems.at[2])
    eo_copy.start()
    home.finish(dn2)
    for copy in small_back:
        copy.wait_recv()
    for copy in small + small_back:
        copy.wait_send()
    home.drain()
    outward.drain()
    copies[4].wait()
    copies[5].wait()
    eo_copy.wait()


def run_experts(n2, cots, table, wg, wu, wd):
    vmem = pl.BlockSpec(memory_space=pltpu.VMEM)
    hbm = pl.BlockSpec(memory_space=pl.ANY)
    sems = pltpu.SemaphoreType.DMA
    low = lambda *shape: pltpu.VMEM(shape, BF)
    struct = jax.ShapeDtypeStruct
    return pl.pallas_call(
        expert_kernel,
        out_shape=(
            struct((128, 1536), F32), struct((16, 8, 128), F32), struct((8, 128, 1536), BF),
            struct((2, 1536, 512), BF), struct((2, 1536, 512), BF), struct((2, 1536, 512), BF),
        ),
        in_specs=[vmem, hbm, vmem, vmem, vmem, vmem],
        out_specs=[vmem, vmem, hbm, hbm, hbm, hbm],
        scratch_shapes=[
            low(16, 128, 1536), low(16, 128, 1536), pltpu.VMEM((16, 8, 128), F32),
            sems((2, 16)), sems((2, 16)), sems,
            low(2, 640, 1536), low(2, 640, 1536), low(8, 160, 256), pltpu.VMEM((2, 640, 1), F32),
            low(2, 640, 512), low(2, 640, 512), low(2, 640, 512), pltpu.VMEM((2, 640, 1), F32),
            low(8, 160, 1536),
            low(8, 128, 1536), low(7, 128, 1536), sems((2, 9)),
            pltpu.VMEM((16, 8, 128), F32), sems((2, 16)),
            low(2, 1536, 512), sems((3,)), low(8, 128, 1536), sems((2, 2)),
        ],
        compiler_params=pltpu.CompilerParams(
            collective_id=1, has_side_effects=True, vmem_limit_bytes=62 << 20
        ),
    )(n2, cots, table, wg, wu, wd)


def forward_kernel(
    x_ref, ids, cot, gains, wr, wq, wk, wv, wo,
    n1, qp, kv, lse, attn, y1, n2, gates, table, turn, cots,
    wqv, wkv, wov, weight_sems, cots_sems, k_sems, v_sems, own_sem,
):
    place = Place()
    me = group_index(place)
    context = place.lo * 4 + place.y
    loads = [
        pltpu.make_async_copy(wk, wkv.at[:, 0:512], weight_sems.at[0]),
        pltpu.make_async_copy(wv, wkv.at[:, 512:1024], weight_sems.at[1]),
        pltpu.make_async_copy(wq, wqv, weight_sems.at[2]),
        pltpu.make_async_copy(wo, wov, weight_sems.at[3]),
    ]
    for load in loads:
        load.start()
    own_copy = pltpu.make_async_copy(cot, cots.at[me], own_sem)
    own_copy.start()
    y_line, z_line = place.line("y"), place.line("z")
    lo_peer = place.at(lo=1)
    greet(
        [device for line in (y_line, z_line) for _, device in line]
        + [lo_peer, place.at(hi=1), place.at(core=1)]
    )

    x = x_ref[...].astype(F32)
    n1[...] = (x * inverse_root(x) * gains[0:1, :]).astype(BF)
    lane = lax.broadcasted_iota(jnp.int32, (128, 128), 1)
    row = lax.broadcasted_iota(jnp.int32, (128, 128), 0)
    freqs = jnp.exp((lane % 32).astype(F32) * (-math.log(10000.0) / 32))
    angles = (row + context * 128).astype(F32) * freqs
    cosine = jnp.cos(angles)
    sine = jnp.where(lane % 64 < 32, -1.0, 1.0) * jnp.sin(angles)
    turn[0] = cosine
    turn[1] = sine
    own_copy.wait()
    spread = Spread(place, cots, cots_sems)
    spread.first()

    loads[0].wait()
    loads[1].wait()
    for j in range(4):
        raw = contract(n1[...], wkv[:, j * 128 : (j + 1) * 128], ((1,), (0,)))
        kv[0, context, :, j * 128 : (j + 1) * 128] = (raw * cosine + swap_halves(raw) * sine).astype(BF)
    kv[1, context] = contract(n1[...], wkv[:, 512:1024], ((1,), (0,))).astype(BF)

    sent = []
    waits = {}

    def push(which, lo, y, device, slot):
        block = kv.at[which, (place.lo + lo) % 2 * 4 + (place.y + y) % 4]
        sems = (k_sems, v_sems)[which]
        copy = send(block, block, (sems.at[0, slot], sems.at[1, slot]), device)
        sent.append(copy)
        waits[which, slot] = copy

    for which in (0, 1):
        push(which, 0, 0, lo_peer, 4)
        for d in (1, 3, 2):
            push(which, 0, 0, place.at(y=d), (4 - d) % 4)

    loads[2].wait()
    for j in range(4):
        raw = contract(n1[...], wqv[:, j * 384 : (j + 1) * 384], ((1,), (0,)))
        turned = []
        for r in range(3):
            block = raw[:, r * 128 : (r + 1) * 128]
            turned.append((block * cosine + swap_halves(block) * sine) * 0.125)
        for r, block in enumerate(to_pairs(turned)):
            qp[j, r * 128 : (r + 1) * 128, :] = block.astype(BF)
    waits[0, 4].wait_recv()
    for d in (1, 3, 2):
        push(0, 1, 0, place.at(y=d), 4 + (4 - d) % 4)
    spread.relay_a()
    for d in (1, 3, 2):
        waits[1, d].wait_recv()
        push(1, 0, d, lo_peer, 4 + d)

    wide = lax.broadcasted_iota(jnp.int32, (128, 128), 1)
    chosen = jnp.zeros((128, 128), F32)
    for k in range(8):
        chosen = chosen + jnp.where(ids[:, k : k + 1] == wide, 1.0, 0.0)
    earlier = jnp.where(lane < row, 1.0, 0.0).astype(BF)
    before = contract(earlier, chosen.astype(BF), ((1,), (0,)))
    slots = jnp.where(chosen > 0.0, before, -1.0).T
    table[...] = jnp.zeros_like(table)
    for g in range(16):
        table[g, 0:2, :] = slots[2 * g : 2 * g + 2, :]

    for d in (1, 3, 2):
        waits[0, d].wait_recv()
        waits[0, 4 + d].wait_recv()
        waits[1, 4 + d].wait_recv()
    waits[1, 4].wait_recv()
    spread.relay_b()

    def attend(j, carry):
        lanes = pl.ds(pl.multiple_of(j * 128, 128), 128)
        keys = kv[0, :, :, lanes].reshape(1024, 128)
        values = kv[1, :, :, lanes].reshape(1024, 128)
        halves = []
        for s in range(2):
            scores = contract(keys, qp[j] * half_mask(s), ((1,), (1,)))
            scores = jnp.where(visible(place, 0, 1024), scores, floor_score)
            top = jnp.max(scores, axis=0, keepdims=True)
            probs = jnp.exp(scores - top)
            total = jnp.sum(probs, axis=0, keepdims=True)
            lse[j * 2 + s] = top + jnp.log(total)
            out = contract(values, probs.astype(BF), ((0,), (0,))) * (1.0 / total)
            halves.append(out[s * 64 : (s + 1) * 64])
        joined = jnp.concatenate(halves, axis=0).T
        for r, block in enumerate(from_pairs([joined[r * 128 : (r + 1) * 128] for r in range(3)])):
            attn[:, pl.ds(pl.multiple_of(j * 384 + r * 128, 128), 128)] = block.astype(BF)
        return carry

    lax.fori_loop(0, 4, attend, 0)
    spread.relay_far()

    loads[3].wait()
    for j in range(4):
        part = slice(j * 384, (j + 1) * 384)
        y1[:, part] = x_ref[:, part].astype(F32) + contract(attn[...], wov[:, part], ((1,), (0,)))
    y = y1[...]
    n2[...] = (y * inverse_root(y) * gains[1:2, :]).astype(BF)
    logits = contract(n2[...], wr[...], ((1,), (0,)))
    logits = jnp.where(chosen > 0.0, logits, -jnp.inf)
    weights = jnp.exp(logits - jnp.max(logits, axis=1, keepdims=True))
    weights = weights / jnp.sum(weights, axis=1, keepdims=True)
    gates[...] = weights
    turned = weights.T
    for g in range(16):
        table[g, 2:4, :] = turned[2 * g : 2 * g + 2, :]
    spread.finish_near()
    spread.finish_far()
    spread.drain()
    for copy in sent:
        copy.wait_send()


def run_forward(x, ids, cot, gains, wr, wq, wk, wv, wo):
    vmem = pl.BlockSpec(memory_space=pltpu.VMEM)
    hbm = pl.BlockSpec(memory_space=pl.ANY)
    sems = pltpu.SemaphoreType.DMA
    low = lambda *shape: pltpu.VMEM(shape, BF)
    struct = jax.ShapeDtypeStruct
    return pl.pallas_call(
        forward_kernel,
        out_shape=(
            struct((128, 1536), BF), struct((4, 384, 128), BF), struct((2, 8, 128, 512), BF),
            struct((8, 1, 384), F32), struct((128, 1536), BF), struct((128, 1536), F32),
            struct((128, 1536), BF), struct((128, 128), F32), struct((16, 8, 128), F32),
            struct((2, 128, 128), F32), struct((16, 128, 1536), BF),
        ),
        in_specs=[vmem] * 5 + [hbm] * 4,
        out_specs=[vmem] * 10 + [hbm],
        scratch_shapes=[
            low(1536, 1536), low(1536, 1024), low(1536, 1536), sems((4,)),
            sems((2, 16)), sems((2, 8)), sems((2, 8)), sems,
        ],
        compiler_params=pltpu.CompilerParams(
            collective_id=2, has_side_effects=True, vmem_limit_bytes=60 << 20
        ),
    )(x, ids, cot, gains, wr, wq, wk, wv, wo)


WIDTH = {"o": 512, "q": 384, "s": 256}
ORDERS = {"o": "xyz", "q": "zyx", "s": "yzx"}


def stream_index(order, block, half):
    at = {"x": half * 2 + block // 16, "y": block // 4 % 4, "z": block % 4}
    return tuple(at[axis] for axis in order)


def fill_stream(out, order, left, right, width):
    for half in range(2):
        columns = right[:, half * width : (half + 1) * width]
        for tile in range(4):
            grads = contract(left[:, tile * 384 : (tile + 1) * 384], columns, ((0,), (0,))).astype(BF)
            for j in range(8):
                index = stream_index(order, tile * 8 + j, half)
                out[(*index, slice(None), slice(0, width))] = grads[j * 48 : (j + 1) * 48]


class Homeward:
    def __init__(self, place, pool, near, landing, sems, near_sems):
        self.place, self.pool, self.near, self.landing, self.sems = place, pool, near, landing, sems
        self.loads = []
        for i, (h, d) in enumerate(((1, 0), (0, 2), (0, 0))):
            self.loads.append(pltpu.make_async_copy(self.chunk(h, d), near.at[i], near_sems.at[i]))
            self.loads[-1].start()
        self.sent = []

    def chunk(self, hi, z):
        return self.pool.at[(self.place.hi + hi) % 2 * 4 + (self.place.z + z) % 4]

    def push(self, src, slot, device):
        pair = (self.sems.at[0, slot], self.sems.at[1, slot])
        self.sent.append(send(src, self.landing.at[slot], pair, device))

    def first(self):
        place = self.place
        self.push(self.chunk(1, 1), 0, place.at(z=1))
        self.push(self.chunk(1, 3), 1, place.at(z=3))
        self.push(self.chunk(1, 2), 2, place.at(hi=1))
        self.push(self.chunk(0, 1), 3, place.at(z=1))
        self.push(self.chunk(0, 3), 4, place.at(z=3))

    def second(self):
        for load in self.loads:
            load.wait()
        near, land = self.near, self.landing
        for copy in self.sent[:3]:
            copy.wait_recv()
        add_rows(near.at[0], [near.at[0], land.at[0], land.at[1]])
        self.push(near.at[0], 5, self.place.at(hi=1))
        add_rows(near.at[1], [near.at[1], land.at[2]])
        self.push(near.at[1], 6, self.place.at(z=2))

    def finish(self, out, base):
        for copy in self.sent[3:]:
            copy.wait_recv()
        add_rows(out, [base, self.near.at[2]] + [self.landing.at[i] for i in (3, 4, 5, 6)])

    def drain(self):
        for copy in self.sent:
            copy.wait_send()


def backward_kernel(
    dn2r, dgate, gates, n2, y1, cot, x_ref, n1, attn, qp, kv, lse, turn, gains, wr,
    wo, wq, wk, wv, eo, eg, eu, ed,
    mixed, gt, gq, gk, gv, go, gs, og, ou, od, far_p, far_q,
    w_big, w_kv, weight_sems,
    n1c, attnc, dqc, dkvc, dbrc, pair_sems,
    dgt, dbr, dap, delta, dq, dk, dv, dy1, dkv, land_a, land_b, land_c, land_d, kv_sems,
    send_o, send_q, send_s, land1_o, land1_q, land1_s, mid_o, mid_q, mid_s,
    land2_o, land2_q, land2_s, last_o, last_q, last_s, land3_o, land3_q, land3_s, dense_sems,
    mine, quarters, quarter_sems,
    near, home_landing, home_sems, near_sems,
    stage, stage_sems, sum_p, sum_q, land_p2, land_q2, expert_sems,
):
    place = Place()
    context = place.lo * 4 + place.y
    y_line, z_line, x_line = (place.line(axis) for axis in "yzx")
    sibling, cross, lo_device = place.at(core=1), place.at(hi=1, core=1), place.at(lo=1)
    other_lo = (place.lo + 1) % 2
    load_o = pltpu.make_async_copy(wo, w_big, weight_sems.at[0])
    load_o.start()
    load_kv = [
        pltpu.make_async_copy(wk, w_kv.at[:, 0:512], weight_sems.at[1]),
        pltpu.make_async_copy(wv, w_kv.at[:, 512:1024], weight_sems.at[2]),
    ]
    for load in load_kv:
        load.start()
    greet([device for line in (y_line, z_line, x_line) for _, device in line] + [sibling, cross])
    pending = []

    mats = (eg, eu, ed)
    stage_p, stage_q = [], []
    at = 0
    for m, mat in enumerate(mats):
        for d, (index, device) in enumerate(y_line):
            pair = (expert_sems.at[0, at], expert_sems.at[1, at])
            stage_p.append(send(mat.at[0, :, index], far_p.at[d, m], pair, device))
            at += 1
        pair = (expert_sems.at[0, at], expert_sems.at[1, at])
        stage_q.append(send(mat.at[1, other_lo], far_q.at[m], pair, lo_device))
        at += 1
    home = Homeward(place, eo, near, home_landing, home_sems, near_sems)
    home.first()

    def share(i, rows, both, half):
        source = rows if half is None else rows.at[1 - place.core]
        pair = (pair_sems.at[0, i], pair_sems.at[1, i])
        copy = send(source, both.at[pl.ds(128, 128)], pair, sibling)
        both[0:128, :] = rows[...] if half is None else rows[place.core]
        pending.append(copy)
        return copy

    share_attn = share(0, attn, attnc, None)
    share_n1 = share(1, n1, n1c, None)

    dgt[...] = jnp.zeros_like(dgt)
    for g in range(16):
        dgt[2 * g : 2 * g + 2, :] = dgate[g, 0:2, :]
    weights = gates[...]
    dgates = dgt[...].T
    dlogits = weights * (dgates - jnp.sum(weights * dgates, axis=1, keepdims=True))
    dlogits = dlogits.astype(BF)
    dn2 = dn2r[...] + contract(dlogits, wr[...], ((1,), (1,)))
    y = y1[...]
    root = inverse_root(y)
    scaled = dn2 * gains[1:2, :]
    inner = jnp.mean(scaled * y, axis=-1, keepdims=True)
    dy = cot[...].astype(F32) + root * scaled - y * (root * root * root * inner)
    dy1[...] = dy
    low = dy.astype(BF)
    dbr[0] = low[:, 0:768]
    dbr[1] = low[:, 768:1536]
    share_dbr = share(2, dbr, dbrc, 1)
    gain_rows = (dn2 * y * root).astype(BF)
    column = jnp.where(lax.broadcasted_iota(jnp.int32, (128, 128), 1) == 32, 1.0, 0.0).astype(BF)
    narrow_left = jnp.concatenate([n2[...], gain_rows], axis=0)
    narrow_right = jnp.concatenate([dlogits, column], axis=0)
    for tile in range(4):
        part = contract(
            narrow_left[:, tile * 384 : (tile + 1) * 384], narrow_right, ((0,), (0,))
        ).astype(BF)
        for j in range(8):
            for half in range(2):
                index = stream_index(ORDERS["o"], tile * 8 + j, half)
                send_o[(*index, slice(None), slice(384, 512))] = part[j * 48 : (j + 1) * 48]

    load_o.wait()
    for j in range(4):
        back = contract(low, w_big[j * 384 : (j + 1) * 384, :], ((1,), (1,)))
        grads = to_pairs([back[:, r * 128 : (r + 1) * 128] for r in range(3)])
        outs = to_pairs(
            [attn[:, j * 384 + r * 128 : j * 384 + (r + 1) * 128].astype(F32) for r in range(3)]
        )
        grads = jnp.concatenate(grads, axis=0).astype(BF)
        dap[j] = grads
        product = (grads.astype(F32) * jnp.concatenate(outs, axis=0)).T
        for s in range(2):
            delta[j * 2 + s] = jnp.sum(product[s * 64 : (s + 1) * 64], axis=0, keepdims=True)
    load_q = pltpu.make_async_copy(wq, w_big, weight_sems.at[0])
    load_q.start()

    sends = {"o": send_o, "q": send_q, "s": send_s}
    lands = {
        "o": (land1_o, land2_o, land3_o), "q": (land1_q, land2_q, land3_q),
        "s": (land1_s, land2_s, land3_s),
    }
    mids = {"o": (mid_o, last_o), "q": (mid_q, last_q), "s": (mid_s, last_s)}
    begin = {"o": 0, "q": 9, "s": 18}
    flight = {}

    def launch(name, phase):
        source = sends[name] if phase == 0 else mids[name][phase - 1]
        flight[name] = scatter_start(
            place, ORDERS[name][phase], source, lands[name][phase], dense_sems,
            begin[name] + 3 * phase,
        )

    def land(name, phase):
        for copy in flight[name]:
            copy.wait_recv()
        pending.extend(flight[name])
        source = sends[name] if phase == 0 else mids[name][phase - 1]
        own = source.at[place.own(ORDERS[name][phase])]
        landing = lands[name][phase]
        if phase == 0:
            out = mids[name][0]

            def body(i, carry):
                a, b = i // 4, i % 4
                total = own[a, b].astype(F32)
                for d in range(3):
                    total = total + landing[d, a, b].astype(F32)
                out[a, b] = total.astype(BF)
                return carry

            lax.fori_loop(0, 16, body, 0)
        elif phase == 1:
            add_up(mids[name][1], own, landing, 4)
        else:
            total = own[...].astype(F32)
            for d in range(3):
                total = total + landing[d].astype(F32)
            mine["oqs".index(name), :, 0 : WIDTH[name]] = total.astype(BF)

    share_attn.wait_recv()
    share_dbr.wait_recv()
    fill_stream(send_o, ORDERS["o"], attnc, dbrc, 384)
    launch("o", 0)

    cosine, sine = turn[0], turn[1]

    def attend(j, carry):
        lanes = pl.ds(pl.multiple_of(j * 128, 128), 128)
        turned = [jnp.zeros((128, 384), F32) for _ in range(2)]
        for block in range(2):
            part = slice(block * 4, (block + 1) * 4)
            keys = kv[0, part, :, lanes].reshape(512, 128)
            values = kv[1, part, :, lanes].reshape(512, 128)
            grad_keys = jnp.zeros((512, 128), F32)
            grad_values = jnp.zeros((512, 128), F32)
            seen = visible(place, block * 512, 512)
            for s in range(2):
                queries = qp[j] * half_mask(s)
                grads = dap[j] * half_mask(s)
                scores = contract(keys, queries, ((1,), (1,)))
                probs = jnp.exp(jnp.where(seen, scores, floor_score) - lse[j * 2 + s])
                back = contract(values, grads, ((1,), (1,)))
                grad_scores = (probs * (back - delta[j * 2 + s])).astype(BF)
                grad_values = grad_values + contract(probs.astype(BF), grads, ((1,), (0,)))
                grad_keys = grad_keys + contract(grad_scores, queries, ((1,), (0,)))
                turned[s] = turned[s] + contract(keys, grad_scores, ((0,), (0,)))
            dkv[part, j, 0] = grad_keys.astype(BF).reshape(4, 128, 128)
            dkv[part, j, 1] = grad_values.astype(BF).reshape(4, 128, 128)
        joined = jnp.concatenate([turned[0][0:64], turned[1][64:128]], axis=0).T * 0.125
        blocks = from_pairs([joined[r * 128 : (r + 1) * 128] for r in range(3)])
        for r, part in enumerate(blocks):
            raw = part * cosine - swap_halves(part) * sine
            lanes = pl.ds(pl.multiple_of((j % 2) * 384 + r * 128, 128), 128)
            dq[j // 2, :, lanes] = raw.astype(BF)
        return carry

    kv_sent = []

    def kv_push(src, dst, slot, device):
        copy = send(src, dst, (kv_sems.at[0, slot], kv_sems.at[1, slot]), device)
        kv_sent.append(copy)
        return copy

    def kv_add(out, count, terms):
        def body(i, carry):
            a, b, c = i // 4, i // 2 % 2, i % 2
            block = out(a)
            total = block[b, c].astype(F32)
            for term in terms:
                total = total + term(a)[b, c].astype(F32)
            block[b, c] = total.astype(BF)
            return carry

        lax.fori_loop(0, count * 4, body, 0)

    first, later = pl.ds(0, 2), pl.ds(2, 2)
    lax.fori_loop(0, 2, attend, 0)
    lead = kv_push(dkv.at[pl.ds(other_lo * 4, 4), first], land_a, 0, lo_device)
    lax.fori_loop(2, 4, attend, 0)
    legs = []
    for d, (index, device) in enumerate(y_line):
        for lo in range(2):
            legs.append(
                kv_push(dkv.at[lo * 4 + index, later], land_c.at[d, lo], 4 + d * 2 + lo, device)
            )
    share_dq = share(3, dq, dqc, 1)
    lead.wait_recv()
    kv_add(lambda a: dkv.at[place.lo * 4 + a, first], 4, [lambda a: land_a.at[a]])
    legs_b = [
        kv_push(dkv.at[place.lo * 4 + index, first], land_b.at[d], 1 + d, device)
        for d, (index, device) in enumerate(y_line)
    ]
    share_n1.wait_recv()
    share_dq.wait_recv()
    fill_stream(send_q, ORDERS["q"], n1c, dqc, 384)
    launch("q", 0)
    for copy in legs:
        copy.wait_recv()
    kv_add(
        lambda a: dkv.at[a * 4 + place.y, later], 2,
        [lambda a, d=d: land_c.at[d, a] for d in range(3)],
    )
    leg_d = kv_push(dkv.at[other_lo * 4 + place.y, later], land_d, 10, lo_device)
    for copy in legs_b:
        copy.wait_recv()

    def key_grads(j, terms):
        total_k = dkv[context, j, 0].astype(F32)
        total_v = dkv[context, j, 1].astype(F32)
        for term in terms:
            total_k = total_k + term[0].astype(F32)
            total_v = total_v + term[1].astype(F32)
        raw = total_k * cosine - swap_halves(total_k) * sine
        lanes = (j % 2) * 256
        dk[j // 2, :, lanes : lanes + 128] = raw.astype(BF)
        dk[j // 2, :, lanes + 128 : lanes + 256] = total_v.astype(BF)

    for j in range(2):
        key_grads(j, [land_b.at[d, j] for d in range(3)])
    leg_d.wait_recv()
    for j in range(2):
        key_grads(2 + j, [land_d.at[j]])
    share_dkv = share(4, dk, dkvc, 1)
    share_dkv.wait_recv()
    fill_stream(send_s, ORDERS["s"], n1c, dkvc, 256)
    launch("s", 0)
    pending.extend(kv_sent)

    for load in load_kv:
        load.wait()
    load_q.wait()
    x = x_ref[...].astype(F32)
    root = inverse_root(x)
    keys = jnp.concatenate([dk[j // 2, :, j % 2 * 256 : j % 2 * 256 + 128] for j in range(4)], axis=1)
    values = jnp.concatenate(
        [dk[j // 2, :, j % 2 * 256 + 128 : j % 2 * 256 + 256] for j in range(4)], axis=1
    )
    both = jnp.concatenate([keys, values], axis=1)
    queries = jnp.concatenate([dq[0], dq[1]], axis=1)
    for j in range(4):
        part = slice(j * 384, (j + 1) * 384)
        gt[:, part] = contract(queries, w_big[part, :], ((1,), (1,))) + contract(
            both, w_kv[part, :], ((1,), (1,))
        )
    scaled = gt[...] * gains[0:1, :]
    inner = jnp.mean(scaled * x, axis=-1, keepdims=True)
    gt[...] = dy1[...] + root * scaled - x * (root * root * root * inner)

    home.second()
    land("o", 0)
    launch("o", 1)
    land("o", 1)
    launch("o", 2)
    land("q", 0)
    launch("q", 1)
    land("s", 0)
    launch("s", 1)
    land("q", 1)
    launch("q", 2)
    land("s", 1)
    launch("s", 2)
    land("o", 2)
    land("q", 2)
    land("s", 2)
    own_quarter = place.core * 2 + place.hi
    gathered = []
    for i, (a, b) in enumerate(((0, 1), (1, 0), (1, 1))):
        pair = (quarter_sems.at[0, i], quarter_sems.at[1, i])
        gathered.append(send(mine, quarters.at[own_quarter], pair, place.at(hi=a, core=b)))
    quarters[own_quarter] = mine[...]

    for copy in stage_p + stage_q:
        copy.wait_recv()
    pending.extend(stage_p + stage_q)
    steps = []
    for m, mat in enumerate(mats):
        for lo in range(2):
            terms = [mat.at[0, lo, place.y]] + [far_p.at[d, m, lo] for d in range(3)]
            steps.append((terms, sum_p.at[lo, m]))
    for m, mat in enumerate(mats):
        for pair_y in range(2):
            for i in range(2):
                y_at = pair_y * 2 + i
                steps.append(([mat.at[1, place.lo, y_at], far_q.at[m, y_at]], sum_q.at[y_at, m]))

    def fetch(step):
        loads = []
        for i, term in enumerate(steps[step][0]):
            loads.append(
                pltpu.make_async_copy(term, stage.at[step % 2, i], stage_sems.at[step % 2, i])
            )
            loads[-1].start()
        return loads

    second = []
    ready = fetch(0)
    for step, (terms, out) in enumerate(steps):
        following = fetch(step + 1) if step + 1 < len(steps) else None
        for load in ready:
            load.wait()

        def fold(i, carry):
            part = pl.ds(pl.multiple_of(i * 48, 16), 48)
            total = stage[step % 2, 0, part].astype(F32)
            for term in range(1, len(terms)):
                total = total + stage[step % 2, term, part].astype(F32)
            out[part] = total.astype(BF)
            return carry

        lax.fori_loop(0, 4, fold, 0)
        ready = following
        if step == 5:
            pair = (expert_sems.at[0, 12], expert_sems.at[1, 12])
            second.append(send(sum_p.at[other_lo], land_p2, pair, lo_device))
    for d, (index, device) in enumerate(y_line):
        pair = (expert_sems.at[0, 13 + d], expert_sems.at[1, 13 + d])
        second.append(send(sum_q.at[index], land_q2.at[d], pair, device))

    home.finish(mixed, y1)
    home.drain()
    for copy in gathered:
        copy.wait_recv()
    pending.extend(gathered)
    for q in range(4):
        go[:, q * 384 : (q + 1) * 384] = quarters[q, 0, :, 0:384].astype(F32)
        gq[:, q * 384 : (q + 1) * 384] = quarters[q, 1, :, 0:384].astype(F32)
        gk[:, q * 128 : (q + 1) * 128] = quarters[q, 2, :, 0:128].astype(F32)
        gv[:, q * 128 : (q + 1) * 128] = quarters[q, 2, :, 128:256].astype(F32)
    narrow = quarters[0, 0, :, 384:512].astype(F32) + quarters[2, 0, :, 384:512].astype(F32)
    rows = pl.ds(pl.multiple_of((context * 4 + place.z) * 48, 16), 48)
    line = jnp.sum(gq[...] * w_big[rows, :].astype(F32), axis=1, keepdims=True)
    line = line + jnp.sum(gk[...] * w_kv[rows, 0:512].astype(F32), axis=1, keepdims=True)
    line = line + jnp.sum(gv[...] * w_kv[rows, 512:1024].astype(F32), axis=1, keepdims=True)
    gs[...] = jnp.where(lax.broadcasted_iota(jnp.int32, (48, 128), 1) == 33, line, narrow)

    for copy in second:
        copy.wait_recv()
    pending.extend(second)
    for m, out in enumerate((og, ou, od)):
        def finish(i, carry):
            part = pl.ds(pl.multiple_of(i * 48, 16), 48)
            out[0, part] = sum_p[place.lo, m, part].astype(F32) + land_p2[m, part].astype(F32)
            total = sum_q[place.y, m, part].astype(F32)
            for d in range(3):
                total = total + land_q2[d, m, part].astype(F32)
            out[1, part] = total
            return carry

        lax.fori_loop(0, 4, finish, 0)
    for copy in pending:
        copy.wait_send()


def run_backward(*operands):
    vmem = pl.BlockSpec(memory_space=pltpu.VMEM)
    hbm = pl.BlockSpec(memory_space=pl.ANY)
    sems = pltpu.SemaphoreType.DMA
    struct = jax.ShapeDtypeStruct
    f32 = lambda *shape: struct(shape, F32)
    low = lambda *shape: pltpu.VMEM(shape, BF)
    high = lambda *shape: pltpu.VMEM(shape, F32)
    wide = [WIDTH[name] for name in "oqs"]
    return pl.pallas_call(
        backward_kernel,
        out_shape=(
            struct((128, 1536), BF), f32(128, 1536),
            f32(48, 1536), f32(48, 512), f32(48, 512), f32(48, 1536), f32(48, 128),
            f32(2, 192, 512), f32(2, 192, 512), f32(2, 192, 512),
            struct((3, 3, 2, 192, 512), BF), struct((3, 4, 192, 512), BF),
        ),
        in_specs=[vmem] * 15 + [hbm] * 8,
        out_specs=[vmem] * 10 + [hbm] * 2,
        scratch_shapes=[
            low(1536, 1536), low(1536, 1024), sems((3,)),
            low(256, 1536), low(256, 1536), low(256, 768), low(256, 512), low(256, 768),
            sems((2, 5)),
            high(128, 128), low(2, 128, 768), low(4, 384, 128), high(8, 1, 384),
            low(2, 128, 768), low(2, 128, 512), low(16, 128), high(128, 1536),
            low(8, 4, 2, 128, 128), low(4, 2, 2, 128, 128), low(3, 2, 2, 128, 128),
            low(3, 2, 2, 2, 128, 128), low(2, 2, 128, 128), sems((2, 11)),
            *[low(4, 4, 4, 48, w) for w in wide],
            *[low(3, 4, 4, 48, w) for w in wide],
            *[low(4, 4, 48, w) for w in wide],
            *[low(3, 4, 48, w) for w in wide],
            *[low(4, 48, w) for w in wide],
            *[low(3, 48, w) for w in wide],
            sems((2, 27)),
            low(3, 48, 512), low(4, 3, 48, 512), sems((2, 3)),
            low(3, 128, 1536), low(7, 128, 1536), sems((2, 7)), sems((3,)),
            low(2, 4, 192, 512), sems((2, 4)),
            low(2, 3, 192, 512), low(4, 3, 192, 512), low(3, 192, 512), low(3, 3, 192, 512),
            sems((2, 16)),
        ],
        compiler_params=pltpu.CompilerParams(
            collective_id=3, has_side_effects=True, vmem_limit_bytes=63 << 20
        ),
    )(*operands)


def shards(
    tokens, expert_ids, w_query, w_key, w_value, w_out, gain_attn, gain_moe, w_router,
    w_gate, w_up, w_down, cotangent,
):
    gains = jnp.stack([gain_attn, gain_moe])
    router = jnp.pad(w_router, ((0, 0), (0, 96)))
    x, cot = tokens[0], cotangent[0]
    n1, qp, kv, lse, attn, y1, n2, gates, table, turn, cots = run_forward(
        x, expert_ids[0], cot, gains, router, w_query, w_key, w_value, w_out
    )
    dn2, dgate, eo, eg, eu, ed = run_experts(n2, cots, table, w_gate, w_up, w_down)
    blocks = lambda grads: grads.reshape(2, 2, 4, 192, 512)
    mixed, gt, gq, gk, gv, go, gs, og, ou, od, _, _ = run_backward(
        dn2, dgate, gates, n2, y1, cot, x, n1, attn, qp, kv, lse, turn, gains, router,
        w_out, w_query, w_key, w_value, eo, blocks(eg), blocks(eu), blocks(ed),
    )
    own = lax.axis_index("context") * 4 + lax.axis_index("dp")
    own_gain = lax.dynamic_slice(gain_attn, (own * 48,), (48,))
    return (
        mixed[None], gt[None], gq, gk, gv, go, gs[:, 33] / own_gain, gs[:, 32], gs[:, :32],
        og, ou, od.transpose(0, 2, 1),
    )


def solution(mesh):
    in_specs = (
        P(("expert", "dp"), "context", None),
        P(("expert", "dp"), "context", None),
        P(),
        P(),
        P(),
        P(),
        P(),
        P(),
        P(),
        P(("expert", "dp"), None, None),
        P(("expert", "dp"), None, None),
        P(("expert", "dp"), None, None),
        P(("expert", "dp"), "context", None),
    )
    out_specs = (
        P(("expert", "dp"), "context", None),
        P(("expert", "dp"), "context", None),
        P(("context", "dp"), None),
        P(("context", "dp"), None),
        P(("context", "dp"), None),
        P(("context", "dp"), None),
        P(("context", "dp")),
        P(("context", "dp")),
        P(("context", "dp"), None),
        P(("expert", "dp"), "context", None),
        P(("expert", "dp"), "context", None),
        P(("expert", "dp"), None, "context"),
    )
    return jax.shard_map(shards, mesh=mesh, in_specs=in_specs, out_specs=out_specs, check_vma=False)
```

time: 534 us -> 364 us (0.68)
  waiting for transfers between devices: 87.7 us -> 0 us
  Pallas kernels: 260 us -> 341 us
  matrix products: 76.1 us -> 0 us
  local copies, waits for them, and re-layouts: 59 us -> 18 us
  other arithmetic: 34 us -> 1.9 us
  between operations: 14.4 us -> 0.73 us
    pallas_call x1 -> x2, Pallas kernels: 141 us -> 253 us  [the longest x1 205 us: run_backward(): pl.pallas_call(backward_kernel, out_shape=(struct((128, 1536), BF), f32(1...]
    dot_general x25 -> x0, matrix products: 76.1 us -> none  [the longest x4 14.7 us: block_scores(): jnp.einsum('qkgd,skd->kgqs', query, key_heads, preferred_element_type=jnp...]
    reduce_scatter x2 -> x0, waiting for transfers between devices: 53 us -> none  [the longest x1 35.5 us: shards(): lax.psum_scatter(grad_value_all.astype(jnp.bfloat16), 'context', scatter_...]
    all_gather x2 -> x0, waiting for transfers between devices: 34.3 us -> none  [the longest x1 22.2 us: shards(): lax.all_gather(key_rows, 'context', axis=0, tiled=True)]
    pallas_call x1, Pallas kernels: 119 us -> 88.1 us  [run_experts(): pl.pallas_call(expert_kernel, out_shape=(struct((128, 1536), F32), struct...]
    dynamic_slice x14 -> x0, local copies, waits for them, and re-layouts: 17.1 us -> none  [attention_forward(): lax.scan(gather_stats, start_stats, (key_blocks, starts))]
    unnamed x104 -> x24, local copies, waits for them, and re-layouts: 24 us -> 14.2 us
    reduce_sum x6 -> x0, other arithmetic: 9.57 us -> none  [the longest x2 8.21 us: gather_stats(): jnp.sum(jnp.exp(scores - new_top[..., None]), axis=-1)]
  transfers between devices with their start and end apart: 4 -> 0, of which waited for: 4 -> 0; matrix products, arithmetic and copies ran while one was open for 11% -> 0% of each run, Pallas kernels for 0% -> 0%
where the time goes in v3:
time: 364 us; the launch traced here: 362 us
  Pallas kernels  341 us (94%)
  local copies, waits for them, and re-layouts  18 us (5%)
    pallas_call x1, Pallas kernels, run_backward(): pl.pallas_call(backward_kernel, out_shape=(struct((128, 1536), BF), f32(1...  205 us
    pallas_call x1, Pallas kernels, run_experts(): pl.pallas_call(expert_kernel, out_shape=(struct((128, 1536), F32), struct...  88.1 us
    pallas_call x1, Pallas kernels, run_forward(): pl.pallas_call(forward_kernel, out_shape=(struct((128, 1536), BF), struct...  47.7 us
    unnamed x24, local copies, waits for them, and re-layouts  14.2 us

profile of v3, /device:TPU:1, one launch (start us, length us, event | category | flops | bytes accessed | tf_op | source)
XLA Modules:
  0.0 361.9 jit_solution(5887276142861786651)
XLA Ops:
  0.6 1.1 copy.29
  1.8 0.8 pad.4.wr
  2.6 0.7 stack.10
  3.3 0.7 stack.9
  4.0 0.6 pad_maximum_fusion.gains
  4.6 1.4 copy.28
  6.0 47.7 %shard_map.220 = (bf16[128,1536]{1,0:T(8,128)(2,1)}, bf16[4,384,128]{2,1,0:T(8,128)(2,1)}, bf16[2,8,128,512]{3,2,1,0:T(8,128)(2,1)}, f32[8,1,384]{2,1,0:T(1,128)...) custom-call(bf16[128,1536]{1,0:T(8,128)(2,1)} %bitcast.13, ...), custom_call_target="tpu_custom_call" | custom-call | tf_op jit(solution)/shard_map/pallas_call | solution.py:645
  53.8 88.1 %shard_map.221 = (f32[128,1536]{1,0:T(8,128)}, f32[16,8,128]{2,1,0:T(8,128)}, bf16[8,128,1536]{2,1,0:T(8,128)(2,1)}, bf16[2,1536,512]{2,1,0:T(8,128)(2,1)}, bf16...) custom-call(bf16[128,1536]{1,0:T(8,128)(2,1)} %get-tuple-element.39.n2, ...), custom_call_target="tpu_custom_call" | custom-call | tf_op jit(solution)/shard_map/pallas_call | solution.py:476
  141.9 205.4 %shard_map.222 = (bf16[128,1536]{1,0:T(8,128)(2,1)}, f32[128,1536]{1,0:T(8,128)}, f32[48,1536]{1,0:T(8,128)}, f32[48,512]{1,0:T(8,128)}, f32[48,512]{1,0:T(8,128...) custom-call(f32[128,1536]{1,0:T(8,128)} %get-tuple-element.42.dn2r, ...), custom_call_target="tpu_custom_call" | custom-call | tf_op jit(solution)/shard_map/pallas_call | solution.py:1115
  347.3 0.0 copy-start.5
  347.3 0.0 copy-start.4
  347.4 0.0 copy-start.3
  347.4 0.0 copy-start.2
  347.4 0.0 copy-start.1
  347.4 1.6 slice_reduce_fusion
  349.0 1.3 dynamic-slice_divide_fusion
  350.3 1.4 copy.30
  351.7 1.8 copy.40
  353.5 0.0 copy-start
  353.5 2.1 copy.41
  355.6 1.7 copy.42
  357.3 0.0 copy-done.5
  357.3 0.6 copy.43
  357.9 0.0 copy-done.4
  357.9 0.6 copy.44
  358.6 0.0 copy-done.3
  358.6 0.7 copy.45
  359.3 0.0 copy-done.2
  359.3 0.9 copy.46
  360.2 0.0 copy-done.1
  360.2 0.9 copy.47
  361.1 0.0 copy-done
  361.1 0.9 copy.48
Async XLA Ops:
  347.3 10.0 %copy-start.5 = (f32[48,512]{1,0:T(8,128)S(1)}, f32[48,512]{1,0:T(8,128)}, u32[]{:S(2)}) copy-start(f32[48,512]{1,0:T(8,128)} %get-tuple-element.107) | copy-start | bytes 294916
  347.3 10.6 %copy-start.4 = (f32[48,512]{1,0:T(8,128)S(1)}, f32[48,512]{1,0:T(8,128)}, u32[]{:S(2)}) copy-start(f32[48,512]{1,0:T(8,128)} %get-tuple-element.108) | copy-start | bytes 294916
  347.4 11.2 %copy-start.3 = (f32[48,1536]{1,0:T(8,128)S(1)}, f32[48,1536]{1,0:T(8,128)}, u32[]{:S(2)}) copy-start(f32[48,1536]{1,0:T(8,128)} %get-tuple-element.109) | copy-start | bytes 884740
  347.4 11.9 %copy-start.2 = (f32[2,192,512]{2,1,0:T(8,128)S(1)}, f32[2,192,512]{2,1,0:T(8,128)}, u32[]{:S(2)}) copy-start(f32[2,192,512]{2,1,0:T(8,128)} %get-tuple-element.113) | copy-start | bytes 2359300
  347.4 12.8 %copy-start.1 = (f32[2,192,512]{2,1,0:T(8,128)S(1)}, f32[2,192,512]{2,1,0:T(8,128)}, u32[]{:S(2)}) copy-start(f32[2,192,512]{2,1,0:T(8,128)} %get-tuple-element.114) | copy-start | bytes 2359300
  353.5 7.6 %copy-start = (f32[2,192,512]{2,1,0:T(8,128)S(1)}, f32[2,192,512]{2,1,0:T(8,128)}, u32[]{:S(2)}) copy-start(f32[2,192,512]{2,1,0:T(8,128)} %get-tuple-element.65) | copy-start | bytes 2359300

commit v4 on v0

v4 whole, which is shorter than its diff:
```python
import math

import jax
import jax.numpy as jnp
from jax import lax
from jax.experimental import pallas as pl
from jax.experimental.pallas import tpu as pltpu
from jax.sharding import PartitionSpec as P

epsilon = 1e-06
floor_score = -1e30
MESH = pl.DeviceIdType.MESH
BF = jnp.bfloat16
F32 = jnp.float32


def low(*shape):
    return pltpu.VMEM(shape, BF)


def high(*shape):
    return pltpu.VMEM(shape, F32)


class Place:
    def __init__(self):
        e, c = lax.axis_index("expert"), lax.axis_index("context")
        self.hi, self.core = e // 2, e % 2
        self.lo, self.y = c // 4, c % 4
        self.z = lax.axis_index("dp")

    def at(self, hi=0, core=0, lo=0, y=0, z=0):
        e = (self.hi + hi) % 2 * 2 + (self.core + core) % 2
        c = (self.lo + lo) % 2 * 4 + (self.y + y) % 4
        return (e, c, (self.z + z) % 4)

    def line(self, axis):
        if axis == "y":
            return [((self.y + d) % 4, self.at(y=d)) for d in (1, 2, 3)]
        if axis == "z":
            return [((self.z + d) % 4, self.at(z=d)) for d in (1, 2, 3)]
        return [
            ((self.hi + a) % 2 * 2 + (self.lo + b) % 2, self.at(hi=a, lo=b))
            for a, b in ((0, 1), (1, 0), (1, 1))
        ]

    def own(self, axis):
        return {"y": self.y, "z": self.z, "x": self.hi * 2 + self.lo}[axis]


def greet(devices):
    barrier = pltpu.get_barrier_semaphore()
    for device in devices:
        pl.semaphore_signal(barrier, inc=1, device_id=device, device_id_type=MESH)
    pl.semaphore_wait(barrier, len(devices))


def send(src, dst, sems, device):
    copy = pltpu.make_async_remote_copy(
        src_ref=src, dst_ref=dst, send_sem=sems[0], recv_sem=sems[1],
        device_id=device, device_id_type=MESH,
    )
    copy.start()
    return copy


def scatter_start(place, axis, src, landing, sems, begin):
    copies = []
    for d, (index, device) in enumerate(place.line(axis)):
        pair = (sems.at[0, begin + d], sems.at[1, begin + d])
        copies.append(send(src.at[index], landing.at[d], pair, device))
    return copies


def add_up(out, own, landing, lead):
    count = landing.shape[0]

    def body(i, carry):
        total = own[i].astype(F32)
        for d in range(count):
            total = total + landing[d, i].astype(F32)
        out[i] = total.astype(out.dtype)
        return carry

    lax.fori_loop(0, lead, body, 0)


def roll_lanes(u, shift):
    return pltpu.roll(u, shift, 1)


def swap_halves(u):
    lane = lax.broadcasted_iota(jnp.int32, u.shape, 1)
    return jnp.where(lane % 64 < 32, roll_lanes(u, 96), roll_lanes(u, 32))


def to_pairs(blocks):
    a, b, c = blocks
    low = lax.broadcasted_iota(jnp.int32, a.shape, 1) < 64
    return [
        jnp.where(low, a, b), jnp.where(low, roll_lanes(a, 64), roll_lanes(c, 64)), jnp.where(low, b, c)
    ]


def from_pairs(blocks):
    a, b, c = blocks
    low = lax.broadcasted_iota(jnp.int32, a.shape, 1) < 64
    turned = roll_lanes(b, 64)
    return [jnp.where(low, a, turned), jnp.where(low, c, a), jnp.where(low, turned, c)]


def inverse_root(values):
    return lax.rsqrt(jnp.mean(values * values, axis=-1, keepdims=True) + epsilon)


def visible(place, start, rows):
    key = lax.broadcasted_iota(jnp.int32, (rows, 384), 0) + start
    query = lax.broadcasted_iota(jnp.int32, (rows, 384), 1) % 128
    return key <= query + (place.lo * 4 + place.y) * 128


def half_mask(s):
    lane = lax.broadcasted_iota(jnp.int32, (1, 128), 1)
    return jnp.where((lane >= 64) == (s == 1), 1.0, 0.0).astype(BF)


def group_peers(place):
    return {
        (c, h, d): place.at(core=c, hi=h, z=d)
        for c in (0, 1) for h in (0, 1) for d in range(4) if (c, h, d) != (0, 0, 0)
    }


def group_index(place, core=0, hi=0, z=0):
    return ((place.hi + hi) % 2 * 2 + (place.core + core) % 2) * 4 + (place.z + z) % 4


class Spread:
    def __init__(self, place, held, sems):
        self.place, self.held, self.sems = place, held, sems
        self.sent, self.waits = [], {}

    def push(self, origin, device, slot, rows=None):
        block = self.held.at[group_index(self.place, hi=origin[0], z=origin[1])]
        if rows is not None:
            block = block.at[pl.ds(rows, 64)]
        pair = (self.sems.at[0, len(self.sent)], self.sems.at[1, slot])
        copy = send(block, block, pair, device)
        self.sent.append(copy)
        self.waits[slot] = copy

    def land(self, slot):
        self.waits[slot].wait_recv()

    def around(self, h):
        self.push((h, 0), self.place.at(z=1), h * 4 + 3)
        self.push((h, 0), self.place.at(z=3), h * 4 + 1)

    def first(self):
        self.push((0, 0), self.place.at(hi=1), 4)
        self.around(0)
        self.push((0, 0), self.place.at(core=1), 8)

    def relay_hi(self):
        self.land(4)
        self.around(1)
        self.push((1, 0), self.place.at(core=1), 12)

    def relay(self, h):
        sibling = self.place.at(core=1)
        self.land(h * 4 + 3)
        self.push((h, 3), self.place.at(z=1), h * 4 + 2, 0)
        self.push((h, 3), sibling, 8 + h * 4 + 3)
        self.land(h * 4 + 1)
        self.push((h, 1), self.place.at(z=3), 16 + h, 64)
        self.push((h, 1), sibling, 8 + h * 4 + 1)

    def last(self, h):
        self.land(h * 4 + 2)
        self.land(16 + h)
        self.push((h, 2), self.place.at(core=1), 8 + h * 4 + 2)

    def finish(self, h):
        for d in range(4):
            self.land(8 + h * 4 + d)

    def drain(self):
        for copy in self.sent:
            copy.wait_send()


def add_rows(out, terms):
    def body(i, carry):
        part = pl.ds(pl.multiple_of(i * 16, 16), 16)
        total = terms[0][part].astype(F32)
        for term in terms[1:]:
            total = total + term[part].astype(F32)
        out[part] = total.astype(out.dtype)
        return carry

    lax.fori_loop(0, out.shape[0] // 16, body, 0)


class Gather:
    def __init__(self, place, parts, pool, halves, wholes, sems):
        self.place, self.parts, self.pool, self.sems = place, parts, pool, sems
        self.halves, self.wholes = halves, wholes
        self.sent, self.waits = [], {}

    def push(self, src, dst, slot, device):
        copy = send(src, dst, (self.sems.at[0, slot], self.sems.at[1, slot]), device)
        self.sent.append(copy)
        self.waits[slot] = copy
        return copy

    def swap(self, hi):
        half = (self.place.hi + hi) % 2
        start = group_index(self.place, core=1, hi=hi) - self.place.z
        return self.push(
            self.parts.at[pl.ds(start, 4)], self.pool.at[pl.ds(half * 4, 4)], hi, self.place.at(core=1)
        )

    def chunk(self, hi, z):
        return self.pool.at[(self.place.hi + hi) % 2 * 4 + (self.place.z + z) % 4]

    def terms(self, hi, z):
        if self.parts is None:
            return [self.chunk(hi, z)]
        return [self.chunk(hi, z), self.parts.at[group_index(self.place, hi=hi, z=z)]]

    def join(self, hi, z, more=()):
        block = self.chunk(hi, z)
        if self.parts is not None or more:
            add_rows(block, [*self.terms(hi, z), *more])
        return block

    def first(self, h):
        block = self.join(h, 2)
        upper, lower = pl.ds(0, 64), pl.ds(64, 64)
        self.push(block.at[upper], self.halves.at[h, 0], 2 + h * 4, self.place.at(z=1))
        self.push(block.at[lower], self.halves.at[h, 1], 3 + h * 4, self.place.at(z=3))
        self.join(h, 1)
        self.join(h, 3)

    def second(self, h):
        for side, d in ((0, 1), (1, 3)):
            part = pl.ds(side * 64, 64)
            self.waits[2 + h * 4 + side].wait_recv()
            block = self.chunk(h, d)
            add_rows(block.at[part], [block.at[part], self.halves.at[h, side]])
            self.push(block, self.wholes.at[h * 2 + side], 4 + h * 4 + side, self.place.at(z=d))

    def third(self):
        for side in range(2):
            self.waits[8 + side].wait_recv()
        block = self.join(1, 0, [self.wholes.at[2], self.wholes.at[3]])
        self.push(block, self.wholes.at[4], 10, self.place.at(hi=1))

    def finish(self, out, more=()):
        for slot in (4, 5, 10):
            self.waits[slot].wait_recv()
        add_rows(out, [*more, *self.terms(0, 0)] + [self.wholes.at[i] for i in (0, 1, 4)])

    def drain(self):
        for copy in self.sent:
            copy.wait_send()


class SpreadShort:
    def __init__(self, place, held, sems):
        self.place, self.held, self.sems = place, held, sems
        self.sent, self.waits = [], {}

    def pair(self, c, h, d):
        slot = c * 8 + h * 4 + d
        return (self.sems.at[0, slot], self.sems.at[1, slot])

    def push(self, origin, target, slot):
        c, h, d = target
        index = group_index(self.place, hi=origin[0], z=origin[1])
        block = self.held.at[index]
        copy = send(block, block, self.pair(*slot), self.place.at(core=c, hi=h, z=d))
        self.sent.append(copy)
        self.waits[slot] = copy

    def land(self, slot):
        self.waits[slot].wait_recv()

    def first(self):
        for d in (1, 3, 2):
            self.push((0, 0), (0, 0, d), (0, 0, (4 - d) % 4))
        self.push((0, 0), (0, 1, 0), (0, 1, 0))
        self.push((0, 0), (1, 0, 0), (1, 0, 0))

    def relay_a(self):
        self.land((0, 1, 0))
        for d in (1, 3):
            self.push((1, 0), (0, 0, d), (0, 1, (4 - d) % 4))
        self.push((1, 0), (1, 0, 0), (1, 1, 0))

    def relay_b(self):
        self.land((0, 0, 2))
        self.push((0, 2), (0, 1, 0), (0, 1, 2))
        self.push((0, 2), (1, 0, 0), (1, 0, 2))
        for d in (1, 3):
            self.land((0, 0, d))
            self.push((0, d), (1, 0, 0), (1, 0, d))

    def finish_near(self):
        for d in range(4):
            self.land((1, 0, d))

    def relay_far(self):
        for d in (1, 3, 2):
            self.land((0, 1, d))
            self.push((1, d), (1, 0, 0), (1, 1, d))

    def finish_far(self):
        for d in range(4):
            self.land((1, 1, d))

    def drain(self):
        for copy in self.sent:
            copy.wait_send()


class GatherShort:
    def __init__(self, place, parts, pool, landing, sems):
        self.place, self.parts, self.pool, self.landing, self.sems = place, parts, pool, landing, sems
        self.sent = []

    def pair(self, slot):
        return (self.sems.at[0, slot], self.sems.at[1, slot])

    def push(self, src, dst, slot, device):
        copy = send(src, dst, self.pair(slot), device)
        self.sent.append(copy)
        return copy

    def swap(self, hi):
        half = (self.place.hi + hi) % 2
        start = group_index(self.place, core=1, hi=hi) - self.place.z
        return self.push(
            self.parts.at[pl.ds(start, 4)], self.pool.at[pl.ds(half * 4, 4)], hi, self.place.at(core=1)
        )

    def chunk(self, hi, z):
        return self.pool.at[(self.place.hi + hi) % 2 * 4 + (self.place.z + z) % 4]

    def mine(self, hi, z):
        return self.parts.at[group_index(self.place, hi=hi, z=z)]

    def join(self, hi, z, more=()):
        block = self.chunk(hi, z)
        add_rows(block, [block, self.mine(hi, z), *more])
        return block

    def near(self):
        place, land = self.place, self.landing
        self.direct = []
        for i, d in enumerate((1, 3)):
            self.direct.append(self.push(self.join(0, d), land.at[3 + i], 5 + i, place.at(z=d)))

    def first(self):
        place, land = self.place, self.landing
        self.cross = []
        for i, d in enumerate((1, 3)):
            self.cross.append(self.push(self.join(1, d), land.at[i], 2 + i, place.at(z=d)))
        self.far = self.push(self.join(1, 2), land.at[2], 4, place.at(hi=1))

    def second(self):
        place, land = self.place, self.landing
        for copy in self.cross:
            copy.wait_recv()
        block = self.join(1, 0, [land.at[0], land.at[1]])
        self.last = [self.push(block, land.at[5], 7, place.at(hi=1))]
        self.far.wait_recv()
        block = self.join(0, 2, [land.at[2]])
        self.last.append(self.push(block, land.at[6], 8, place.at(z=2)))

    def finish(self, out):
        for copy in self.direct + self.last:
            copy.wait_recv()
        land = self.landing
        add_rows(out, [self.chunk(0, 0), self.mine(0, 0), land.at[3], land.at[4], land.at[5], land.at[6]])

    def drain(self):
        for copy in self.sent:
            copy.wait_send()


class Columns:
    def __init__(self, place, own, held, sems, own_sem):
        self.place, self.own, self.held, self.sems = place, own, held, sems
        self.sent, self.waits = [], {}
        self.local = pltpu.make_async_copy(own, held.at[0, self.context()], own_sem)
        self.local.start()

    def context(self, lo=0, y=0):
        return (self.place.lo + lo) % 2 * 4 + (self.place.y + y) % 4

    def push(self, src, side, lo, y, device, slot):
        pair = (self.sems.at[0, len(self.sent)], self.sems.at[1, slot])
        copy = send(src, self.held.at[side, self.context(lo, y)], pair, device)
        self.sent.append(copy)
        self.waits[slot] = copy

    def first(self):
        place = self.place
        self.push(self.own, 0, 0, 0, place.at(lo=1), 4)
        for d in (1, 3, 2):
            self.push(self.own, 0, 0, 0, place.at(y=d), (4 - d) % 4)
        self.push(self.own, 1, 0, 0, place.at(core=1), 8)

    def cross(self, lo, y):
        self.waits[lo * 4 + y].wait_recv()
        block = self.held.at[0, self.context(lo, y)]
        self.push(block, 1, lo, y, self.place.at(core=1), 8 + lo * 4 + y)
        return block

    def second(self):
        block = self.cross(1, 0)
        for d in (1, 3, 2):
            self.push(block, 0, 1, 0, self.place.at(y=d), 4 + (4 - d) % 4)
        for d in (1, 3, 2):
            self.cross(0, d)

    def third(self):
        for d in (1, 3, 2):
            self.cross(1, d)

    def finish(self):
        for slot in range(8):
            self.waits[8 + slot].wait_recv()
        self.local.wait()
        for copy in self.sent:
            copy.wait_send()


def contract(left, right, dims):
    return lax.dot_general(left, right, (dims, ((), ())), preferred_element_type=F32)


STREAMS = {
    "o1": ("zxy", 256, 0), "o2": ("zyx", 256, 256), "q1": ("zxy", 256, 512),
    "q2": ("yxz", 128, 768), "s1": ("xzy", 128, 896), "s2": ("zyx", 128, 1024),
}
ALL_WIDE = 1152


def stream_index(order, block, half):
    at = {"x": half * 2 + block // 16, "y": block // 4 % 4, "z": block % 4}
    return tuple(at[axis] for axis in order)


class Streams:
    def __init__(self, place, buffers, sems, mine):
        self.place, self.buffers, self.sems, self.mine = place, buffers, sems, mine
        self.flight, self.sent = {}, []

    def put(self, name, tile, half, grads, begin=0):
        order = STREAMS[name][0]
        width = grads.shape[1]
        for j in range(8):
            index = stream_index(order, tile * 8 + j, half)
            self.buffers[name][0][(*index, slice(None), slice(begin, begin + width))] = (
                grads[j * 48 : (j + 1) * 48]
            )

    def source(self, name, phase):
        return self.buffers[name][2 * phase]

    def launch(self, name, phase):
        begin = list(STREAMS).index(name) * 9 + 3 * phase
        copies = scatter_start(
            self.place, STREAMS[name][0][phase], self.source(name, phase),
            self.buffers[name][2 * phase + 1], self.sems, begin,
        )
        self.flight[name] = copies
        self.sent.extend(copies)

    def land(self, name, phase):
        for copy in self.flight[name]:
            copy.wait_recv()
        order, width, begin = STREAMS[name]
        own = self.source(name, phase).at[self.place.own(order[phase])]
        landing = self.buffers[name][2 * phase + 1]
        if phase == 2:
            total = own[...].astype(F32)
            for d in range(3):
                total = total + landing[d].astype(F32)
            self.mine[:, begin : begin + width] = total.astype(BF)
            return
        out = self.source(name, phase + 1)
        if phase == 1:
            add_up(out, own, landing, 4)
            return

        def body(i, carry):
            a, b = i // 4, i % 4
            total = own[a, b].astype(F32)
            for d in range(3):
                total = total + landing[d, a, b].astype(F32)
            out[a, b] = total.astype(BF)
            return carry

        lax.fori_loop(0, 16, body, 0)

    def step(self, name, phase):
        self.land(name, phase)
        if phase < 2:
            self.launch(name, phase + 1)


def layer_kernel(
    x_far, ids, cot_far, gain_attn, gain_moe, wr, wq, wk, wv, wo, wg_far, wu_far, wd_far,
    mixed_far, gt_far, quarters, experts_far, eg, eu, ed, far_p, far_q, n1t_all,
    kv, qp, lse, attn, y1, n2, gates, turn, dn2r, dgate, eo_pool, home_halves, home_wholes,
    ready, weight_sems, expert_load_sems, own_sem, cots_sems, k_sems, v_sems,
    table_sems, rows_sems, gather_sems, dgate_sems, stage_sems, eo_sems, column_sems, column_sem, far_sems,
    column_load_sems, pair_sems, kv_sems, dense_sems, quarter_sems, home_sems, fold_sems, expert_sems,
    out_sems,
):
    def early(cots, rows, tables, table, pool, landing, n1t, wg, wu, wd):
        expert_loads = [
            pltpu.make_async_copy(far, near, expert_load_sems.at[i])
            for i, (far, near) in enumerate(((wg_far, wg), (wu_far, wu), (wd_far, wd)))
        ]

        def forward(n1, x_ref, wqv, wkv, wov):
            place = Place()
            me = group_index(place)
            context = place.lo * 4 + place.y
            own_copy = pltpu.make_async_copy(cot_far, cots.at[me], own_sem)
            own_copy.start()
            loads = [
                pltpu.make_async_copy(x_far, x_ref, weight_sems.at[4]),
                pltpu.make_async_copy(wk, wkv.at[:, 0:512], weight_sems.at[0]),
                pltpu.make_async_copy(wv, wkv.at[:, 512:1024], weight_sems.at[1]),
                pltpu.make_async_copy(wq, wqv, weight_sems.at[2]),
                pltpu.make_async_copy(wo, wov, weight_sems.at[3]),
            ]
            for load in loads:
                load.start()
            for load in expert_loads:
                load.start()
            greet(
                list(group_peers(place).values())
                + [place.at(y=d) for d in (1, 2, 3)] + [place.at(lo=1), place.at(hi=1, lo=1)]
            )
            lo_peer = place.at(lo=1)
            spread = Spread(place, cots, cots_sems)
            own_copy.wait()
            spread.first()
            loads.pop(0).wait()
            x = x_ref[...].astype(F32)
            n1[...] = (x * inverse_root(x) * gain_attn[...].reshape(1, 1536)).astype(BF)
            lane = lax.broadcasted_iota(jnp.int32, (128, 128), 1)
            row = lax.broadcasted_iota(jnp.int32, (128, 128), 0)
            freqs = jnp.exp((lane % 32).astype(F32) * (-math.log(10000.0) / 32))
            angles = (row + context * 128).astype(F32) * freqs
            cosine = jnp.cos(angles)
            sine = jnp.where(lane % 64 < 32, -1.0, 1.0) * jnp.sin(angles)
            turn[0] = cosine
            turn[1] = sine

            loads[0].wait()
            loads[1].wait()
            for j in range(4):
                raw = contract(n1[...], wkv[:, j * 128 : (j + 1) * 128], ((1,), (0,)))
                kv[0, context, :, j * 128 : (j + 1) * 128] = (raw * cosine + swap_halves(raw) * sine).astype(BF)
            kv[1, context] = contract(n1[...], wkv[:, 512:1024], ((1,), (0,))).astype(BF)

            sent = []
            waits = {}

            def push(which, lo, y, device, slot):
                block = kv.at[which, (place.lo + lo) % 2 * 4 + (place.y + y) % 4]
                sems = (k_sems, v_sems)[which]
                copy = send(block, block, (sems.at[0, slot], sems.at[1, slot]), device)
                sent.append(copy)
                waits[which, slot] = copy

            for which in (0, 1):
                push(which, 0, 0, lo_peer, 4)
                for d in (1, 3, 2):
                    push(which, 0, 0, place.at(y=d), (4 - d) % 4)

            loads[2].wait()
            for j in range(4):
                raw = contract(n1[...], wqv[:, j * 384 : (j + 1) * 384], ((1,), (0,)))
                turned = []
                for r in range(3):
                    block = raw[:, r * 128 : (r + 1) * 128]
                    turned.append((block * cosine + swap_halves(block) * sine) * 0.125)
                for r, block in enumerate(to_pairs(turned)):
                    qp[j, r * 128 : (r + 1) * 128, :] = block.astype(BF)
            waits[0, 4].wait_recv()
            for d in (1, 3, 2):
                push(0, 1, 0, place.at(y=d), 4 + (4 - d) % 4)
            spread.relay_hi()
            for d in (1, 3, 2):
                waits[1, d].wait_recv()
                push(1, 0, d, lo_peer, 4 + d)

            spread.relay(0)
            for j in range(12):
                part = slice(j * 128, (j + 1) * 128)
                n1t[part, :] = n1[:, part].astype(F32).T.astype(BF)

            picked = jnp.zeros((128, 128), F32)
            for k in range(8):
                picked = picked + jnp.where(ids[k : k + 1, :] == row, 1.0, 0.0)
            chosen = picked.T
            earlier = jnp.where(lane < row, 1.0, 0.0).astype(BF)
            before = contract(earlier, chosen.astype(BF), ((1,), (0,)))
            slots = jnp.where(chosen > 0.0, before, -1.0).T
            table[...] = jnp.zeros_like(table)
            for g in range(16):
                table[g, 0:2, :] = slots[2 * g : 2 * g + 2, :]

            for d in (1, 3, 2):
                waits[0, d].wait_recv()
                waits[0, 4 + d].wait_recv()
                waits[1, 4 + d].wait_recv()
            waits[1, 4].wait_recv()
            spread.relay(1)

            def attend(j, carry):
                lanes = pl.ds(pl.multiple_of(j * 128, 128), 128)
                keys = kv[0, :, :, lanes].reshape(1024, 128)
                values = kv[1, :, :, lanes].reshape(1024, 128)
                halves = []
                for s in range(2):
                    scores = contract(keys, qp[j] * half_mask(s), ((1,), (1,)))
                    scores = jnp.where(visible(place, 0, 1024), scores, floor_score)
                    top = jnp.max(scores, axis=0, keepdims=True)
                    probs = jnp.exp(scores - top)
                    total = jnp.sum(probs, axis=0, keepdims=True)
                    lse[j * 2 + s] = top + jnp.log(total)
                    out = contract(values, probs.astype(BF), ((0,), (0,))) * (1.0 / total)
                    halves.append(out[s * 64 : (s + 1) * 64])
                joined = jnp.concatenate(halves, axis=0).T
                for r, block in enumerate(from_pairs([joined[r * 128 : (r + 1) * 128] for r in range(3)])):
                    attn[:, pl.ds(pl.multiple_of(j * 384 + r * 128, 128), 128)] = block.astype(BF)
                return carry

            lax.fori_loop(0, 4, attend, 0)
            spread.last(0)

            loads[3].wait()
            for j in range(4):
                part = slice(j * 384, (j + 1) * 384)
                y1[:, part] = x_ref[:, part].astype(F32) + contract(attn[...], wov[:, part], ((1,), (0,)))
            y = y1[...]
            n2[...] = (y * inverse_root(y) * gain_moe[...].reshape(1, 1536)).astype(BF)
            logits = jnp.concatenate(
                [contract(n2[...], wr[...], ((1,), (1,))), jnp.zeros((128, 96), F32)], axis=1
            )
            logits = jnp.where(chosen > 0.0, logits, -jnp.inf)
            weights = jnp.exp(logits - jnp.max(logits, axis=1, keepdims=True))
            weights = weights / jnp.sum(weights, axis=1, keepdims=True)
            gates[...] = weights
            turned = weights.T
            for g in range(16):
                table[g, 2:4, :] = turned[2 * g : 2 * g + 2, :]
            spread.last(1)
            spread.finish(0)
            spread.finish(1)
            spread.drain()
            for copy in sent:
                copy.wait_send()

        def experts(
            x_rows, c_rows, pick, gate, dg, dhg, dhu, gact, drow, back, dgate_out,
        ):
            place = Place()
            peers = group_peers(place)
            me = group_index(place)
            y_line, lo_device = place.line("y"), place.at(lo=1)

            small = []
            tables[me] = table[me]
            for (c, h, d), device in peers.items():
                slot = c * 8 + h * 4 + d
                pair = (table_sems.at[0, slot], table_sems.at[1, c * 8 + h * 4 + (4 - d) % 4])
                small.append(send(table.at[group_index(place, c, h, d)], tables.at[me], pair, device))
            rows[me] = n2[...]
            spread_rows = SpreadShort(place, rows, rows_sems)
            spread_rows.first()
            columns = Columns(place, n1t, n1t_all, column_sems, column_sem)
            columns.first()
            for copy in small:
                copy.wait_recv()

            slots = lax.broadcasted_iota(jnp.int32, (80, 256), 0).astype(F32)
            second = lax.broadcasted_iota(jnp.int32, (1, 256), 1) >= 128

            def select(pair_index):
                parts = []
                for e in range(2):
                    here = jnp.concatenate(
                        [tables[pair_index * 2, e : e + 1, :], tables[pair_index * 2 + 1, e : e + 1, :]], axis=1
                    )
                    here = jnp.where(here < 0.0, -1000.0, here + jnp.where(second, 40.0, 0.0))
                    weight = jnp.concatenate(
                        [tables[pair_index * 2, 2 + e : 3 + e, :], tables[pair_index * 2 + 1, 2 + e : 3 + e, :]],
                        axis=1,
                    )
                    hit = slots == here
                    parts.append(jnp.where(hit, 1.0, 0.0).astype(BF))
                    place_rows = pl.ds(pl.multiple_of(pair_index * 80, 80), 80)
                    gate[e, place_rows, :] = jnp.sum(jnp.where(hit, weight, 0.0), axis=1, keepdims=True)
                pick[pair_index] = jnp.concatenate(parts, axis=0)

            def pull(pair_index, held, out):
                both = jnp.concatenate([held[pair_index * 2], held[pair_index * 2 + 1]], axis=0)
                picked = contract(pick[pair_index], both, ((1,), (0,))).astype(BF)
                place_rows = pl.ds(pl.multiple_of(pair_index * 80, 80), 80)
                out[0, place_rows, :] = picked[0:80]
                out[1, place_rows, :] = picked[80:160]

            def all_pairs(body):
                def step(i, carry):
                    body(i)
                    return carry
                lax.fori_loop(0, 8, step, 0)

            def side_pairs(c, h, body):
                base = (group_index(place, core=c, hi=h) - place.z) // 2

                def step(i, carry):
                    body(base + i)
                    return carry

                lax.fori_loop(0, 2, step, 0)

            all_pairs(select)
            all_pairs(lambda p: pull(p, cots, c_rows))
            expert_loads[2].wait()

            def back_rows(i, carry):
                e, m = i // 2, i % 2
                part = pl.ds(pl.multiple_of(m * 320, 320), 320)
                back[e, part, :] = contract(c_rows[e, part, :], wd[e], ((1,), (1,)))
                return carry

            lax.fori_loop(0, 4, back_rows, 0)

            def work(h):
                m = (place.hi + h) % 2
                part = pl.ds(pl.multiple_of(m * 320, 320), 320)

                def step(e, carry):
                    x = x_rows[e, part, :]
                    hg = contract(x, wg[e].reshape(1536, 512), ((1,), (0,)))
                    hu = contract(x, wu[e], ((1,), (0,)))
                    turned = back[e, part, :]
                    weight = gate[e, part, :]
                    sig = 1.0 / (1.0 + jnp.exp(-hg))
                    silu = hg * sig
                    act = silu * hu
                    dg[e, part, :] = jnp.sum(act * turned, axis=1, keepdims=True)
                    gact[e, part, :] = (weight * act).astype(BF)
                    dact = weight * turned
                    low_hg = (dact * hu * (sig + silu * (1.0 - sig))).astype(BF)
                    low_hu = (dact * silu).astype(BF)
                    dhg[e, part, :] = low_hg
                    dhu[e, part, :] = low_hu
                    made = (
                        contract(low_hg, wg[e].reshape(1536, 512), ((1,), (1,))) + contract(low_hu, wu[e], ((1,), (1,)))
                    ).astype(BF)
                    for j in range(4):
                        drow[m * 4 + j, pl.ds(pl.multiple_of(e * 80, 80), 80), :] = made[j * 80 : (j + 1) * 80]
                    return carry

                lax.fori_loop(0, 2, step, 0)

            def put_back(pair_index, out):
                both = contract(pick[pair_index], drow[pair_index], ((0,), (0,))).astype(BF)
                out[pair_index * 2] = both[0:128]
                out[pair_index * 2 + 1] = both[128:256]

            def gate_grads(pair_index):
                chosen = pick[pair_index].astype(F32)
                for e in range(2):
                    column = dg[e, pl.ds(pl.multiple_of(pair_index * 80, 80), 80), :]
                    line = jnp.sum(chosen[e * 80 : (e + 1) * 80] * column, axis=0, keepdims=True)
                    dgate_out[pair_index * 2, e : e + 1, :] = line[:, 0:128]
                    dgate_out[pair_index * 2 + 1, e : e + 1, :] = line[:, 128:256]

            home = GatherShort(place, cots, pool, landing, gather_sems)
            spread_rows.relay_a()
            spread_rows.relay_b()
            spread_rows.finish_near()
            side_pairs(0, 0, lambda p: pull(p, rows, x_rows))
            side_pairs(1, 0, lambda p: pull(p, rows, x_rows))
            expert_loads[0].wait()
            expert_loads[1].wait()
            work(0)
            side_pairs(1, 0, lambda p: put_back(p, cots))
            near_swap = home.swap(0)
            spread_rows.relay_far()
            side_pairs(0, 0, lambda p: put_back(p, cots))
            columns.second()
            spread_rows.finish_far()
            side_pairs(0, 1, lambda p: pull(p, rows, x_rows))
            side_pairs(1, 1, lambda p: pull(p, rows, x_rows))
            near_swap.wait_recv()
            home.near()
            work(1)
            side_pairs(1, 1, lambda p: put_back(p, cots))
            far_swap = home.swap(1)
            side_pairs(0, 1, lambda p: put_back(p, cots))
            dgate_out[...] = jnp.zeros_like(dgate_out)
            all_pairs(gate_grads)
            small_back = []
            dgate[me] = dgate_out[me]
            for (c, h, d), device in peers.items():
                slot = c * 8 + h * 4 + d
                pair = (dgate_sems.at[0, slot], dgate_sems.at[1, c * 8 + h * 4 + (4 - d) % 4])
                small_back.append(send(dgate_out.at[group_index(place, c, h, d)], dgate.at[me], pair, device))
            far_swap.wait_recv()
            home.first()
            spread_rows.drain()
            columns.third()

            def outputs(i, carry):
                e, m = i // 2, i % 2
                part = pl.ds(pl.multiple_of(m * 320, 320), 320)
                made = contract(gact[e, part, :], wd[e], ((1,), (0,))).astype(BF)
                for j in range(4):
                    drow[m * 4 + j, pl.ds(pl.multiple_of(e * 80, 80), 80), :] = made[j * 80 : (j + 1) * 80]
                return carry

            lax.fori_loop(0, 4, outputs, 0)
            home.second()
            all_pairs(lambda p: put_back(p, rows))
            outward = Gather(place, rows, eo_pool, None, None, eo_sems)
            out_swaps = [outward.swap(0), outward.swap(1)]
            copies, far = {}, []
            other_lo = (place.lo + 1) % 2
            order = [
                (e, left, right, out, m)
                for left, right, out, m in ((x_rows, dhg, eg, 0), (x_rows, dhu, eu, 1), (c_rows, gact, ed, 2))
                for e in range(2)
            ]

            def forward(step):
                copies[step].wait()
                e, _, _, out, m = order[step]
                if e == 0:
                    for d, (index, device) in enumerate(y_line):
                        pair = (far_sems.at[0, m * 4 + d], far_sems.at[1, m * 4 + d])
                        far.append(send(out.at[0, :, index], far_p.at[d, m], pair, device))
                else:
                    pair = (far_sems.at[0, m * 4 + 3], far_sems.at[1, m * 4 + 3])
                    far.append(send(out.at[1, other_lo], far_q.at[m], pair, lo_device))

            for step, (e, left, right, out, m) in enumerate(order):
                slot = step % 2
                if step >= 2:
                    forward(step - 2)

                def weight_grad(i, carry):
                    tile = pl.ds(pl.multiple_of(i * 384, 128), 384)
                    grads = contract(left[e, :, tile], right[e], ((0,), (0,))).astype(BF)
                    wg[slot, i // 2, pl.ds(i % 2 * 2, 2)] = grads.reshape(2, 192, 512)
                    return carry

                lax.fori_loop(0, 4, weight_grad, 0)
                copies[step] = pltpu.make_async_copy(wg.at[slot], out.at[e], stage_sems.at[slot])
                copies[step].start()
            forward(4)
            forward(5)
            for copy in out_swaps:
                copy.wait_recv()
            for h in range(2):
                for d in range(4):
                    outward.join(h, d)
            home.finish(dn2r)
            for copy in small_back:
                copy.wait_recv()
            for copy in small + small_back:
                copy.wait_send()
            home.drain()
            outward.drain()
            columns.finish()

        pl.run_scoped(
            forward, low(128, 1536), low(128, 1536), low(1536, 1536), low(1536, 1024), low(1536, 1536)
        )
        pl.run_scoped(
            experts, low(2, 640, 1536), low(2, 640, 1536), low(8, 160, 256),
            high(2, 640, 1), high(2, 640, 1), low(2, 640, 512), low(2, 640, 512), low(2, 640, 512),
            low(8, 160, 1536), high(2, 640, 512), high(16, 8, 128),
        )

    def late(
        x_ref, cot, big, w_v, attnc, dqc, dbrc, dkvs, dgt, dbr, dap, delta, dq, dk, dy1, dkv,
        land_a, land_b, land_c, land_d, mine, stage, sum_p, sum_q, land_p2, land_q2, experts, mixed, gt, *rest,
    ):
        buffers = {name: rest[i * 6 : i * 6 + 6] for i, name in enumerate(STREAMS)}
        place = Place()
        context = place.lo * 4 + place.y
        y_line, z_line, x_line = (place.line(axis) for axis in "yzx")
        sibling, cross, lo_device = place.at(core=1), place.at(hi=1, core=1), place.at(lo=1)
        other_lo = (place.lo + 1) % 2
        load_o = pltpu.make_async_copy(wo, big.at[:, 0:1536], weight_sems.at[0])
        load_o.start()
        load_v = pltpu.make_async_copy(wv, w_v, weight_sems.at[1])
        load_v.start()
        load_x = pltpu.make_async_copy(x_far, x_ref, weight_sems.at[3])
        load_x.start()
        load_cot = pltpu.make_async_copy(cot_far, cot, weight_sems.at[4])
        load_cot.start()
        others = [device for line in (y_line, z_line, x_line) for _, device in line] + [sibling, cross]
        for device in others:
            pl.semaphore_signal(ready, inc=1, device_id=device, device_id_type=MESH)
        pl.semaphore_wait(ready, len(others))
        pending = []

        def share(i, source, both):
            pair = (pair_sems.at[0, i], pair_sems.at[1, i])
            copy = send(source, both, pair, sibling)
            pending.append(copy)
            return copy

        lower = pl.ds(128, 128)
        share_attn = share(0, attn, attnc.at[lower])
        attnc[0:128, :] = attn[...]

        home = Gather(place, None, eo_pool, home_halves, home_wholes, home_sems)
        home.first(1)
        home.first(0)

        dgt[...] = jnp.zeros_like(dgt)
        for g in range(16):
            dgt[2 * g : 2 * g + 2, :] = dgate[g, 0:2, :]
        weights = gates[...]
        dgates = dgt[...].T
        dlogits = weights * (dgates - jnp.sum(weights * dgates, axis=1, keepdims=True))
        dlogits = dlogits.astype(BF)
        dn2 = dn2r[...] + contract(dlogits[:, 0:32], wr[...], ((1,), (0,)))
        y = y1[...]
        root = inverse_root(y)
        scaled = dn2 * gain_moe[...].reshape(1, 1536)
        inner = jnp.mean(scaled * y, axis=-1, keepdims=True)
        load_cot.wait()
        dy = cot[...].astype(F32) + root * scaled - y * (root * root * root * inner)
        dy1[...] = dy
        low = dy.astype(BF)
        dbr[0] = low[:, 0:768]
        dbr[1] = low[:, 768:1536]
        share_dbr = share(1, dbr.at[1 - place.core], dbrc.at[lower])
        dbrc[0:128, :] = dbr[place.core]

        load_o.wait()
        for j in range(4):
            back = contract(low, big[j * 384 : (j + 1) * 384, 0:1536], ((1,), (1,)))
            grads = to_pairs([back[:, r * 128 : (r + 1) * 128] for r in range(3)])
            outs = to_pairs(
                [attn[:, j * 384 + r * 128 : j * 384 + (r + 1) * 128].astype(F32) for r in range(3)]
            )
            grads = jnp.concatenate(grads, axis=0).astype(BF)
            dap[j] = grads
            product = (grads.astype(F32) * jnp.concatenate(outs, axis=0)).T
            for s in range(2):
                delta[j * 2 + s] = jnp.sum(product[s * 64 : (s + 1) * 64], axis=0, keepdims=True)
        load_columns = []
        for side in range(2):
            for c in range(8):
                at = side * 8 + c
                load_columns.append(
                    pltpu.make_async_copy(
                        n1t_all.at[side, c], big.at[:, at * 128 : (at + 1) * 128], column_load_sems.at[at]
                    )
                )
                load_columns[-1].start()

        home.second(1)
        home.second(0)
        streams = Streams(place, buffers, dense_sems, mine)
        gain_rows = (dn2 * y * root).astype(BF)
        column = jnp.where(lax.broadcasted_iota(jnp.int32, (128, 128), 1) == 32, 1.0, 0.0).astype(BF)
        narrow_left = jnp.concatenate([n2[...], gain_rows], axis=0)
        narrow_right = jnp.concatenate([dlogits, column], axis=0)
        for tile in range(4):
            part = contract(
                narrow_left[:, tile * 384 : (tile + 1) * 384], narrow_right, ((0,), (0,))
            ).astype(BF)
            for half in range(2):
                streams.put("o2", tile, half, part, 128)
        share_attn.wait_recv()
        share_dbr.wait_recv()
        for tile in range(4):
            for half in range(2):
                grads = contract(
                    attnc[:, tile * 384 : (tile + 1) * 384], dbrc[:, half * 384 : (half + 1) * 384],
                    ((0,), (0,)),
                ).astype(BF)
                streams.put("o1", tile, half, grads[:, 0:256])
                streams.put("o2", tile, half, grads[:, 256:384])
        streams.launch("o1", 0)
        streams.launch("o2", 0)

        cosine, sine = turn[0], turn[1]
        lane = lax.broadcasted_iota(jnp.int32, (1, 128), 1)
        freqs = jnp.exp((lane % 32).astype(F32) * (-math.log(10000.0) / 32))
        sign = jnp.where(lane % 64 < 32, -1.0, 1.0)

        def turn_back(u, cos, sin):
            return u * cos - swap_halves(u) * sin

        def attend(j, carry):
            lanes = pl.ds(pl.multiple_of(j * 128, 128), 128)
            turned = [jnp.zeros((128, 384), F32) for _ in range(2)]
            for block in range(2):
                part = slice(block * 4, (block + 1) * 4)
                keys = kv[0, part, :, lanes].reshape(512, 128)
                values = kv[1, part, :, lanes].reshape(512, 128)
                grad_keys = jnp.zeros((512, 128), F32)
                grad_values = jnp.zeros((512, 128), F32)
                seen = visible(place, block * 512, 512)
                for s in range(2):
                    queries = qp[j] * half_mask(s)
                    grads = dap[j] * half_mask(s)
                    scores = contract(keys, queries, ((1,), (1,)))
                    probs = jnp.exp(jnp.where(seen, scores, floor_score) - lse[j * 2 + s])
                    back = contract(values, grads, ((1,), (1,)))
                    grad_scores = (probs * (back - delta[j * 2 + s])).astype(BF)
                    grad_values = grad_values + contract(probs.astype(BF), grads, ((1,), (0,)))
                    grad_keys = grad_keys + contract(grad_scores, queries, ((1,), (0,)))
                    turned[s] = turned[s] + contract(keys, grad_scores, ((0,), (0,)))
                dkv[part, j, 1] = grad_values.astype(BF).reshape(4, 128, 128)
                for b in range(4):
                    shift = ((block * 4 + b - context) * 128).astype(F32) * freqs
                    cos, sin = jnp.cos(shift), sign * jnp.sin(shift)
                    raw = turn_back(
                        grad_keys[b * 128 : (b + 1) * 128],
                        cosine * cos - sine * sin, sine * cos + cosine * sin,
                    )
                    dkv[block * 4 + b, j, 0] = raw.astype(BF)
            joined = jnp.concatenate([turned[0][0:64], turned[1][64:128]], axis=0).T * 0.125
            blocks = from_pairs([joined[r * 128 : (r + 1) * 128] for r in range(3)])
            for r, part in enumerate(blocks):
                lanes = pl.ds(pl.multiple_of((j % 2) * 384 + r * 128, 128), 128)
                dq[j // 2, :, lanes] = turn_back(part, cosine, sine).astype(BF)
            return carry

        def attend_core(core):
            def step(i, carry):
                return attend(core * 2 + i, carry)

            lax.fori_loop(0, 2, step, 0)

        kv_sent = []

        def kv_push(src, dst, slot, device):
            copy = send(src, dst, (kv_sems.at[0, slot], kv_sems.at[1, slot]), device)
            kv_sent.append(copy)
            return copy

        def kv_add(out, count, terms):
            def body(i, carry):
                a, b, c = i // 4, i // 2 % 2, i % 2
                block = out(a)
                total = block[b, c].astype(F32)
                for term in terms:
                    total = total + term(a)[b, c].astype(F32)
                block[b, c] = total.astype(BF)
                return carry

            lax.fori_loop(0, count * 4, body, 0)

        other = 1 - place.core
        first, later = pl.ds(other * 2, 2), pl.ds(place.core * 2, 2)
        attend_core(other)
        share_dq = share(2, dq.at[other], dqc.at[lower])
        share_dkv = share(3, dkv.at[:, first], dkvs)
        lead = kv_push(dkv.at[pl.ds(other_lo * 4, 4), first], land_a, 0, lo_device)
        streams.step("o1", 0)
        streams.step("o2", 0)
        attend_core(place.core)
        dqc[0:128, :] = dq[place.core]
        share_dq.wait_recv()
        for load in load_columns:
            load.wait()
        own_lanes = pl.ds(pl.multiple_of(context * 128, 128), 128)
        their_lanes = pl.ds(pl.multiple_of(1024 + context * 128, 128), 128)
        for tile in range(4):
            rows = slice(tile * 384, (tile + 1) * 384)
            left = jnp.concatenate([big[rows, own_lanes], big[rows, their_lanes]], axis=1)
            for half in range(2):
                grads = contract(left, dqc[:, half * 384 : (half + 1) * 384], ((1,), (0,))).astype(BF)
                streams.put("q1", tile, half, grads[:, 0:256])
                streams.put("q2", tile, half, grads[:, 256:384])
        streams.launch("q1", 0)
        streams.launch("q2", 0)
        share_dkv.wait_recv()
        own_right = jnp.concatenate(
            [dkv[:, place.core * 2 + h, which].reshape(1024, 128) for h in range(2) for which in range(2)],
            axis=1,
        )
        their_right = jnp.concatenate(
            [dkvs[:, h, which].reshape(1024, 128) for h in range(2) for which in range(2)], axis=1
        )
        for tile in range(4):
            rows = slice(tile * 384, (tile + 1) * 384)
            grads = contract(big[rows, 0:1024], own_right, ((1,), (0,))) + contract(
                big[rows, 1024:2048], their_right, ((1,), (0,))
            )
            grads = grads.astype(BF)
            for half in range(2):
                streams.put("s1", tile, half, grads[:, half * 256 : half * 256 + 128])
                streams.put("s2", tile, half, grads[:, half * 256 + 128 : half * 256 + 256])
        streams.launch("s1", 0)
        streams.launch("s2", 0)
        load_q = pltpu.make_async_copy(wq, big.at[:, 0:1536], weight_sems.at[0])
        load_k = pltpu.make_async_copy(wk, big.at[:, 1536:2048], weight_sems.at[2])
        load_q.start()
        load_k.start()

        legs = []
        for d, (index, device) in enumerate(y_line):
            for lo in range(2):
                legs.append(
                    kv_push(dkv.at[lo * 4 + index, later], land_c.at[d, lo], 4 + d * 2 + lo, device)
                )
        lead.wait_recv()
        share_dkv.wait_send()
        pending.pop()
        kv_add(lambda a: dkv.at[place.lo * 4 + a, first], 4, [lambda a: land_a.at[a]])
        legs_b = [
            kv_push(dkv.at[place.lo * 4 + index, first], land_b.at[d], 1 + d, device)
            for d, (index, device) in enumerate(y_line)
        ]
        home.third()

        mats = (eg, eu, ed)
        second = []

        def fold_expert(m):
            mat = mats[m]
            arrived = [far_p.at[0, 0]] * 3 + [far_q.at[0]]
            for i, block in enumerate(arrived):
                sems = (far_sems.at[0, m * 4 + i], far_sems.at[1, m * 4 + i])
                copy = pltpu.make_async_remote_copy(
                    src_ref=block, dst_ref=block, send_sem=sems[0], recv_sem=sems[1],
                    device_id=sibling, device_id_type=MESH,
                )
                copy.wait()
            steps = []
            for lo in range(2):
                terms = [mat.at[0, lo, place.y]]
                for d in range(3):
                    terms.append(far_p.at[d, m, lo])
                steps.append((terms, sum_p.at[lo, m]))
            for y_at in range(4):
                steps.append(([mat.at[1, place.lo, y_at], far_q.at[m, y_at]], sum_q.at[y_at, m]))

            def fetch(step):
                loads = []
                for i, term in enumerate(steps[step][0]):
                    loads.append(
                        pltpu.make_async_copy(term, stage.at[step % 2, i], fold_sems.at[step % 2, i])
                    )
                    loads[-1].start()
                return loads

            ready = fetch(0)
            for step, (terms, out) in enumerate(steps):
                following = fetch(step + 1) if step + 1 < len(steps) else None
                for load in ready:
                    load.wait()

                def fold(i, carry):
                    part = pl.ds(pl.multiple_of(i * 48, 16), 48)
                    total = stage[step % 2, 0, part].astype(F32)
                    for term in range(1, len(terms)):
                        total = total + stage[step % 2, term, part].astype(F32)
                    out[part] = total.astype(BF)
                    return carry

                lax.fori_loop(0, 4, fold, 0)
                ready = following
            pair = (expert_sems.at[0, 4 + m * 4], expert_sems.at[1, 4 + m * 4])
            second.append(send(sum_p.at[other_lo, m], land_p2.at[m], pair, lo_device))
            for d, (index, device) in enumerate(y_line):
                pair = (expert_sems.at[0, 5 + m * 4 + d], expert_sems.at[1, 5 + m * 4 + d])
                second.append(send(sum_q.at[index, m], land_q2.at[d, m], pair, device))

        fold_expert(0)
        fold_expert(1)
        streams.step("o1", 1)
        streams.step("o2", 1)
        streams.step("q2", 0)
        streams.step("s1", 0)
        streams.step("s2", 0)
        streams.step("q1", 0)
        for copy in legs:
            copy.wait_recv()
        kv_add(
            lambda a: dkv.at[a * 4 + place.y, later], 2,
            [lambda a, d=d: land_c.at[d, a] for d in range(3)],
        )
        leg_d = kv_push(dkv.at[other_lo * 4 + place.y, later], land_d, 10, lo_device)
        streams.step("q2", 1)
        streams.step("s1", 1)
        streams.step("s2", 1)
        streams.step("q1", 1)
        for name in STREAMS:
            streams.land(name, 2)
        own_quarter = place.core * 2 + place.hi
        gathered = []
        for i, (a, b) in enumerate(((0, 1), (1, 0), (1, 1))):
            pair = (quarter_sems.at[0, i], quarter_sems.at[1, i])
            gathered.append(send(mine, quarters.at[own_quarter], pair, place.at(hi=a, core=b)))
        own_quarters = pltpu.make_async_copy(mine, quarters.at[own_quarter], weight_sems.at[5])
        own_quarters.start()

        for copy in legs_b:
            copy.wait_recv()

        def key_grads(core, terms):
            for i in range(2):
                for which in range(2):
                    total = dkv[context, core * 2 + i, which].astype(F32)
                    for term in terms:
                        total = total + term(i, which).astype(F32)
                    lanes = pl.ds(pl.multiple_of((which * 4 + core * 2 + i) * 128, 128), 128)
                    dk[:, lanes] = total.astype(BF)

        key_grads(other, [lambda i, w, d=d: land_b[d, i, w] for d in range(3)])
        leg_d.wait_recv()
        key_grads(place.core, [lambda i, w: land_d[i, w]])
        load_q.wait()
        load_k.wait()
        load_v.wait()
        load_x.wait()
        x = x_ref[...].astype(F32)
        root = inverse_root(x)
        queries = jnp.concatenate([dq[0], dq[1]], axis=1)
        for j in range(4):
            part = slice(j * 384, (j + 1) * 384)
            gt[:, part] = (
                contract(queries, big[part, 0:1536], ((1,), (1,)))
                + contract(dk[:, 0:512], big[part, 1536:2048], ((1,), (1,)))
                + contract(dk[:, 512:1024], w_v[part, :], ((1,), (1,)))
            )
        scaled = gt[...] * gain_attn[...].reshape(1, 1536)
        inner = jnp.mean(scaled * x, axis=-1, keepdims=True)
        gt[...] = dy1[...] + root * scaled - x * (root * root * root * inner)

        outs = [pltpu.make_async_copy(gt, gt_far, out_sems.at[0])]
        outs[0].start()
        fold_expert(2)
        home.finish(mixed, [y1])
        outs.append(pltpu.make_async_copy(mixed, mixed_far, out_sems.at[1]))
        outs[1].start()
        home.drain()
        for copy in gathered:
            copy.wait_recv()
        for copy in second:
            copy.wait_recv()
        for m in range(3):
            def finish(i, carry):
                part = pl.ds(pl.multiple_of(i * 48, 16), 48)
                experts[m, 0, part] = sum_p[place.lo, m, part].astype(F32) + land_p2[m, part].astype(F32)
                total = sum_q[place.y, m, part].astype(F32)
                for d in range(3):
                    total = total + land_q2[d, m, part].astype(F32)
                experts[m, 1, part] = total
                return carry

            lax.fori_loop(0, 4, finish, 0)
        outs.append(pltpu.make_async_copy(experts, experts_far, out_sems.at[2]))
        outs[2].start()
        for copy in pending + kv_sent + gathered + second + streams.sent:
            copy.wait_send()
        own_quarters.wait()
        for copy in outs:
            copy.wait()

    pl.run_scoped(
        early, low(16, 128, 1536), low(16, 128, 1536), high(16, 8, 128), high(16, 8, 128),
        low(8, 128, 1536), low(7, 128, 1536), low(1536, 128),
        low(2, 2, 4, 192, 512), low(2, 1536, 512), low(2, 512, 1536),
    )
    buffers = []
    for _, width, _ in STREAMS.values():
        buffers += [
            low(4, 4, 4, 48, width), low(3, 4, 4, 48, width), low(4, 4, 48, width),
            low(3, 4, 48, width), low(4, 48, width), low(3, 48, width),
        ]
    pl.run_scoped(
        late, low(128, 1536), low(128, 1536), low(1536, 2048), low(1536, 512),
        low(256, 1536), low(256, 768), low(256, 768), low(8, 2, 2, 128, 128),
        high(128, 128), low(2, 128, 768), low(4, 384, 128), high(8, 1, 384),
        low(2, 128, 768), low(128, 1024), high(128, 1536), low(8, 4, 2, 128, 128),
        low(4, 2, 2, 128, 128), low(3, 2, 2, 128, 128), low(3, 2, 2, 2, 128, 128), low(2, 2, 128, 128),
        low(48, ALL_WIDE), low(2, 4, 192, 512),
        low(2, 3, 192, 512), low(4, 3, 192, 512), low(3, 192, 512), low(3, 3, 192, 512),
        high(3, 2, 192, 512), low(128, 1536), high(128, 1536), *buffers,
    )


def run_layer(*operands):
    vmem = pl.BlockSpec(memory_space=pltpu.VMEM)
    hbm = pl.BlockSpec(memory_space=pl.ANY)
    sems = pltpu.SemaphoreType.DMA
    struct = jax.ShapeDtypeStruct
    return pl.pallas_call(
        layer_kernel,
        out_shape=(
            struct((128, 1536), BF), struct((128, 1536), F32), struct((4, 48, ALL_WIDE), BF),
            struct((3, 2, 192, 512), F32),
            *[struct((2, 2, 4, 192, 512), BF)] * 3,
            struct((3, 3, 2, 192, 512), BF), struct((3, 4, 192, 512), BF), struct((2, 8, 1536, 128), BF),
        ),
        in_specs=[hbm, vmem, hbm, vmem, vmem, vmem] + [hbm] * 7,
        out_specs=[hbm] * 10,
        scratch_shapes=[
            low(2, 8, 128, 512), low(4, 384, 128), high(8, 1, 384), low(128, 1536), high(128, 1536),
            low(128, 1536), high(128, 128), high(2, 128, 128), high(128, 1536), high(16, 8, 128),
            low(8, 128, 1536), low(2, 2, 64, 1536), low(5, 128, 1536),
            pltpu.SemaphoreType.REGULAR, sems((6,)), sems((3,)), sems, sems((2, 18)), sems((2, 8)),
            sems((2, 8)),
            sems((2, 16)), sems((2, 16)), sems((2, 9)), sems((2, 16)), sems((2,)), sems((2, 2)),
            sems((2, 16)), sems, sems((2, 12)),
            sems((16,)), sems((2, 4)), sems((2, 11)), sems((2, 9 * len(STREAMS))), sems((2, 3)),
            sems((2, 11)), sems((2, 4)), sems((2, 16)), sems((3,)),
        ],
        compiler_params=pltpu.CompilerParams(
            collective_id=0, has_side_effects=True, vmem_limit_bytes=63 << 20
        ),
    )(*operands)


def finish_kernel(
    mixed, gt, quarters, experts, gain, wq, wk, wv,
    mixed_out, gt_out, gq, gk, gv, go, ga, gm, gr, og, ou, od,
    rows_q, rows_kv, sems,
):
    place = Place()
    start = ((place.lo * 4 + place.y) * 4 + place.z) * 48
    rows = pl.ds(pl.multiple_of(start, 16), 48)
    loads = [
        pltpu.make_async_copy(wq.at[rows, :], rows_q, sems.at[0]),
        pltpu.make_async_copy(wk.at[rows, :], rows_kv.at[0], sems.at[1]),
        pltpu.make_async_copy(wv.at[rows, :], rows_kv.at[1], sems.at[2]),
    ]
    for load in loads:
        load.start()
    mixed_out[0] = mixed[...]
    gt_out[0] = gt[...]
    for q in range(4):
        go[:, q * 384 : (q + 1) * 384] = quarters[q, :, 0:384].astype(F32)
        gq[:, q * 384 : (q + 1) * 384] = quarters[q, :, 512:896].astype(F32)
        gk[:, q * 128 : (q + 1) * 128] = quarters[q, :, 896:1024].astype(F32)
        gv[:, q * 128 : (q + 1) * 128] = quarters[q, :, 1024:1152].astype(F32)
    narrow = quarters[0, :, 384:512].astype(F32) + quarters[2, :, 384:512].astype(F32)
    og[...] = experts[0]
    ou[...] = experts[1]
    for e in range(2):
        od[e] = experts[2, e].T
    for load in loads:
        load.wait()
    line = jnp.sum(gq[...] * rows_q[...].astype(F32), axis=1, keepdims=True)
    line = line + jnp.sum(gk[...] * rows_kv[0].astype(F32), axis=1, keepdims=True)
    line = line + jnp.sum(gv[...] * rows_kv[1].astype(F32), axis=1, keepdims=True)
    column = lax.broadcasted_iota(jnp.int32, (48, 1536), 1) - lax.broadcasted_iota(jnp.int32, (48, 1536), 0)
    own_gain = jnp.sum(jnp.where(column == start, gain[...].reshape(1, 1536), 0.0), axis=1, keepdims=True)
    both = jnp.where(
        lax.broadcasted_iota(jnp.int32, (48, 128), 1) == 33, line / own_gain, narrow
    )
    flat = jnp.concatenate([both, jnp.zeros((80, 128), F32)], axis=0).T
    gr[...] = flat[0:32, 0:48]
    gm[...] = flat[32:33, 0:48]
    ga[...] = flat[33:34, 0:48]


def run_finish(*operands):
    vmem = pl.BlockSpec(memory_space=pltpu.VMEM)
    hbm = pl.BlockSpec(memory_space=pl.ANY)
    f32 = lambda *shape: jax.ShapeDtypeStruct(shape, F32)
    return pl.pallas_call(
        finish_kernel,
        out_shape=(
            jax.ShapeDtypeStruct((1, 128, 1536), BF), f32(1, 128, 1536),
            f32(48, 1536), f32(48, 512), f32(48, 512), f32(48, 1536), f32(1, 48), f32(1, 48), f32(32, 48),
            f32(2, 192, 512), f32(2, 192, 512), f32(2, 512, 192),
        ),
        in_specs=[vmem] * 5 + [hbm] * 3,
        out_specs=[vmem] * 12,
        scratch_shapes=[low(48, 1536), low(2, 48, 512), pltpu.SemaphoreType.DMA((3,))],
        compiler_params=pltpu.CompilerParams(vmem_limit_bytes=63 << 20),
    )(*operands)


def shards(
    tokens, expert_ids, w_query, w_key, w_value, w_out, gain_attn, gain_moe, w_router,
    w_gate, w_up, w_down, cotangent,
):
    mixed, gt, quarters, experts, *_ = run_layer(
        tokens[0], expert_ids[0].T, cotangent[0], gain_attn, gain_moe, w_router.T,
        w_query, w_key, w_value, w_out, w_gate.reshape(2, 2, 4, 192, 512), w_up, w_down,
    )
    mixed, gt, gq, gk, gv, go, ga, gm, gr, og, ou, od = run_finish(
        mixed, gt, quarters, experts, gain_attn, w_query, w_key, w_value
    )
    return (mixed, gt, gq, gk, gv, go, ga.reshape(48), gm.reshape(48), gr.T, og, ou, od)


def solution(mesh):
    in_specs = (
        P(("expert", "dp"), "context", None),
        P(("expert", "dp"), "context", None),
        P(),
        P(),
        P(),
        P(),
        P(),
        P(),
        P(),
        P(("expert", "dp"), None, None),
        P(("expert", "dp"), None, None),
        P(("expert", "dp"), None, None),
        P(("expert", "dp"), "context", None),
    )
    out_specs = (
        P(("expert", "dp"), "context", None),
        P(("expert", "dp"), "context", None),
        P(("context", "dp"), None),
        P(("context", "dp"), None),
        P(("context", "dp"), None),
        P(("context", "dp"), None),
        P(("context", "dp")),
        P(("context", "dp")),
        P(("context", "dp"), None),
        P(("expert", "dp"), "context", None),
        P(("expert", "dp"), "context", None),
        P(("expert", "dp"), None, "context"),
    )
    return jax.shard_map(shards, mesh=mesh, in_specs=in_specs, out_specs=out_specs, check_vma=False)
```

time: 1600 us -> 273 us (0.17)
  waiting for transfers between devices: 1160 us -> 0 us
  Pallas kernels: 0 us -> 267 us
  matrix products: 121 us -> 0 us
  local copies, waits for them, and re-layouts: 109 us -> 2.42 us
  other arithmetic: 68.3 us -> 0 us
  blocking collectives: 65.8 us -> 0 us
  starting transfers between devices: 45.7 us -> 0 us
    reduce_scatter x9 -> x0, waiting for transfers between devices: 814 us -> none  [the longest x1 170 us: shards(): lax.psum_scatter(dense_terms[3].astype(jnp.bfloat16), ('context', 'dp'),...]
    pallas_call x0 -> x2, Pallas kernels: none -> 267 us  [the longest x1 262 us: run_layer(): pl.pallas_call(layer_kernel, out_shape=(struct((128, 1536), BF), struct((...]
    all_to_all x4 -> x0, waiting for transfers between devices: 124 us -> none  [the longest x1 37.2 us: shards(): lax.all_to_all(produced, ('expert', 'dp'), split_axis=0, concat_axis=0, t...]
    dot_general x38 -> x0, matrix products: 121 us -> none  [the longest x2 8.58 us: weigh_values(): jnp.einsum('kgqs,skd->qkgd', probs, value_heads, preferred_element_type=j...]
    unnamed x15 -> x0, waiting for transfers between devices: 100 us -> none
    psum x2 -> x0, waiting for transfers between devices: 83.2 us -> none  [the longest x1 47.1 us: shards(): lax.psum(partial_sums[1].astype(jnp.bfloat16), 'expert').astype(jnp.float32)]
    unnamed x1 -> x0, blocking collectives: 65.8 us -> none
    all_to_all x4 -> x0, starting transfers between devices: 44.7 us -> none  [the longest x1 12.2 us: shards(): lax.all_to_all(dispatch_rows(spread), ('expert', 'dp'), split_axis=0, con...]
  transfers between devices with their start and end apart: 18 -> 0, of which waited for: 18 -> 0; matrix products, arithmetic and copies ran while one was open for 10% -> 0% of each run, Pallas kernels for 0% -> 0%
where the time goes in v4:
time: 273 us; the launch traced here: 270 us
  Pallas kernels  267 us (98%)
    pallas_call x1, Pallas kernels, run_layer(): pl.pallas_call(layer_kernel, out_shape=(struct((128, 1536), BF), struct((...  262 us

profile of v4, /device:TPU:1, one launch (start us, length us, event | category | flops | bytes accessed | tf_op | source)
XLA Modules:
  0.0 270.4 jit_solution(372601630275591066)
XLA Ops:
  0.6 262.1 %shard_map.220 = (bf16[128,1536]{1,0:T(8,128)(2,1)}, f32[128,1536]{1,0:T(8,128)}, bf16[4,48,1152]{2,1,0:T(8,128)(2,1)}, f32[3,2,192,512]{3,2,1,0:T(8,128)}, bf16...) custom-call(bf16[128,1536]{1,0:T(8,128)(2,1)} %bitcast.11, ...), custom_call_target="tpu_custom_call" | custom-call | tf_op jit(solution)/shard_map/pallas_call | solution.py:1313
  262.8 5.2 %shard_map.221 = (bf16[1,128,1536]{2,1,0:T(8,128)(2,1)}, f32[1,128,1536]{2,1,0:T(8,128)}, f32[48,1536]{1,0:T(8,128)}, f32[48,512]{1,0:T(8,128)}, f32[48,512]{1,0...) custom-call(bf16[128,1536]{1,0:T(8,128)(2,1)} %get-tuple-element.28., ...), custom_call_target="tpu_custom_call" | custom-call | tf_op jit(solution)/shard_map/pallas_call | solution.py:1387
  268.0 2.4 copy.25

commit v5 on v4

--- a/solution.py
+++ b/solution.py
@@ -442,7 +442,7 @@
 
 
 STREAMS = {
-    "o1": ("zxy", 256, 0), "o2": ("zyx", 256, 256), "q1": ("zxy", 256, 512),
+    "o1": ("yxz", 256, 0), "o2": ("zyx", 256, 256), "q1": ("zxy", 256, 512),
     "q2": ("yxz", 128, 768), "s1": ("xzy", 128, 896), "s2": ("zyx", 128, 1024),
 }
 ALL_WIDE = 1152
@@ -825,19 +825,6 @@
             spread_rows.drain()
             columns.third()
 
-            def outputs(i, carry):
-                e, m = i // 2, i % 2
-                part = pl.ds(pl.multiple_of(m * 320, 320), 320)
-                made = contract(gact[e, part, :], wd[e], ((1,), (0,))).astype(BF)
-                for j in range(4):
-                    drow[m * 4 + j, pl.ds(pl.multiple_of(e * 80, 80), 80), :] = made[j * 80 : (j + 1) * 80]
-                return carry
-
-            lax.fori_loop(0, 4, outputs, 0)
-            home.second()
-            all_pairs(lambda p: put_back(p, rows))
-            outward = Gather(place, rows, eo_pool, None, None, eo_sems)
-            out_swaps = [outward.swap(0), outward.swap(1)]
             copies, far = {}, []
             other_lo = (place.lo + 1) % 2
             order = [
@@ -871,8 +858,23 @@
                 lax.fori_loop(0, 4, weight_grad, 0)
                 copies[step] = pltpu.make_async_copy(wg.at[slot], out.at[e], stage_sems.at[slot])
                 copies[step].start()
+                if step == 2:
+                    home.second()
             forward(4)
             forward(5)
+
+            def outputs(i, carry):
+                e, m = i // 2, i % 2
+                part = pl.ds(pl.multiple_of(m * 320, 320), 320)
+                made = contract(gact[e, part, :], wd[e], ((1,), (0,))).astype(BF)
+                for j in range(4):
+                    drow[m * 4 + j, pl.ds(pl.multiple_of(e * 80, 80), 80), :] = made[j * 80 : (j + 1) * 80]
+                return carry
+
+            lax.fori_loop(0, 4, outputs, 0)
+            all_pairs(lambda p: put_back(p, rows))
+            outward = Gather(place, rows, eo_pool, None, None, eo_sems)
+            out_swaps = [outward.swap(0), outward.swap(1)]
             for copy in out_swaps:
                 copy.wait_recv()
             for h in range(2):
@@ -1198,6 +1200,7 @@
         streams.step("s1", 0)
         streams.step("s2", 0)
         streams.step("q1", 0)
+        fold_expert(2)
         for copy in legs:
             copy.wait_recv()
         kv_add(
@@ -1254,16 +1257,16 @@
 
         outs = [pltpu.make_async_copy(gt, gt_far, out_sems.at[0])]
         outs[0].start()
-        fold_expert(2)
         home.finish(mixed, [y1])
         outs.append(pltpu.make_async_copy(mixed, mixed_far, out_sems.at[1]))
         outs[1].start()
         home.drain()
         for copy in gathered:
             copy.wait_recv()
-        for copy in second:
-            copy.wait_recv()
         for m in range(3):
+            for copy in second[m * 4 : m * 4 + 4]:
+                copy.wait_recv()
+
             def finish(i, carry):
                 part = pl.ds(pl.multiple_of(i * 48, 16), 48)
                 experts[m, 0, part] = sum_p[place.lo, m, part].astype(F32) + land_p2[m, part].astype(F32)
@@ -1274,8 +1277,8 @@
                 return carry
 
             lax.fori_loop(0, 4, finish, 0)
-        outs.append(pltpu.make_async_copy(experts, experts_far, out_sems.at[2]))
-        outs[2].start()
+            outs.append(pltpu.make_async_copy(experts.at[m], experts_far.at[m], out_sems.at[2 + m]))
+            outs[-1].start()
         for copy in pending + kv_sent + gathered + second + streams.sent:
             copy.wait_send()
         own_quarters.wait()
@@ -1329,7 +1332,7 @@
             sems((2, 16)), sems((2, 16)), sems((2, 9)), sems((2, 16)), sems((2,)), sems((2, 2)),
             sems((2, 16)), sems, sems((2, 12)),
             sems((16,)), sems((2, 4)), sems((2, 11)), sems((2, 9 * len(STREAMS))), sems((2, 3)),
-            sems((2, 11)), sems((2, 4)), sems((2, 16)), sems((3,)),
+            sems((2, 11)), sems((2, 4)), sems((2, 16)), sems((5,)),
         ],
         compiler_params=pltpu.CompilerParams(
             collective_id=0, has_side_effects=True, vmem_limit_bytes=63 << 20
@@ -1362,8 +1365,7 @@
     narrow = quarters[0, :, 384:512].astype(F32) + quarters[2, :, 384:512].astype(F32)
     og[...] = experts[0]
     ou[...] = experts[1]
-    for e in range(2):
-        od[e] = experts[2, e].T
+    od[...] = experts[2]
     for load in loads:
         load.wait()
     line = jnp.sum(gq[...] * rows_q[...].astype(F32), axis=1, keepdims=True)
@@ -1389,7 +1391,7 @@
         out_shape=(
             jax.ShapeDtypeStruct((1, 128, 1536), BF), f32(1, 128, 1536),
             f32(48, 1536), f32(48, 512), f32(48, 512), f32(48, 1536), f32(1, 48), f32(1, 48), f32(32, 48),
-            f32(2, 192, 512), f32(2, 192, 512), f32(2, 512, 192),
+            f32(2, 192, 512), f32(2, 192, 512), f32(2, 192, 512),
         ),
         in_specs=[vmem] * 5 + [hbm] * 3,
         out_specs=[vmem] * 12,
@@ -1409,7 +1411,7 @@
     mixed, gt, gq, gk, gv, go, ga, gm, gr, og, ou, od = run_finish(
         mixed, gt, quarters, experts, gain_attn, w_query, w_key, w_value
     )
-    return (mixed, gt, gq, gk, gv, go, ga.reshape(48), gm.reshape(48), gr.T, og, ou, od)
+    return (mixed, gt, gq, gk, gv, go, ga.reshape(48), gm.reshape(48), gr.T, og, ou, od.transpose(0, 2, 1))
 
 
 def solution(mesh):

time: 273 us -> 252 us (0.923)
  Pallas kernels: 267 us -> 250 us
    pallas_call x1, Pallas kernels: 262 us -> 245 us  [run_layer(): pl.pallas_call(layer_kernel, out_shape=(struct((128, 1536), BF), struct((...]
where the time goes in v5:
time: 252 us; the launch traced here: 251 us
  Pallas kernels  250 us (99%)
    pallas_call x1, Pallas kernels, run_layer(): pl.pallas_call(layer_kernel, out_shape=(struct((128, 1536), BF), struct((...  245 us
    pallas_call x1, Pallas kernels, run_finish(): pl.pallas_call(finish_kernel, out_shape=(jax.ShapeDtypeStruct((1, 128, 15...  5.12 us

profile of v5, /device:TPU:1, one launch (start us, length us, event | category | flops | bytes accessed | tf_op | source)
XLA Modules:
  0.0 251.2 jit_solution(14730784536564806814)
XLA Ops:
  0.6 245.3 %shard_map.220 = (bf16[128,1536]{1,0:T(8,128)(2,1)}, f32[128,1536]{1,0:T(8,128)}, bf16[4,48,1152]{2,1,0:T(8,128)(2,1)}, f32[3,2,192,512]{3,2,1,0:T(8,128)}, bf16...) custom-call(bf16[128,1536]{1,0:T(8,128)(2,1)} %bitcast.12, ...), custom_call_target="tpu_custom_call" | custom-call | tf_op jit(solution)/shard_map/pallas_call | solution.py:1316
  245.9 5.1 %shard_map.221 = (bf16[1,128,1536]{2,1,0:T(8,128)(2,1)}, f32[1,128,1536]{2,1,0:T(8,128)}, f32[48,1536]{1,0:T(8,128)}, f32[48,512]{1,0:T(8,128)}, f32[48,512]{1,0...) custom-call(bf16[128,1536]{1,0:T(8,128)(2,1)} %get-tuple-element.28., ...), custom_call_target="tpu_custom_call" | custom-call | tf_op jit(solution)/shard_map/pallas_call | solution.py:1389

commit v6 on v5

--- a/solution.py
+++ b/solution.py
@@ -443,7 +443,7 @@
 
 STREAMS = {
     "o1": ("yxz", 256, 0), "o2": ("zyx", 256, 256), "q1": ("zxy", 256, 512),
-    "q2": ("yxz", 128, 768), "s1": ("xzy", 128, 896), "s2": ("zyx", 128, 1024),
+    "q2": ("zyx", 128, 768), "s1": ("xzy", 128, 896), "s2": ("zyx", 128, 1024),
 }
 ALL_WIDE = 1152
 

time: 252 us -> 249 us (0.988)
  Pallas kernels: 250 us -> 247 us
    pallas_call x1, Pallas kernels: 245 us -> 242 us  [run_layer(): pl.pallas_call(layer_kernel, out_shape=(struct((128, 1536), BF), struct((...]
where the time goes in v6:
time: 249 us; the launch traced here: 248 us
  Pallas kernels  247 us (99%)
    pallas_call x1, Pallas kernels, run_layer(): pl.pallas_call(layer_kernel, out_shape=(struct((128, 1536), BF), struct((...  242 us
    pallas_call x1, Pallas kernels, run_finish(): pl.pallas_call(finish_kernel, out_shape=(jax.ShapeDtypeStruct((1, 128, 15...  5.12 us

profile of v6, /device:TPU:1, one launch (start us, length us, event | category | flops | bytes accessed | tf_op | source)
XLA Modules:
  0.0 248.1 jit_solution(1820518665680840168)
XLA Ops:
  0.6 242.1 %shard_map.220 = (bf16[128,1536]{1,0:T(8,128)(2,1)}, f32[128,1536]{1,0:T(8,128)}, bf16[4,48,1152]{2,1,0:T(8,128)(2,1)}, f32[3,2,192,512]{3,2,1,0:T(8,128)}, bf16...) custom-call(bf16[128,1536]{1,0:T(8,128)(2,1)} %bitcast.12, ...), custom_call_target="tpu_custom_call" | custom-call | tf_op jit(solution)/shard_map/pallas_call | solution.py:1316
  242.8 5.1 %shard_map.221 = (bf16[1,128,1536]{2,1,0:T(8,128)(2,1)}, f32[1,128,1536]{2,1,0:T(8,128)}, f32[48,1536]{1,0:T(8,128)}, f32[48,512]{1,0:T(8,128)}, f32[48,512]{1,0...) custom-call(bf16[128,1536]{1,0:T(8,128)(2,1)} %get-tuple-element.28., ...), custom_call_target="tpu_custom_call" | custom-call | tf_op jit(solution)/shard_map/pallas_call | solution.py:1389
